TPU v7x, 32 devices: a whole 2x2x4 slice. The times are simulated.
32 devices in a mesh: replica: 4 (over x, core), fsdp: 8 (over z, y).
Axes of the slice: x: 2, y: 2, z: 4, core: 2. Of those that a mesh axis runs over, the one named last changes fastest.
Arguments:
- tokens: bfloat16 [8192, 2048], P(('replica', 'fsdp')), may hold values from -6 to 6
- inner_q: bfloat16 [4, 2048, 2048], P('replica', 'fsdp')
- inner_k: bfloat16 [4, 2048, 512], P('replica', 'fsdp')
- inner_v: bfloat16 [4, 2048, 512], P('replica', 'fsdp')
- outer_q: float32 [2048, 2048], P('fsdp')
- outer_k: float32 [2048, 512], P('fsdp')
- outer_v: float32 [2048, 512], P('fsdp')
- moment_q: float32 [2048, 2048], P('fsdp', 'replica'), may hold values from -0.09375 to 0.09375
- moment_k: float32 [2048, 512], P('fsdp', 'replica'), may hold values from -0.09375 to 0.09375
- value_momentum: float32 [2048, 512], P('fsdp', 'replica'), may hold values from -0.09375 to 0.09375
Outputs:
- projected: bfloat16 [8192, 3072], P(('replica', 'fsdp'))
- updated_outer_query: float32 [2048, 2048], P('fsdp')
- updated_outer_key: float32 [2048, 512], P('fsdp')
- new_outer_v: float32 [2048, 512], P('fsdp')
- new_moment_q: float32 [2048, 2048], P('fsdp', 'replica')
- new_moment_k: float32 [2048, 512], P('fsdp', 'replica')
- new_moment_v: float32 [2048, 512], P('fsdp', 'replica')
All inputs are finite; a program needn't handle non-finite values.
Results may differ from a plain program's by a relative error of at most 0.005.
Values may be sent and summed in bfloat16 or wider, within the bound.
No kernel may reach another device: no remote copies, remote signals or barrier semaphores. Data moves between devices by JAX's collectives and lax.ppermute only.
A program may use at most 64 MiB of HBM per device.

v0:
```python
import jax
import jax.numpy as jnp
from jax import lax
from jax.sharding import PartitionSpec as P

LEARN_RATE = 0.7
MOMENTUM_BETA = 0.9


def per_device(
    tokens, inner_q, inner_k, inner_v, outer_q, outer_k, outer_v, moment_q, moment_k, value_momentum
):
    worker_count = lax.axis_size("replica")
    worker_index = lax.axis_index("replica")
    outers = (outer_q, outer_k, outer_v)
    moments = (moment_q, moment_k, value_momentum)
    differences = tuple(
        (
            outer - inner[0].astype(jnp.float32)
            for outer, inner in zip(outers, (inner_q, inner_k, inner_v))
        )
    )
    summed = lax.psum_scatter(differences, "replica", scatter_dimension=1, tiled=True)
    owned_outer = []
    owned_moment = []
    for total, outer, outer_momentum in zip(summed, outers, moments):
        width = outer_momentum.shape[1]
        pseudo = total / worker_count
        new_moment = MOMENTUM_BETA * outer_momentum + pseudo
        own_slice = lax.dynamic_slice_in_dim(outer, worker_index * width, width, 1)
        owned_outer.append(own_slice - LEARN_RATE * (pseudo + MOMENTUM_BETA * new_moment))
        owned_moment.append(new_moment)
    full_outer = lax.all_gather(tuple(owned_outer), "replica", axis=1, tiled=True)
    local_fresh = jnp.concatenate([weight.astype(jnp.bfloat16) for weight in full_outer], axis=1)
    fresh = lax.all_gather(local_fresh, "fsdp", axis=0, tiled=True)
    projected = jnp.dot(tokens, fresh, preferred_element_type=jnp.float32).astype(jnp.bfloat16)
    return (
        projected,
        full_outer[0],
        full_outer[1],
        full_outer[2],
        owned_moment[0],
        owned_moment[1],
        owned_moment[2],
    )


def solution(mesh):
    placed = (
        P(("replica", "fsdp"), None),
        P("replica", "fsdp", None),
        P("replica", "fsdp", None),
        P("replica", "fsdp", None),
        P("fsdp", None),
        P("fsdp", None),
        P("fsdp", None),
        P("fsdp", "replica"),
        P("fsdp", "replica"),
        P("fsdp", "replica"),
    )
    return jax.shard_map(
        per_device,
        mesh=mesh,
        in_specs=placed,
        out_specs=(
            P(("replica", "fsdp"), None),
            P("fsdp", None),
            P("fsdp", None),
            P("fsdp", None),
            P("fsdp", "replica"),
            P("fsdp", "replica"),
            P("fsdp", "replica"),
        ),
        check_vma=False,
    )
```

profile of v0, /device:TPU:0, one launch (start us, length us, event | category | flops | bytes accessed | tf_op | source)
XLA Modules:
  0.0 321.0 jit_solution(3848993660080032980)
XLA Ops:
  7.2 0.0 copy-start
  7.2 0.0 reduce-scatter.4.cloned.1.call-start
  7.2 3.6 %convert_subtract_fusion = f32[256,2048]{1,0:T(8,128)} fusion(f32[256,2048]{1,0:T(8,128)} %param.14, bf16[1,256,2048]{2,1,0:T(8,128)(2,1)} %param.11), kind=kLoop, calls=%fused_computation.2 | loop fusion | flops 1048576 | bytes 5242880 | tf_op jit(solution)/shard_map/sub | solution.py:19
  10.9 0.0 copy-start.6
  10.9 0.0 copy-start.9
  10.9 0.0 reduce-scatter.4.cloned.1.call-update
  10.9 0.0 copy-start.8
  10.9 0.0 reduce-scatter.6.cloned.1.call-start
  11.0 0.9 copy-done.6
  11.9 0.1 copy-done.9
  12.0 0.9 convert_subtract_fusion.2
  12.8 0.0 reduce-scatter.6.cloned.1.call-update
  12.8 0.0 reduce-scatter.8.cloned.1.call-start
  12.9 0.0 copy-done.7
  12.9 0.0 copy-done.10
  12.9 0.9 convert_subtract_fusion.1
  13.8 0.0 reduce-scatter.8.cloned.1.call-update
  13.8 0.0 all-gather.3.cloned.1.call-start
  13.9 0.0 copy-start.12
  13.9 31.4 %reduce-scatter.4.cloned.1.call-done = f32[256,512]{1,0:T(8,128)} async-done(((f32[256,2048]{1,0:T(8,128)}), f32[256,512]{1,0:T(8,128)}) %reduce-scatter.4.cloned.1.call-update) | async-done | bytes 524304 | tf_op jit(solution)/shard_map/reduce_scatter | solution.py:23
  45.3 0.0 copy-done.8
  45.3 2.3 multiply_subtract_fusion
  47.6 0.0 all-gather.3.cloned.1.call-update
  47.7 0.0 all-gather.5.cloned.1.call-start
  47.7 22.5 %reduce-scatter.6.cloned.1.call-done = f32[256,128]{1,0:T(8,128)} async-done(((f32[256,512]{1,0:T(8,128)}), f32[256,128]{1,0:T(8,128)}) %reduce-scatter.6.cloned.1.call-update) | async-done | bytes 131088 | tf_op jit(solution)/shard_map/reduce_scatter | solution.py:23
  70.2 0.0 copy-done.11
  70.2 1.6 multiply_subtract_fusion.2
  71.8 6.8 %all_gather.13 = f32[256,512]{1,0:T(8,128)S(1)} all-gather(f32[256,128]{1,0:T(8,128)S(1)} %get-tuple-element.16), channel_id=1, replica_groups=mesh['replica'=4,'fsdp'=8] {'replica'}, dimensions={1}, use_global_device_ids=true | all-gather | bytes 655360 | tf_op jit(solution)/shard_map/all_gather | solution.py:33
  78.5 0.8 copy-done.2
  79.4 15.6 %reduce-scatter.8.cloned.1.call-done = f32[256,128]{1,0:T(8,128)} async-done(((f32[256,512]{1,0:T(8,128)}), f32[256,128]{1,0:T(8,128)}) %reduce-scatter.8.cloned.1.call-update) | async-done | bytes 131088 | tf_op jit(solution)/shard_map/reduce_scatter | solution.py:23
  95.0 0.0 copy-done.12
  95.0 1.6 multiply_subtract_fusion.1
  96.6 6.8 %all_gather.14 = f32[256,512]{1,0:T(8,128)S(1)} all-gather(f32[256,128]{1,0:T(8,128)S(1)} %get-tuple-element.18), channel_id=1, replica_groups=mesh['replica'=4,'fsdp'=8] {'replica'}, dimensions={1}, use_global_device_ids=true | all-gather | bytes 655360 | tf_op jit(solution)/shard_map/all_gather | solution.py:33
  103.3 0.8 copy-done.4
  104.2 15.5 %all-gather.3.cloned.1.call-done = f32[256,2048]{1,0:T(8,128)} async-done(((f32[256,512]{1,0:T(8,128)}), f32[256,2048]{1,0:T(8,128)}) %all-gather.3.cloned.1.call-update) | async-done | bytes 2097168 | tf_op jit(solution)/shard_map/all_gather | solution.py:33
  119.6 1.7 convert_element_type.35
  121.4 1.3 pad_maximum_fusion
  122.7 0.0 all-gather.5.cloned.1.call-update
  122.7 176.6 %all-gather.5.cloned.1.call-done = bf16[2048,3072]{1,0:T(8,128)(2,1)} async-done(((bf16[256,3072]{1,0:T(8,128)(2,1)}), bf16[2048,3072]{1,0:T(8,128)(2,1)}) %all-gather.5.cloned.1.call-update) | async-done | bytes 12582928 | tf_op jit(solution)/shard_map/all_gather | solution.py:35
  299.3 0.0 copy-done
  299.3 9.4 %fusion = bf16[256,3072]{0,1:T(8,128)(2,1)} fusion(bf16[2048,3072]{1,0:T(8,128)(2,1)} %all-gather.5.cloned.1.call-done, bf16[256,2048]{1,0:T(8,128)(2,1)S(1)} %copy-done), kind=kOutput, calls=%fused_computation.1 | convolution fusion | flops 3222011904 | bytes 15204352 | tf_op jit(solution)/shard_map/dot_general | solution.py:36
  308.7 2.7 copy.17
  311.5 0.0 copy-done.1
  311.5 1.3 copy.21
  312.8 0.0 copy-done.3
  312.8 0.8 copy.22
  313.6 0.0 copy-done.5
  313.6 0.8 copy.23
  (10 shorter events, 0.1 us)
Async XLA Ops:
  7.2 292.1 %copy-start = (bf16[256,2048]{1,0:T(8,128)(2,1)S(1)}, bf16[256,2048]{1,0:T(8,128)(2,1)}, u32[]{:S(2)}) copy-start(bf16[256,2048]{1,0:T(8,128)(2,1)} %param.10) | copy-start | bytes 3145732
  7.2 38.1 %reduce-scatter.4.cloned.1.call-start = ((), (), s32[]{:S(2)}) async-start(), calls=%async_computation.3 | async-start | bytes 2621440 | tf_op jit(solution)/shard_map/reduce_scatter | solution.py:23
  10.9 1.0 copy-start.6
  10.9 1.1 copy-start.9
  10.9 2.0 copy-start.7
  10.9 2.1 copy-start.10
  10.9 34.4 %copy-start.8 = (f32[256,512]{1,0:T(8,128)S(1)}, f32[256,512]{1,0:T(8,128)}, u32[]{:S(2)}) copy-start(f32[256,512]{1,0:T(8,128)} %param.17) | copy-start | bytes 1572868
  10.9 59.3 %reduce-scatter.6.cloned.1.call-start = ((), (), s32[]{:S(2)}) async-start(), calls=%async_computation.5 | async-start | bytes 655360 | tf_op jit(solution)/shard_map/reduce_scatter | solution.py:23
  12.8 82.1 %reduce-scatter.8.cloned.1.call-start = ((), (), s32[]{:S(2)}) async-start(), calls=%async_computation.6 | async-start | bytes 655360 | tf_op jit(solution)/shard_map/reduce_scatter | solution.py:23
  13.8 56.4 %copy-start.11 = (f32[256,128]{1,0:T(8,128)S(1)}, f32[256,128]{1,0:T(8,128)}, u32[]{:S(2)}) copy-start(f32[256,128]{1,0:T(8,128)} %param.18) | copy-start | bytes 393220
  13.8 105.8 %all-gather.3.cloned.1.call-start = ((), (), s32[]{:S(2)}) async-start(), calls=%async_computation.4 | async-start | bytes 2621440 | tf_op jit(solution)/shard_map/all_gather | solution.py:33
  13.9 81.1 %copy-start.12 = (f32[256,128]{1,0:T(8,128)S(1)}, f32[256,128]{1,0:T(8,128)}, u32[]{:S(2)}) copy-start(f32[256,128]{1,0:T(8,128)} %param.19) | copy-start | bytes 393220
  47.7 251.6 %all-gather.5.cloned.1.call-start = ((), (), s32[]{:S(2)}) async-start(), calls=%async_computation.7 | async-start | bytes 14155776 | tf_op jit(solution)/shard_map/all_gather | solution.py:35
  78.5 0.8 copy-start.2
  103.3 0.8 copy-start.4
  308.7 2.7 copy-start.1
  311.5 1.4 copy-start.3
  311.5 2.2 copy-start.5
Sparse Core Ops, SparseCore 0:
  11.1 34.1 reduce-scatter.3
  48.5 21.6 reduce-scatter.5
  73.3 21.6 reduce-scatter.7
  97.0 22.5 all-gather.2
  122.8 176.4 all-gather.4
where the time goes:
time: 321 us
  waiting for transfers between devices  262 us (82%)
  other arithmetic  14 us (4%)
  between operations  13.9 us (4%)
  blocking collectives  13.5 us (4%)
  matrix products  9.44 us (3%)
  local copies, waits for them, and re-layouts  8.31 us (3%)
    all_gather x1, waiting for transfers between devices, per_device(): fresh = lax.all_gather(local_fresh, 'fsdp', axis=0, tiled=True)  177 us
    reduce_scatter x3, waiting for transfers between devices, per_device(): lax.psum_scatter(differences, 'replica', scatter_dimension=1, tiled=True)  69.5 us
    all_gather x1, waiting for transfers between devices, per_device(): lax.all_gather(tuple(owned_outer), 'replica', axis=1, tiled=True)  15.5 us
    all_gather x2, blocking collectives, per_device(): lax.all_gather(tuple(owned_outer), 'replica', axis=1, tiled=True)  13.5 us
    dot_general x1, matrix products, per_device(): jnp.dot(tokens, fresh, preferred_element_type=jnp.float32)  9.44 us
    unnamed x30, local copies, waits for them, and re-layouts  8.31 us
  transfers between devices with their start and end apart: 5, of which 5 were waited for; matrix products, arithmetic and copies ran while one was open for 2% of the time, Pallas kernels for 0%

commit v1 on v0

v1 whole, which is shorter than its diff:
```python
import functools

import jax
import jax.numpy as jnp
from jax import lax
from jax.experimental import pallas as pl
from jax.experimental.pallas import tpu as pltpu
from jax.sharding import PartitionSpec as P

LEARN_RATE = 0.7
MOMENTUM_BETA = 0.9
SMALL_VMEM = 12 * 1024 * 1024
LONGEST_RING = 16


def from_replica(x, distance):
    count = lax.axis_size("replica")
    return lax.ppermute(x, "replica", [(i, i ^ distance) for i in range(count)])


def ring_member(p, n):
    return 2 * p if p < n // 2 else 2 * (n - 1 - p) + 1


def source_of(row, steps, n):
    p = jnp.where(row % 2 == 0, row // 2, n - 1 - row // 2)
    p = (p - steps + n) % n
    return jnp.where(p < n // 2, 2 * p, 2 * (n - 1 - p) + 1)


def after(x, *others):
    return lax.optimization_barrier((x, *others))[0]


def fetch(sources, buffers, sems):
    copies = [pltpu.make_async_copy(a, b, sems.at[i]) for i, (a, b) in enumerate(zip(sources, buffers))]
    for copy in copies:
        copy.start()
    for copy in copies:
        copy.wait()


def columns_at(ref, block, width):
    return ref.at[:, pl.ds(pl.multiple_of(block * width, width), width)]


def in_hbm(arrays):
    return [pltpu.with_memory_space_constraint(a, pltpu.HBM) for a in arrays]


def blocks_of(arrays, widths):
    return [pltpu.VMEM((a.shape[0], w), a.dtype) for a, w in zip(arrays, widths * 3)]


def spread(pieces, outs):
    edges = [0]
    for piece in pieces:
        edges.append(edges[-1] + piece.shape[1])
    left = 0
    for out in outs:
        right = left + out.shape[1]
        for piece, start in zip(pieces, edges):
            low, high = max(left, start), min(right, start + piece.shape[1])
            if low < high:
                out[:, low - left : high - left] = piece[:, low - start : high - start].astype(out.dtype)
        left = right


def pair_sums(inners, siblings, outers):
    sums = []
    for inner, sibling, outer in zip(inners, siblings, outers):
        base = outer[...]
        sums.append(base + base - (inner[...].astype(jnp.float32) + sibling[...].astype(jnp.float32)))
    return sums


def far_kernel(where, *refs):
    sources, outs, buffers, sems = refs[:9], refs[9:11], refs[11:20], refs[20]
    block = lax.bitwise_xor(where[0], 2)
    fetch([columns_at(r, block, b.shape[1]) for r, b in zip(sources, buffers)], buffers, sems)
    spread(pair_sums(buffers[:3], buffers[3:6], buffers[6:]), outs)


def near_kernel(where, *refs):
    sources, moments = refs[:9], refs[9:12]
    sums, own, packed, buffers, sems = refs[12:14], refs[14:16], refs[16:18], refs[18:27], refs[27]
    fetch([columns_at(r, where[0], b.shape[1]) for r, b in zip(sources, buffers)], buffers, sems)
    spread(pair_sums(buffers[:3], buffers[3:6], buffers[6:]), sums)
    spread(buffers[6:], own)
    spread(moments, packed)


def sums_call(kernel, where, inners, siblings, outers, moments, widths, shapes, name):
    arrays = (*inners, *siblings, *outers)
    return pl.pallas_call(
        kernel,
        out_shape=shapes,
        in_specs=[pl.BlockSpec(memory_space=pltpu.SMEM)]
        + [pl.BlockSpec(memory_space=pl.ANY)] * 9
        + [pl.BlockSpec(memory_space=pltpu.VMEM)] * len(moments),
        out_specs=[pl.BlockSpec(memory_space=pltpu.VMEM)] * len(shapes),
        scratch_shapes=[*blocks_of(arrays, widths), pltpu.SemaphoreType.DMA((9,))],
        compiler_params=pltpu.CompilerParams(vmem_limit_bytes=SMALL_VMEM),
        name=name,
    )(where, *in_hbm(inners), *siblings, *in_hbm(outers), *moments)


def subtract_kernel(where, outer_q, outer_k, outer_v, *refs):
    deltas, outs = refs[:-3], refs[-3:]
    outers = (outer_q, outer_k, outer_v)
    me = where[0]
    for distance, delta in enumerate(deltas):
        block = lax.bitwise_xor(me, distance)
        start = 0
        for outer, out in zip(outers, outs):
            width = outer.shape[1] // len(deltas)
            columns = pl.ds(pl.multiple_of(block * width, width), width)
            out[:, columns] = outer[:, columns] - delta[:, start : start + width].astype(jnp.float32)
            start += width


def subtract(where, outers, deltas):
    return pl.pallas_call(
        subtract_kernel,
        out_shape=[jax.ShapeDtypeStruct(o.shape, o.dtype) for o in outers],
        in_specs=[pl.BlockSpec(memory_space=pltpu.SMEM)]
        + [pl.BlockSpec(memory_space=pltpu.VMEM)] * (len(outers) + len(deltas)),
        out_specs=[pl.BlockSpec(memory_space=pltpu.VMEM)] * len(outers),
        compiler_params=pltpu.CompilerParams(vmem_limit_bytes=SMALL_VMEM),
        name="outer_minus_delta",
    )(where, *outers, *deltas)


def place_kernel(widths, where, *refs):
    sources, out = refs[:-1], refs[-1]
    count = len(sources) // 2
    for distance in range(count):
        block = lax.bitwise_xor(where[0], distance)
        targets, start = [], 0
        for width in widths:
            targets.append(out.at[:, pl.ds(pl.multiple_of(start + block * width, width), width)])
            start += count * width
        spread(sources[2 * distance : 2 * distance + 2], targets)


def place(where, pieces, widths):
    parts = [part for piece in pieces for part in piece]
    return pl.pallas_call(
        functools.partial(place_kernel, widths),
        out_shape=jax.ShapeDtypeStruct((parts[0].shape[0], len(pieces) * sum(widths)), jnp.bfloat16),
        in_specs=[pl.BlockSpec(memory_space=pltpu.SMEM)]
        + [pl.BlockSpec(memory_space=pltpu.VMEM)] * len(parts),
        out_specs=pl.BlockSpec(memory_space=pltpu.VMEM),
        compiler_params=pltpu.CompilerParams(vmem_limit_bytes=SMALL_VMEM),
        name="place_columns",
    )(where, *parts)


def per_device(
    tokens, inner_q, inner_k, inner_v, outer_q, outer_k, outer_v, moment_q, moment_k, value_momentum
):
    count = lax.axis_size("replica")
    n = lax.axis_size("fsdp")
    me = lax.axis_index("replica")
    row = lax.axis_index("fsdp")
    inners = (inner_q[0], inner_k[0], inner_v[0])
    outers = (outer_q, outer_k, outer_v)
    moments = (moment_q, moment_k, value_momentum)
    widths = [m.shape[1] for m in moments]
    rows = outer_q.shape[0]
    mine = tokens.shape[0]
    total_width = sum(widths)
    streams = (total_width // 2, total_width - total_width // 2)

    def shapes(dtype):
        return [jax.ShapeDtypeStruct((rows, w), dtype) for w in streams]

    where = me.astype(jnp.int32).reshape(1)
    siblings = [from_replica(a, 1) for a in inners]
    fars = sums_call(far_kernel, where, inners, siblings, outers, (), widths, shapes(jnp.bfloat16), "far_sums")
    remotes = [from_replica(far, 2) for far in fars]
    near = sums_call(
        near_kernel, where, inners, siblings, outers, moments, widths, shapes(jnp.float32) * 3, "near_sums"
    )
    fresh, deltas, new_moments = [], [], []
    for own, outer, moment, remote in zip(near[:2], near[2:4], near[4:], remotes):
        pseudo = (own + remote.astype(jnp.float32)) / count
        new_moment = MOMENTUM_BETA * moment + pseudo
        delta = LEARN_RATE * (pseudo + MOMENTUM_BETA * new_moment)
        fresh.append((outer - delta).astype(jnp.bfloat16))
        deltas.append(delta.astype(jnp.bfloat16))
        new_moments.append(new_moment)

    tokens_1 = from_replica(after(tokens, *fars), 1)
    tokens_2 = from_replica(after(tokens, *remotes), 2)
    near_tokens = jnp.concatenate([tokens, tokens_1], axis=0)

    up = [(ring_member(p, n), ring_member((p + 1) % n, n)) for p in range(n)]
    down = [(b, a) for a, b in up]
    more, less = n // 2, n - 1 - n // 2

    def product(lhs, steps, block):
        lanes = lax.dynamic_slice_in_dim(lhs, source_of(row, steps, n) * rows, rows, 1)
        return jnp.dot(lanes, block, preferred_element_type=jnp.float32)

    delta = jnp.concatenate(deltas, axis=1)
    arrived = [[(0, part)] for part in fresh]
    near_totals = [product(near_tokens, 0, part) for part in fresh]
    if n > LONGEST_RING:
        gathered = [lax.all_gather(part, "fsdp", axis=0, tiled=True) for part in fresh]
        tokens_3 = from_replica(tokens_2, 1)
        far_tokens = jnp.concatenate([tokens_2, tokens_3], axis=0)
        delta_2 = from_replica(after(delta, tokens_3), 2)
        near_totals = [jnp.dot(near_tokens, g, preferred_element_type=jnp.float32) for g in gathered]
        far_totals = [jnp.dot(far_tokens, g, preferred_element_type=jnp.float32) for g in gathered]
    else:
        ups, downs = list(fresh), list(fresh)
        limits = ((more, less), (less, more))
        far_totals = [None] * len(fresh)
        for step in range(1, more + 1):
            for index, (up_limit, down_limit) in enumerate(limits):
                before = near_totals[index]
                if step <= up_limit:
                    ups[index] = lax.ppermute(after(ups[index], before), "fsdp", up)
                    arrived[index].append((step, ups[index]))
                if step <= down_limit:
                    downs[index] = lax.ppermute(after(downs[index], before), "fsdp", down)
                    arrived[index].append((-step, downs[index]))
                if step == more:
                    far_totals[index] = sum(product(far_tokens, *a) for a in arrived[index][:-1])
                    arrived[index][-1] = (arrived[index][-1][0], after(arrived[index][-1][1], far_totals[index], delta_2))
                    far_totals[index] += product(far_tokens, *arrived[index][-1])
                for a in arrived[index][2 * step - 1 :]:
                    near_totals[index] += product(near_tokens, *a)
            if step == 2:
                tokens_2 = after(tokens_2, ups[1])
                tokens_3 = from_replica(tokens_2, 1)
                far_tokens = jnp.concatenate([tokens_2, tokens_3], axis=0)
                delta_2 = from_replica(after(delta, tokens_3), 2)

    pieces = [[], [], [], []]
    for near_total, far_total in zip(near_totals, far_totals):
        out = near_total.astype(jnp.bfloat16)
        far_out = far_total.astype(jnp.bfloat16)
        pieces[2].append(from_replica(far_out[:mine], 2))
        pieces[3].append(from_replica(far_out[mine:], 3))
        pieces[0].append(out[:mine])
        pieces[1].append(from_replica(out[mine:], 1))

    delta_1 = from_replica(after(delta, delta_2), 1)
    delta_3 = from_replica(after(delta_2, delta_1), 1)
    new_outers = subtract(where, outers, [delta, delta_1, delta_2, delta_3])
    projected = place(where, pieces, widths)
    new_moment = jnp.concatenate(new_moments, axis=1)
    edge = widths[0] + widths[1]
    return (
        projected,
        *new_outers,
        new_moment[:, : widths[0]],
        new_moment[:, widths[0] : edge],
        new_moment[:, edge:],
    )


def solution(mesh):
    placed = (
        P(("replica", "fsdp"), None),
        P("replica", "fsdp", None),
        P("replica", "fsdp", None),
        P("replica", "fsdp", None),
        P("fsdp", None),
        P("fsdp", None),
        P("fsdp", None),
        P("fsdp", "replica"),
        P("fsdp", "replica"),
        P("fsdp", "replica"),
    )
    return jax.shard_map(
        per_device,
        mesh=mesh,
        in_specs=placed,
        out_specs=(
            P(("replica", "fsdp"), None),
            P("fsdp", None),
            P("fsdp", None),
            P("fsdp", None),
            P("fsdp", "replica"),
            P("fsdp", "replica"),
            P("fsdp", "replica"),
        ),
        check_vma=False,
    )
```

time: 321 us -> 90 us (0.28)
  waiting for transfers between devices: 262 us -> 43.7 us
  starting transfers between devices: 0.21 us -> 26.3 us
  blocking collectives: 13.5 us -> 0 us
  between operations: 13.9 us -> 1.05 us
  other arithmetic: 14 us -> 1.19 us
  local copies, waits for them, and re-layouts: 8.31 us -> 1.32 us
  Pallas kernels: 0 us -> 6.59 us
    all_gather x2 -> x0, waiting for transfers between devices: 192 us -> none  [the longest x1 177 us: per_device(): fresh = lax.all_gather(local_fresh, 'fsdp', axis=0, tiled=True)]
    reduce_scatter x3 -> x0, waiting for transfers between devices: 69.5 us -> none  [per_device(): lax.psum_scatter(differences, 'replica', scatter_dimension=1, tiled=True)]
    ppermute x0 -> x31, waiting for transfers between devices: none -> 43.7 us  [the longest x17 30.5 us: from_replica(): return lax.ppermute(x, 'replica', [(i, i ^ distance) for i in range(count)])]
    ppermute x0 -> x31, starting transfers between devices: none -> 26.3 us  [the longest x17 11 us: from_replica(): return lax.ppermute(x, 'replica', [(i, i ^ distance) for i in range(count)])]
    all_gather x2 -> x0, blocking collectives: 13.5 us -> none  [per_device(): lax.all_gather(tuple(owned_outer), 'replica', axis=1, tiled=True)]
    sub x6 -> x0, other arithmetic: 10.9 us -> none  [the longest x3 5.53 us: per_device(): own_slice - LEARN_RATE * (pseudo + MOMENTUM_BETA * new_moment)]
    unnamed x30 -> x16, local copies, waits for them, and re-layouts: 8.31 us -> 0.24 us
    pallas_call x0 -> x4, Pallas kernels: none -> 6.59 us  [the longest x2 3.15 us: sums_call(): pl.pallas_call(kernel, out_shape=shapes, in_specs=[pl.BlockSpec(memory_sp...]
  transfers between devices with their start and end apart: 5 -> 31, of which waited for: 5 -> 20; matrix products, arithmetic and copies ran while one was open for 2% -> 13% of each run, Pallas kernels for 0% -> 3%
where the time goes in v1:
time: 90 us; the launch traced here: 89.8 us
  waiting for transfers between devices  43.7 us (49%)
  starting transfers between devices  26.3 us (29%)
  matrix products  9.64 us (11%)
  Pallas kernels  6.59 us (7%)
  local copies, waits for them, and re-layouts  1.32 us (1%)
  other arithmetic  1.19 us (1%)
  between operations  1.05 us (1%)
    ppermute x17, waiting for transfers between devices, from_replica(): return lax.ppermute(x, 'replica', [(i, i ^ distance) for i in range(count)])  30.5 us
    ppermute x17, starting transfers between devices, from_replica(): return lax.ppermute(x, 'replica', [(i, i ^ distance) for i in range(count)])  11 us
    ppermute x7, starting transfers between devices, per_device(): downs[index] = lax.ppermute(after(downs[index], before), 'fsdp', down)  10.3 us
    dot_general x32, matrix products, product(): return jnp.dot(lanes, block, preferred_element_type=jnp.float32)  9.64 us
    ppermute x7, waiting for transfers between devices, per_device(): downs[index] = lax.ppermute(after(downs[index], before), 'fsdp', down)  7.83 us
    ppermute x7, waiting for transfers between devices, per_device(): ups[index] = lax.ppermute(after(ups[index], before), 'fsdp', up)  5.41 us
    ppermute x7, starting transfers between devices, per_device(): ups[index] = lax.ppermute(after(ups[index], before), 'fsdp', up)  4.99 us
    pallas_call x2, Pallas kernels, sums_call(): pl.pallas_call(kernel, out_shape=shapes, in_specs=[pl.BlockSpec(memory_sp...  3.15 us
  transfers between devices with their start and end apart: 31, of which 20 were waited for; matrix products, arithmetic and copies ran while one was open for 13% of the time, Pallas kernels for 3%

profile of v1, /device:TPU:0, one launch (start us, length us, event | category | flops | bytes accessed | tf_op | source)
XLA Modules:
  0.0 89.8 jit_solution(5683503558464382973)
XLA Ops:
  0.6 0.5 collective-permute-start
  1.2 0.4 collective-permute-start.2
  1.7 2.4 %collective-permute-done.1.refs_4_ = bf16[256,512]{1,0:T(8,128)(2,1)S(1)} collective-permute-done((bf16[256,512]{1,0:T(8,128)(2,1)}, bf16[256,512]{1,0:T(8,128)(2,1)S(1)}, u32[]{:S(2)}, u32[]{:S(2)}) %collective-permute-start.1) | collective-permute-done | bytes 262176 | tf_op jit(solution)/shard_map/ppermute | solution.py:18
  4.0 0.4 collective-permute-done.2.refs_5_
  4.4 1.6 %far_sums.1 = (bf16[256,384]{1,0:T(8,128)(2,1)S(1)}, bf16[256,384]{1,0:T(8,128)(2,1)S(1)}) custom-call(s32[1]{0:T(128)} %bitcast.where, bf16[256,2048]{1,0:T(8,128)(2,1)} %bitcast.37, bf16[256,512]{1,0:T(8,128)(2,1)} %bitcast.40, bf16[256,512]{1,0:T(8,128)(2,1)} %bitcast.43, bf16[256,2048]{1,0:T(8,128)(2,1)S(1)} %collective-permute-done.refs_3_, ...), custom_call_target="tpu_custom_call" | custom-call | tf_op jit(solution)/shard_map/far_sums/pallas_call | solution.py:95
  6.0 2.9 %collective-permute-start.4 = (bf16[256,384]{1,0:T(8,128)(2,1)S(1)}, bf16[256,384]{1,0:T(8,128)(2,1)S(1)}, u32[]{:S(2)}, u32[]{:S(2)}) collective-permute-start(bf16[256,384]{1,0:T(8,128)(2,1)S(1)} %get-tuple-element.38), channel_id=1, source_target_pairs={{0,16},{8,24},{16,0},{24,8},{1,17},{9,25},{17,1},{25,9},{2,18},{10... | collective-permute-start | bytes 589832 | tf_op jit(solution)/shard_map/ppermute | solution.py:18
  9.2 1.6 %near_sums.1 = (f32[256,384]{1,0:T(8,128)S(1)}, f32[256,384]{1,0:T(8,128)S(1)}, f32[256,384]{1,0:T(8,128)S(1)}, f32[256,384]{1,0:T(8,128)S(1)}, f32[256,384]{1,0:T(8,128)S(1)}, /*index=5*/f32[256,384]{1,0:T(8,128)S(1)}) custom-call(s32[1]{0:T(128)} %bitcast.where, bf16[256,2048]{1,0:T(8,128)(2,1)} %bitcast.38, bf16[256,512]{1,0:T(8,128)(2,1)} %bitcast.41, ...), custom_call_target="tpu_custom_call" | custom-call | tf_op jit(solution)/shard_map/near_sums/pallas_call | solution.py:95
  10.8 3.9 %collective-permute-done.4 = bf16[256,384]{1,0:T(8,128)(2,1)S(1)} collective-permute-done((bf16[256,384]{1,0:T(8,128)(2,1)S(1)}, bf16[256,384]{1,0:T(8,128)(2,1)S(1)}, u32[]{:S(2)}, u32[]{:S(2)}) %collective-permute-start.4) | collective-permute-done | bytes 196640 | tf_op jit(solution)/shard_map/ppermute | solution.py:18
  14.6 3.7 %collective-permute-done.12 = bf16[256,384]{1,0:T(8,128)(2,1)S(1)} collective-permute-done((bf16[256,384]{1,0:T(8,128)(2,1)S(1)}, bf16[256,384]{1,0:T(8,128)(2,1)S(1)}, u32[]{:S(2)}, u32[]{:S(2)}) %collective-permute-start.12) | collective-permute-done | bytes 196640 | tf_op jit(solution)/shard_map/ppermute | solution.py:18
  18.4 1.7 %collective-permute-start.13 = (bf16[256,2048]{1,0:T(8,128)(2,1)S(1)}, bf16[256,2048]{1,0:T(8,128)(2,1)S(1)}, u32[]{:S(2)}, u32[]{:S(2)}) collective-permute-start(bf16[256,2048]{1,0:T(8,128)(2,1)S(1)} %copy-done.6), channel_id=1, source_target_pairs={{0,16},{8,24},{16,0},{24,8},{1,17},{9,25},{17,1},{25,9},{2,18},{10... | collective-permute-start | bytes 3145736 | tf_op jit(solution)/shard_map/ppermute | solution.py:18
  20.4 0.9 pad_maximum_fusion
  21.7 1.6 %collective-permute-start.6 = (bf16[256,384]{1,0:T(8,128)(2,1)S(1)}, bf16[256,384]{1,0:T(8,128)(2,1)S(1)}, u32[]{:S(2)}, u32[]{:S(2)}) collective-permute-start(bf16[256,384]{1,0:T(8,128)(2,1)S(1)} %get-tuple-element.44), channel_id=1, source_target_pairs={{2,0},{4,2},{6,4},{7,6},{5,7},{3,5},{1,3},{0,1},{10,8},{12,10},{14... | collective-permute-start | bytes 589832 | tf_op jit(solution)/shard_map/ppermute | solution.py:227
  23.3 0.5 collective-permute-start.5
  24.1 1.6 %collective-permute-start.14 = (bf16[256,384]{1,0:T(8,128)(2,1)S(1)}, bf16[256,384]{1,0:T(8,128)(2,1)S(1)}, u32[]{:S(2)}, u32[]{:S(2)}) collective-permute-start(bf16[256,384]{1,0:T(8,128)(2,1)S(1)} %get-tuple-element.54), channel_id=1, source_target_pairs={{0,2},{2,4},{4,6},{6,7},{7,5},{5,3},{3,1},{1,0},{8,10},{10,12},{12... | collective-permute-start | bytes 589832 | tf_op jit(solution)/shard_map/ppermute | solution.py:224
  25.7 0.5 collective-permute-start.15
  26.2 2.5 %collective-permute-done.6 = bf16[256,384]{1,0:T(8,128)(2,1)S(1)} collective-permute-done((bf16[256,384]{1,0:T(8,128)(2,1)S(1)}, bf16[256,384]{1,0:T(8,128)(2,1)S(1)}, u32[]{:S(2)}, u32[]{:S(2)}) %collective-permute-start.6) | collective-permute-done | bytes 196640 | tf_op jit(solution)/shard_map/ppermute | solution.py:227
  29.0 1.9 %collective-permute-done.5 = bf16[256,384]{1,0:T(8,128)(2,1)S(1)} collective-permute-done((bf16[256,384]{1,0:T(8,128)(2,1)S(1)}, bf16[256,384]{1,0:T(8,128)(2,1)S(1)}, u32[]{:S(2)}, u32[]{:S(2)}) %collective-permute-start.5) | collective-permute-done | bytes 196640 | tf_op jit(solution)/shard_map/ppermute | solution.py:224
  31.2 1.6 %collective-permute-start.8 = (bf16[256,384]{1,0:T(8,128)(2,1)S(1)}, bf16[256,384]{1,0:T(8,128)(2,1)S(1)}, u32[]{:S(2)}, u32[]{:S(2)}) collective-permute-start(bf16[256,384]{1,0:T(8,128)(2,1)S(1)} %collective-permute-done.6), channel_id=1, source_target_pairs={{2,0},{4,2},{6,4},{7,6},{5,7},{3,5},{1,3},{0,1},{10,8},{12,10},{14... | collective-permute-start | bytes 589832 | tf_op jit(solution)/shard_map/ppermute | solution.py:227
  32.9 0.4 collective-permute-start.7
  33.9 1.0 %collective-permute-done.14 = bf16[256,384]{1,0:T(8,128)(2,1)S(1)} collective-permute-done((bf16[256,384]{1,0:T(8,128)(2,1)S(1)}, bf16[256,384]{1,0:T(8,128)(2,1)S(1)}, u32[]{:S(2)}, u32[]{:S(2)}) %collective-permute-start.14) | collective-permute-done | bytes 196640 | tf_op jit(solution)/shard_map/ppermute | solution.py:224
  35.2 0.7 collective-permute-start.16
  35.9 1.4 %collective-permute-start.19 = (bf16[256,384]{1,0:T(8,128)(2,1)S(1)}, bf16[256,384]{1,0:T(8,128)(2,1)S(1)}, u32[]{:S(2)}, u32[]{:S(2)}) collective-permute-start(bf16[256,384]{1,0:T(8,128)(2,1)S(1)} %collective-permute-done.15), channel_id=1, source_target_pairs={{2,0},{4,2},{6,4},{7,6},{5,7},{3,5},{1,3},{0,1},{10,8},{12,10},{14... | collective-permute-start | bytes 589832 | tf_op jit(solution)/shard_map/ppermute | solution.py:227
  37.3 1.8 %collective-permute-done.8 = bf16[256,384]{1,0:T(8,128)(2,1)S(1)} collective-permute-done((bf16[256,384]{1,0:T(8,128)(2,1)S(1)}, bf16[256,384]{1,0:T(8,128)(2,1)S(1)}, u32[]{:S(2)}, u32[]{:S(2)}) %collective-permute-start.8) | collective-permute-done | bytes 196640 | tf_op jit(solution)/shard_map/ppermute | solution.py:227
  39.7 1.6 %collective-permute-start.10 = (bf16[256,384]{1,0:T(8,128)(2,1)S(1)}, bf16[256,384]{1,0:T(8,128)(2,1)S(1)}, u32[]{:S(2)}, u32[]{:S(2)}) collective-permute-start(bf16[256,384]{1,0:T(8,128)(2,1)S(1)} %collective-permute-done.8), channel_id=1, source_target_pairs={{2,0},{4,2},{6,4},{7,6},{5,7},{3,5},{1,3},{0,1},{10,8},{12,10},{14... | collective-permute-start | bytes 589832 | tf_op jit(solution)/shard_map/ppermute | solution.py:227
  41.3 0.5 collective-permute-start.9
  41.8 1.3 %collective-permute-done.13 = bf16[256,2048]{1,0:T(8,128)(2,1)S(1)} collective-permute-done((bf16[256,2048]{1,0:T(8,128)(2,1)S(1)}, bf16[256,2048]{1,0:T(8,128)(2,1)S(1)}, u32[]{:S(2)}, u32[]{:S(2)}) %collective-permute-start.13) | collective-permute-done | bytes 1048608 | tf_op jit(solution)/shard_map/ppermute | solution.py:18
  44.0 1.6 %collective-permute-start.21 = (bf16[256,384]{1,0:T(8,128)(2,1)S(1)}, bf16[256,384]{1,0:T(8,128)(2,1)S(1)}, u32[]{:S(2)}, u32[]{:S(2)}) collective-permute-start(bf16[256,384]{1,0:T(8,128)(2,1)S(1)} %collective-permute-done.19), channel_id=1, source_target_pairs={{2,0},{4,2},{6,4},{7,6},{5,7},{3,5},{1,3},{0,1},{10,8},{12,10},{14... | collective-permute-start | bytes 589832 | tf_op jit(solution)/shard_map/ppermute | solution.py:227
  45.6 0.5 collective-permute-start.20
  46.5 0.5 collective-permute-done.9
  47.3 0.8 collective-permute-start.11
  48.1 3.3 %collective-permute-done.21 = bf16[256,384]{1,0:T(8,128)(2,1)S(1)} collective-permute-done((bf16[256,384]{1,0:T(8,128)(2,1)S(1)}, bf16[256,384]{1,0:T(8,128)(2,1)S(1)}, u32[]{:S(2)}, u32[]{:S(2)}) %collective-permute-start.21) | collective-permute-done | bytes 196640 | tf_op jit(solution)/shard_map/ppermute | solution.py:227
  51.6 1.7 %collective-permute-done.20 = bf16[256,384]{1,0:T(8,128)(2,1)S(1)} collective-permute-done((bf16[256,384]{1,0:T(8,128)(2,1)S(1)}, bf16[256,384]{1,0:T(8,128)(2,1)S(1)}, u32[]{:S(2)}, u32[]{:S(2)}) %collective-permute-start.20) | collective-permute-done | bytes 196640 | tf_op jit(solution)/shard_map/ppermute | solution.py:224
  53.6 2.0 %collective-permute-start.22 = (bf16[256,384]{1,0:T(8,128)(2,1)S(1)}, bf16[256,384]{1,0:T(8,128)(2,1)S(1)}, u32[]{:S(2)}, u32[]{:S(2)}) collective-permute-start(bf16[256,384]{1,0:T(8,128)(2,1)S(1)} %collective-permute-done.21), channel_id=1, source_target_pairs={{2,0},{4,2},{6,4},{7,6},{5,7},{3,5},{1,3},{0,1},{10,8},{12,10},{14... | collective-permute-start | bytes 589832 | tf_op jit(solution)/shard_map/ppermute | solution.py:227
  55.7 0.8 collective-permute-start.18
  61.0 4.1 %collective-permute-done.18.refs_2_ = bf16[256,768]{1,0:T(8,128)(2,1)S(1)} collective-permute-done((bf16[256,768]{1,0:T(8,128)(2,1)S(1)}, bf16[256,768]{1,0:T(8,128)(2,1)S(1)}, u32[]{:S(2)}, u32[]{:S(2)}) %collective-permute-start.18) | collective-permute-done | bytes 393248 | tf_op jit(solution)/shard_map/ppermute | solution.py:18
  66.2 0.5 collective-permute-start.24
  66.8 0.9 collective-permute-start.25
  68.0 0.4 collective-permute-done.29.refs_1_
  68.7 0.9 collective-permute-start.26
  69.6 0.8 collective-permute-start.27
  70.4 0.9 %collective-permute-start.28 = (bf16[256,384]{1,0:T(8,128)(2,1)S(1)}, bf16[256,384]{1,0:T(8,128)(2,1)S(1)}, u32[]{:S(2)}, u32[]{:S(2)}) collective-permute-start(bf16[256,384]{1,0:T(8,128)(2,1)S(1)} %get-tuple-element.77), channel_id=1, source_target_pairs={{0,24},{8,16},{16,8},{24,0},{1,25},{9,17},{17,9},{25,1},{2,26},{10... | collective-permute-start | bytes 589832 | tf_op jit(solution)/shard_map/ppermute | solution.py:18
  71.4 0.7 fusion.106
  72.1 2.5 %collective-permute-done.25.refs_4_ = bf16[256,384]{1,0:T(8,128)(2,1)S(1)} collective-permute-done((bf16[256,384]{1,0:T(8,128)(2,1)S(1)}, bf16[256,384]{1,0:T(8,128)(2,1)S(1)}, u32[]{:S(2)}, u32[]{:S(2)}) %collective-permute-start.25) | collective-permute-done | bytes 196640 | tf_op jit(solution)/shard_map/ppermute | solution.py:18
  74.6 4.2 %collective-permute-done.26.refs_5_ = bf16[256,384]{1,0:T(8,128)(2,1)S(1)} collective-permute-done((bf16[256,384]{1,0:T(8,128)(2,1)S(1)}, bf16[256,384]{1,0:T(8,128)(2,1)S(1)}, u32[]{:S(2)}, u32[]{:S(2)}) %collective-permute-start.26) | collective-permute-done | bytes 196640 | tf_op jit(solution)/shard_map/ppermute | solution.py:18
  78.8 3.3 %collective-permute-done.27.refs_6_ = bf16[256,384]{1,0:T(8,128)(2,1)S(1)} collective-permute-done((bf16[256,384]{1,0:T(8,128)(2,1)S(1)}, bf16[256,384]{1,0:T(8,128)(2,1)S(1)}, u32[]{:S(2)}, u32[]{:S(2)}) %collective-permute-start.27) | collective-permute-done | bytes 196640 | tf_op jit(solution)/shard_map/ppermute | solution.py:18
  82.1 4.2 %collective-permute-done.28.refs_7_ = bf16[256,384]{1,0:T(8,128)(2,1)S(1)} collective-permute-done((bf16[256,384]{1,0:T(8,128)(2,1)S(1)}, bf16[256,384]{1,0:T(8,128)(2,1)S(1)}, u32[]{:S(2)}, u32[]{:S(2)}) %collective-permute-start.28) | collective-permute-done | bytes 196640 | tf_op jit(solution)/shard_map/ppermute | solution.py:18
  86.3 1.4 %place_columns.1 = bf16[256,3072]{1,0:T(8,128)(2,1)} custom-call(s32[1]{0:T(128)} %bitcast.where, bf16[256,384]{1,0:T(8,128)(2,1)S(1)} %get-tuple-element.84.refs_0_, bf16[256,384]{1,0:T(8,128)(2,1)S(1)} %get-tuple-element.82.refs_1_, bf16[256,384]{1,0:T(8,128)(2,1)S(1)} %collective-permute-done.23.refs_2_, ...), custom_call_target="tpu_custom_call" | custom-call | tf_op jit(solution)/shard_map/place_columns/pallas_call | solution.py:148
  87.8 2.0 %outer_minus_delta.1 = (f32[256,2048]{1,0:T(8,128)}, f32[256,512]{1,0:T(8,128)}, f32[256,512]{1,0:T(8,128)}) custom-call(s32[1]{0:T(128)} %bitcast.where, f32[256,2048]{1,0:T(8,128)S(1)} %copy-done, f32[256,512]{1,0:T(8,128)S(1)} %copy-done.1, f32[256,512]{1,0:T(8,128)S(1)} %copy-done.2, bf16[256,768]{1,0:T(8,128)(2,1)S(1)} %pad_maximum_fusion.1.refs_0_, ...), custom_call_target="tpu_custom_call" | custom-call | tf_op jit(solution)/shard_map/outer_minus_delta/pallas_call | solution.py:123
  (77 shorter events, 11.7 us)
Async XLA Ops:
  0.6 3.8 %collective-permute-start = (bf16[256,2048]{1,0:T(8,128)(2,1)}, bf16[256,2048]{1,0:T(8,128)(2,1)S(1)}, u32[]{:S(2)}, u32[]{:S(2)}) collective-permute-start(bf16[256,2048]{1,0:T(8,128)(2,1)} %bitcast.36), channel_id=1, source_target_pairs={{0,8},{8,0},{16,24},{24,16},{1,9},{9,1},{17,25},{25,17},{2,10},{10... | collective-permute-start | bytes 3145736 | tf_op jit(solution)/shard_map/ppermute | solution.py:18
  1.1 2.9 %collective-permute-start.1 = (bf16[256,512]{1,0:T(8,128)(2,1)}, bf16[256,512]{1,0:T(8,128)(2,1)S(1)}, u32[]{:S(2)}, u32[]{:S(2)}) collective-permute-start(bf16[256,512]{1,0:T(8,128)(2,1)} %bitcast.39), channel_id=1, source_target_pairs={{0,8},{8,0},{16,24},{24,16},{1,9},{9,1},{17,25},{25,17},{2,10},{10... | collective-permute-start | bytes 786440 | tf_op jit(solution)/shard_map/ppermute | solution.py:18
  1.2 3.2 %collective-permute-start.2 = (bf16[256,512]{1,0:T(8,128)(2,1)}, bf16[256,512]{1,0:T(8,128)(2,1)S(1)}, u32[]{:S(2)}, u32[]{:S(2)}) collective-permute-start(bf16[256,512]{1,0:T(8,128)(2,1)} %bitcast.42), channel_id=1, source_target_pairs={{0,8},{8,0},{16,24},{24,16},{1,9},{9,1},{17,25},{25,17},{2,10},{10... | collective-permute-start | bytes 786440 | tf_op jit(solution)/shard_map/ppermute | solution.py:18
  4.4 4.6 %copy-start.6 = (bf16[256,2048]{1,0:T(8,128)(2,1)S(1)}, bf16[256,2048]{1,0:T(8,128)(2,1)}, u32[]{:S(2)}) copy-start(bf16[256,2048]{1,0:T(8,128)(2,1)} %param.10) | copy-start | bytes 3145732
  6.0 3.2 %copy-start.3 = (f32[256,512]{1,0:T(8,128)S(1)}, f32[256,512]{1,0:T(8,128)}, u32[]{:S(2)}) copy-start(f32[256,512]{1,0:T(8,128)} %refs_9_.1) | copy-start | bytes 1572868
  6.0 3.2 %copy-start.4 = (f32[256,128]{1,0:T(8,128)S(1)}, f32[256,128]{1,0:T(8,128)}, u32[]{:S(2)}) copy-start(f32[256,128]{1,0:T(8,128)} %refs_10_.1) | copy-start | bytes 393220
  6.0 3.2 %copy-start.5 = (f32[256,128]{1,0:T(8,128)S(1)}, f32[256,128]{1,0:T(8,128)}, u32[]{:S(2)}) copy-start(f32[256,128]{1,0:T(8,128)} %refs_11_.1) | copy-start | bytes 393220
  6.0 8.6 %collective-permute-start.4 = (bf16[256,384]{1,0:T(8,128)(2,1)S(1)}, bf16[256,384]{1,0:T(8,128)(2,1)S(1)}, u32[]{:S(2)}, u32[]{:S(2)}) collective-permute-start(bf16[256,384]{1,0:T(8,128)(2,1)S(1)} %get-tuple-element.38), channel_id=1, source_target_pairs={{0,16},{8,24},{16,0},{24,8},{1,17},{9,25},{17,1},{25,9},{2,18},{10... | collective-permute-start | bytes 589832 | tf_op jit(solution)/shard_map/ppermute | solution.py:18
  8.9 9.4 %collective-permute-start.12 = (bf16[256,384]{1,0:T(8,128)(2,1)S(1)}, bf16[256,384]{1,0:T(8,128)(2,1)S(1)}, u32[]{:S(2)}, u32[]{:S(2)}) collective-permute-start(bf16[256,384]{1,0:T(8,128)(2,1)S(1)} %get-tuple-element.39), channel_id=1, source_target_pairs={{0,16},{8,24},{16,0},{24,8},{1,17},{9,25},{17,1},{25,9},{2,18},{10... | collective-permute-start | bytes 589832 | tf_op jit(solution)/shard_map/ppermute | solution.py:18
  9.0 12.3 %collective-permute-start.3 = (bf16[256,2048]{1,0:T(8,128)(2,1)S(1)}, bf16[256,2048]{1,0:T(8,128)(2,1)S(1)}, u32[]{:S(2)}, u32[]{:S(2)}) collective-permute-start(bf16[256,2048]{1,0:T(8,128)(2,1)S(1)} %copy-done.6), channel_id=1, source_target_pairs={{0,8},{8,0},{16,24},{24,16},{1,9},{9,1},{17,25},{25,17},{2,10},{10... | collective-permute-start | bytes 3145736 | tf_op jit(solution)/shard_map/ppermute | solution.py:18
  18.4 24.7 %collective-permute-start.13 = (bf16[256,2048]{1,0:T(8,128)(2,1)S(1)}, bf16[256,2048]{1,0:T(8,128)(2,1)S(1)}, u32[]{:S(2)}, u32[]{:S(2)}) collective-permute-start(bf16[256,2048]{1,0:T(8,128)(2,1)S(1)} %copy-done.6), channel_id=1, source_target_pairs={{0,16},{8,24},{16,0},{24,8},{1,17},{9,25},{17,1},{25,9},{2,18},{10... | collective-permute-start | bytes 3145736 | tf_op jit(solution)/shard_map/ppermute | solution.py:18
  21.7 7.0 %collective-permute-start.6 = (bf16[256,384]{1,0:T(8,128)(2,1)S(1)}, bf16[256,384]{1,0:T(8,128)(2,1)S(1)}, u32[]{:S(2)}, u32[]{:S(2)}) collective-permute-start(bf16[256,384]{1,0:T(8,128)(2,1)S(1)} %get-tuple-element.44), channel_id=1, source_target_pairs={{2,0},{4,2},{6,4},{7,6},{5,7},{3,5},{1,3},{0,1},{10,8},{12,10},{14... | collective-permute-start | bytes 589832 | tf_op jit(solution)/shard_map/ppermute | solution.py:227
  23.3 7.6 %collective-permute-start.5 = (bf16[256,384]{1,0:T(8,128)(2,1)S(1)}, bf16[256,384]{1,0:T(8,128)(2,1)S(1)}, u32[]{:S(2)}, u32[]{:S(2)}) collective-permute-start(bf16[256,384]{1,0:T(8,128)(2,1)S(1)} %get-tuple-element.44), channel_id=1, source_target_pairs={{0,2},{2,4},{4,6},{6,7},{7,5},{5,3},{3,1},{1,0},{8,10},{10,12},{12... | collective-permute-start | bytes 589832 | tf_op jit(solution)/shard_map/ppermute | solution.py:224
  24.1 10.8 %collective-permute-start.14 = (bf16[256,384]{1,0:T(8,128)(2,1)S(1)}, bf16[256,384]{1,0:T(8,128)(2,1)S(1)}, u32[]{:S(2)}, u32[]{:S(2)}) collective-permute-start(bf16[256,384]{1,0:T(8,128)(2,1)S(1)} %get-tuple-element.54), channel_id=1, source_target_pairs={{0,2},{2,4},{4,6},{6,7},{7,5},{5,3},{3,1},{1,0},{8,10},{10,12},{12... | collective-permute-start | bytes 589832 | tf_op jit(solution)/shard_map/ppermute | solution.py:224
  25.7 7.8 %collective-permute-start.15 = (bf16[256,384]{1,0:T(8,128)(2,1)S(1)}, bf16[256,384]{1,0:T(8,128)(2,1)S(1)}, u32[]{:S(2)}, u32[]{:S(2)}) collective-permute-start(bf16[256,384]{1,0:T(8,128)(2,1)S(1)} %get-tuple-element.54), channel_id=1, source_target_pairs={{2,0},{4,2},{6,4},{7,6},{5,7},{3,5},{1,3},{0,1},{10,8},{12,10},{14... | collective-permute-start | bytes 589832 | tf_op jit(solution)/shard_map/ppermute | solution.py:227
  31.2 7.8 %collective-permute-start.8 = (bf16[256,384]{1,0:T(8,128)(2,1)S(1)}, bf16[256,384]{1,0:T(8,128)(2,1)S(1)}, u32[]{:S(2)}, u32[]{:S(2)}) collective-permute-start(bf16[256,384]{1,0:T(8,128)(2,1)S(1)} %collective-permute-done.6), channel_id=1, source_target_pairs={{2,0},{4,2},{6,4},{7,6},{5,7},{3,5},{1,3},{0,1},{10,8},{12,10},{14... | collective-permute-start | bytes 589832 | tf_op jit(solution)/shard_map/ppermute | solution.py:227
  32.9 6.5 %collective-permute-start.7 = (bf16[256,384]{1,0:T(8,128)(2,1)S(1)}, bf16[256,384]{1,0:T(8,128)(2,1)S(1)}, u32[]{:S(2)}, u32[]{:S(2)}) collective-permute-start(bf16[256,384]{1,0:T(8,128)(2,1)S(1)} %collective-permute-done.5), channel_id=1, source_target_pairs={{0,2},{2,4},{4,6},{6,7},{7,5},{5,3},{3,1},{1,0},{8,10},{10,12},{12... | collective-permute-start | bytes 589832 | tf_op jit(solution)/shard_map/ppermute | solution.py:224
  35.2 8.1 %collective-permute-start.16 = (bf16[256,384]{1,0:T(8,128)(2,1)S(1)}, bf16[256,384]{1,0:T(8,128)(2,1)S(1)}, u32[]{:S(2)}, u32[]{:S(2)}) collective-permute-start(bf16[256,384]{1,0:T(8,128)(2,1)S(1)} %collective-permute-done.14), channel_id=1, source_target_pairs={{0,2},{2,4},{4,6},{6,7},{7,5},{5,3},{3,1},{1,0},{8,10},{10,12},{12... | collective-permute-start | bytes 589832 | tf_op jit(solution)/shard_map/ppermute | solution.py:224
  35.9 7.4 %collective-permute-start.19 = (bf16[256,384]{1,0:T(8,128)(2,1)S(1)}, bf16[256,384]{1,0:T(8,128)(2,1)S(1)}, u32[]{:S(2)}, u32[]{:S(2)}) collective-permute-start(bf16[256,384]{1,0:T(8,128)(2,1)S(1)} %collective-permute-done.15), channel_id=1, source_target_pairs={{2,0},{4,2},{6,4},{7,6},{5,7},{3,5},{1,3},{0,1},{10,8},{12,10},{14... | collective-permute-start | bytes 589832 | tf_op jit(solution)/shard_map/ppermute | solution.py:227
  39.7 6.5 %collective-permute-start.10 = (bf16[256,384]{1,0:T(8,128)(2,1)S(1)}, bf16[256,384]{1,0:T(8,128)(2,1)S(1)}, u32[]{:S(2)}, u32[]{:S(2)}) collective-permute-start(bf16[256,384]{1,0:T(8,128)(2,1)S(1)} %collective-permute-done.8), channel_id=1, source_target_pairs={{2,0},{4,2},{6,4},{7,6},{5,7},{3,5},{1,3},{0,1},{10,8},{12,10},{14... | collective-permute-start | bytes 589832 | tf_op jit(solution)/shard_map/ppermute | solution.py:227
  41.3 5.7 %collective-permute-start.9 = (bf16[256,384]{1,0:T(8,128)(2,1)S(1)}, bf16[256,384]{1,0:T(8,128)(2,1)S(1)}, u32[]{:S(2)}, u32[]{:S(2)}) collective-permute-start(bf16[256,384]{1,0:T(8,128)(2,1)S(1)} %collective-permute-done.7), channel_id=1, source_target_pairs={{0,2},{2,4},{4,6},{6,7},{7,5},{5,3},{3,1},{1,0},{8,10},{10,12},{12... | collective-permute-start | bytes 589832 | tf_op jit(solution)/shard_map/ppermute | solution.py:224
  43.3 12.3 %collective-permute-start.17 = (bf16[256,2048]{1,0:T(8,128)(2,1)S(1)}, bf16[256,2048]{1,0:T(8,128)(2,1)S(1)}, u32[]{:S(2)}, u32[]{:S(2)}) collective-permute-start(bf16[256,2048]{1,0:T(8,128)(2,1)S(1)} %collective-permute-done.13), channel_id=1, source_target_pairs={{0,8},{8,0},{16,24},{24,16},{1,9},{9,1},{17,25},{25,17},{2,10},{10... | collective-permute-start | bytes 3145736 | tf_op jit(solution)/shard_map/ppermute | solution.py:18
  44.0 7.4 %collective-permute-start.21 = (bf16[256,384]{1,0:T(8,128)(2,1)S(1)}, bf16[256,384]{1,0:T(8,128)(2,1)S(1)}, u32[]{:S(2)}, u32[]{:S(2)}) collective-permute-start(bf16[256,384]{1,0:T(8,128)(2,1)S(1)} %collective-permute-done.19), channel_id=1, source_target_pairs={{2,0},{4,2},{6,4},{7,6},{5,7},{3,5},{1,3},{0,1},{10,8},{12,10},{14... | collective-permute-start | bytes 589832 | tf_op jit(solution)/shard_map/ppermute | solution.py:227
  45.6 7.7 %collective-permute-start.20 = (bf16[256,384]{1,0:T(8,128)(2,1)S(1)}, bf16[256,384]{1,0:T(8,128)(2,1)S(1)}, u32[]{:S(2)}, u32[]{:S(2)}) collective-permute-start(bf16[256,384]{1,0:T(8,128)(2,1)S(1)} %collective-permute-done.16), channel_id=1, source_target_pairs={{0,2},{2,4},{4,6},{6,7},{7,5},{5,3},{3,1},{1,0},{8,10},{10,12},{12... | collective-permute-start | bytes 589832 | tf_op jit(solution)/shard_map/ppermute | solution.py:224
  47.3 13.7 %collective-permute-start.11 = (bf16[256,384]{1,0:T(8,128)(2,1)S(1)}, bf16[256,384]{1,0:T(8,128)(2,1)S(1)}, u32[]{:S(2)}, u32[]{:S(2)}) collective-permute-start(bf16[256,384]{1,0:T(8,128)(2,1)S(1)} %collective-permute-done.9), channel_id=1, source_target_pairs={{0,2},{2,4},{4,6},{6,7},{7,5},{5,3},{3,1},{1,0},{8,10},{10,12},{12... | collective-permute-start | bytes 589832 | tf_op jit(solution)/shard_map/ppermute | solution.py:224
  53.6 12.1 %collective-permute-start.22 = (bf16[256,384]{1,0:T(8,128)(2,1)S(1)}, bf16[256,384]{1,0:T(8,128)(2,1)S(1)}, u32[]{:S(2)}, u32[]{:S(2)}) collective-permute-start(bf16[256,384]{1,0:T(8,128)(2,1)S(1)} %collective-permute-done.21), channel_id=1, source_target_pairs={{2,0},{4,2},{6,4},{7,6},{5,7},{3,5},{1,3},{0,1},{10,8},{12,10},{14... | collective-permute-start | bytes 589832 | tf_op jit(solution)/shard_map/ppermute | solution.py:227
  55.7 9.4 %collective-permute-start.18 = (bf16[256,768]{1,0:T(8,128)(2,1)S(1)}, bf16[256,768]{1,0:T(8,128)(2,1)S(1)}, u32[]{:S(2)}, u32[]{:S(2)}) collective-permute-start(bf16[256,768]{1,0:T(8,128)(2,1)S(1)} %pad_maximum_fusion.1.refs_0_), channel_id=1, source_target_pairs={{0,16},{8,24},{16,0},{24,8},{1,17},{9,25},{17,1},{25,9},{2,18},{10... | collective-permute-start | bytes 1179656 | tf_op jit(solution)/shard_map/ppermute | solution.py:18
  66.1 3.5 %collective-permute-start.23 = (bf16[256,384]{1,0:T(8,128)(2,1)S(1)}, bf16[256,384]{1,0:T(8,128)(2,1)S(1)}, u32[]{:S(2)}, u32[]{:S(2)}) collective-permute-start(bf16[256,384]{1,0:T(8,128)(2,1)S(1)} %get-tuple-element.83), channel_id=1, source_target_pairs={{0,8},{8,0},{16,24},{24,16},{1,9},{9,1},{17,25},{25,17},{2,10},{10... | collective-permute-start | bytes 589832 | tf_op jit(solution)/shard_map/ppermute | solution.py:18
  66.2 4.2 %collective-permute-start.24 = (bf16[256,384]{1,0:T(8,128)(2,1)S(1)}, bf16[256,384]{1,0:T(8,128)(2,1)S(1)}, u32[]{:S(2)}, u32[]{:S(2)}) collective-permute-start(bf16[256,384]{1,0:T(8,128)(2,1)S(1)} %get-tuple-element.81), channel_id=1, source_target_pairs={{0,8},{8,0},{16,24},{24,16},{1,9},{9,1},{17,25},{25,17},{2,10},{10... | collective-permute-start | bytes 589832 | tf_op jit(solution)/shard_map/ppermute | solution.py:18
  66.7 1.8 %collective-permute-start.29 = (bf16[256,768]{1,0:T(8,128)(2,1)S(1)}, bf16[256,768]{1,0:T(8,128)(2,1)S(1)}, u32[]{:S(2)}, u32[]{:S(2)}) collective-permute-start(bf16[256,768]{1,0:T(8,128)(2,1)S(1)} %pad_maximum_fusion.1.refs_0_), channel_id=1, source_target_pairs={{0,8},{8,0},{16,24},{24,16},{1,9},{9,1},{17,25},{25,17},{2,10},{10... | collective-permute-start | bytes 1179656 | tf_op jit(solution)/shard_map/ppermute | solution.py:18
  66.8 7.8 %collective-permute-start.25 = (bf16[256,384]{1,0:T(8,128)(2,1)S(1)}, bf16[256,384]{1,0:T(8,128)(2,1)S(1)}, u32[]{:S(2)}, u32[]{:S(2)}) collective-permute-start(bf16[256,384]{1,0:T(8,128)(2,1)S(1)} %get-tuple-element.80), channel_id=1, source_target_pairs={{0,16},{8,24},{16,0},{24,8},{1,17},{9,25},{17,1},{25,9},{2,18},{10... | collective-permute-start | bytes 589832 | tf_op jit(solution)/shard_map/ppermute | solution.py:18
  68.0 19.8 %copy-start = (f32[256,2048]{1,0:T(8,128)S(1)}, f32[256,2048]{1,0:T(8,128)}, u32[]{:S(2)}) copy-start(f32[256,2048]{1,0:T(8,128)} %outer_q.1) | copy-start | bytes 6291460
  68.0 19.8 %copy-start.1 = (f32[256,512]{1,0:T(8,128)S(1)}, f32[256,512]{1,0:T(8,128)}, u32[]{:S(2)}) copy-start(f32[256,512]{1,0:T(8,128)} %outer_k.1) | copy-start | bytes 1572868
  68.0 19.7 %copy-start.2 = (f32[256,512]{1,0:T(8,128)S(1)}, f32[256,512]{1,0:T(8,128)}, u32[]{:S(2)}) copy-start(f32[256,512]{1,0:T(8,128)} %outer_v.1) | copy-start | bytes 1572868
  68.5 19.3 %collective-permute-start.30 = (bf16[256,768]{1,0:T(8,128)(2,1)S(1)}, bf16[256,768]{1,0:T(8,128)(2,1)S(1)}, u32[]{:S(2)}, u32[]{:S(2)}) collective-permute-start(bf16[256,768]{1,0:T(8,128)(2,1)S(1)} %collective-permute-done.18.refs_2_), channel_id=1, source_target_pairs={{0,8},{8,0},{16,24},{24,16},{1,9},{9,1},{17,25},{25,17},{2,10},{10... | collective-permute-start | bytes 1179656 | tf_op jit(solution)/shard_map/ppermute | solution.py:18
  68.7 10.1 %collective-permute-start.26 = (bf16[256,384]{1,0:T(8,128)(2,1)S(1)}, bf16[256,384]{1,0:T(8,128)(2,1)S(1)}, u32[]{:S(2)}, u32[]{:S(2)}) collective-permute-start(bf16[256,384]{1,0:T(8,128)(2,1)S(1)} %get-tuple-element.78), channel_id=1, source_target_pairs={{0,16},{8,24},{16,0},{24,8},{1,17},{9,25},{17,1},{25,9},{2,18},{10... | collective-permute-start | bytes 589832 | tf_op jit(solution)/shard_map/ppermute | solution.py:18
  69.6 12.5 %collective-permute-start.27 = (bf16[256,384]{1,0:T(8,128)(2,1)S(1)}, bf16[256,384]{1,0:T(8,128)(2,1)S(1)}, u32[]{:S(2)}, u32[]{:S(2)}) collective-permute-start(bf16[256,384]{1,0:T(8,128)(2,1)S(1)} %get-tuple-element.79), channel_id=1, source_target_pairs={{0,24},{8,16},{16,8},{24,0},{1,25},{9,17},{17,9},{25,1},{2,26},{10... | collective-permute-start | bytes 589832 | tf_op jit(solution)/shard_map/ppermute | solution.py:18
  70.4 15.9 %collective-permute-start.28 = (bf16[256,384]{1,0:T(8,128)(2,1)S(1)}, bf16[256,384]{1,0:T(8,128)(2,1)S(1)}, u32[]{:S(2)}, u32[]{:S(2)}) collective-permute-start(bf16[256,384]{1,0:T(8,128)(2,1)S(1)} %get-tuple-element.77), channel_id=1, source_target_pairs={{0,24},{8,16},{16,8},{24,0},{1,25},{9,17},{17,9},{25,1},{2,26},{10... | collective-permute-start | bytes 589832 | tf_op jit(solution)/shard_map/ppermute | solution.py:18

commit v2 on v0

v2 whole, which is shorter than its diff:
```python
import functools

import jax
import jax.numpy as jnp
from jax import lax
from jax.experimental import pallas as pl
from jax.experimental.pallas import tpu as pltpu
from jax.sharding import PartitionSpec as P

LEARN_RATE = 0.7
MOMENTUM_BETA = 0.9
SMALL_VMEM = 20 * 1024 * 1024
SHORTEST_RING = 8
LONGEST_RING = 16


def from_replica(x, distance):
    count = lax.axis_size("replica")
    return lax.ppermute(x, "replica", [(i, i ^ distance) for i in range(count)])


def ring_member(p, n):
    return 2 * p if p < n // 2 else 2 * (n - 1 - p) + 1


def source_of(row, steps, n):
    p = jnp.where(row % 2 == 0, row // 2, n - 1 - row // 2)
    p = (p - steps + n) % n
    return jnp.where(p < n // 2, 2 * p, 2 * (n - 1 - p) + 1)


def after(x, *others):
    return lax.optimization_barrier((x, *others))[0]


def fetch(sources, buffers, sems):
    copies = [pltpu.make_async_copy(a, b, sems.at[i]) for i, (a, b) in enumerate(zip(sources, buffers))]
    for copy in copies:
        copy.start()
    for copy in copies:
        copy.wait()


def columns_at(ref, block, width):
    return ref.at[:, pl.ds(pl.multiple_of(block * width, width), width)]


def in_hbm(arrays):
    return [pltpu.with_memory_space_constraint(a, pltpu.HBM) for a in arrays]


def spread(pieces, outs):
    edges = [0]
    for piece in pieces:
        edges.append(edges[-1] + piece.shape[1])
    left = 0
    for out in outs:
        right = left + out.shape[1]
        for piece, start in zip(pieces, edges):
            low, high = max(left, start), min(right, start + piece.shape[1])
            if low < high:
                out[:, low - left : high - left] = piece[:, low - start : high - start].astype(out.dtype)
        left = right


def columns_call(kernel, name, where, arrays, shapes, buffers):
    return pl.pallas_call(
        kernel,
        out_shape=shapes,
        in_specs=[pl.BlockSpec(memory_space=pltpu.SMEM)] + [pl.BlockSpec(memory_space=pl.ANY)] * len(arrays),
        out_specs=[pl.BlockSpec(memory_space=pltpu.VMEM)] * len(shapes),
        scratch_shapes=[*buffers, pltpu.SemaphoreType.DMA((len(arrays) * 2,))],
        compiler_params=pltpu.CompilerParams(vmem_limit_bytes=SMALL_VMEM),
        name=name,
    )(where, *in_hbm(arrays))


def pack_kernel(widths, distances, where, *refs):
    sources, outs, sems = refs[: len(widths)], refs[len(widths) : -1], refs[-1]
    views, targets = [], []
    for distance, out in zip(distances, outs):
        left = 0
        for source, width in zip(sources, widths):
            views.append(columns_at(source, lax.bitwise_xor(where[0], distance), width))
            targets.append(out.at[:, pl.ds(left, width)])
            left += width
    fetch(views, targets, sems)


def pack(where, arrays, widths, distances, name):
    shapes = [jax.ShapeDtypeStruct((arrays[0].shape[0], sum(widths)), arrays[0].dtype) for _ in distances]
    kernel = functools.partial(pack_kernel, widths, distances)
    return columns_call(kernel, name, where, arrays, shapes, [])


def half_kernel(distance, where, *refs):
    sources, outs, buffers, sems = refs[:6], refs[6:-7], refs[-7:-1], refs[-1]
    block = lax.bitwise_xor(where[0], distance)
    fetch([columns_at(r, block, b.shape[1]) for r, b in zip(sources, buffers)], buffers, sems)
    left = 0
    for inner, outer in zip(buffers[:3], buffers[3:]):
        columns = pl.ds(left, outer.shape[1])
        base = outer[...]
        outs[0][:, columns] = base - inner[...].astype(jnp.float32)
        outs[1][:, columns] = base
        left += outer.shape[1]


def own_kernel(count, half, outer, sibling, remote, moment_q, moment_k, moment_v, *outs):
    delta, new_moments = outs[0], outs[1:]
    left = 0
    for moment, new in zip((moment_q, moment_k, moment_v), new_moments):
        columns = pl.ds(left, moment.shape[1])
        own = half[:, columns] + (outer[:, columns] - sibling[:, columns].astype(jnp.float32))
        pseudo = (own + remote[:, columns].astype(jnp.float32)) / count
        new_moment = MOMENTUM_BETA * moment[...] + pseudo
        step = LEARN_RATE * (pseudo + MOMENTUM_BETA * new_moment)
        new[...] = new_moment
        delta[:, columns] = step.astype(jnp.bfloat16)
        left += moment.shape[1]


def own_step(half, outer, sibling, remote, moments, count):
    shapes = [jax.ShapeDtypeStruct(half.shape, jnp.bfloat16)]
    shapes += [jax.ShapeDtypeStruct(m.shape, jnp.float32) for m in moments]
    return pl.pallas_call(
        functools.partial(own_kernel, count),
        out_shape=shapes,
        in_specs=[pl.BlockSpec(memory_space=pltpu.VMEM)] * 7,
        out_specs=[pl.BlockSpec(memory_space=pltpu.VMEM)] * len(shapes),
        compiler_params=pltpu.CompilerParams(vmem_limit_bytes=SMALL_VMEM),
        name="own_step",
    )(half, outer, sibling, remote, *moments)


def fresh_kernel(count, first, half, outer, sibling, remote, moment_q, moment_k, moment_v, out):
    left, last = 0, first + out.shape[1]
    for moment in (moment_q, moment_k, moment_v):
        low, high = max(left, first), min(left + moment.shape[1], last)
        if low < high:
            columns = pl.ds(low, high - low)
            own = half[:, columns] + (outer[:, columns] - sibling[:, columns].astype(jnp.float32))
            pseudo = (own + remote[:, low - first : high - first].astype(jnp.float32)) / count
            new_moment = MOMENTUM_BETA * moment[:, low - left : high - left] + pseudo
            step = LEARN_RATE * (pseudo + MOMENTUM_BETA * new_moment)
            out[:, low - first : high - first] = (outer[:, columns] - step).astype(jnp.bfloat16)
        left += moment.shape[1]


def fresh_columns(half, outer, sibling, remote, moments, first, count):
    return pl.pallas_call(
        functools.partial(fresh_kernel, count, first),
        out_shape=jax.ShapeDtypeStruct(remote.shape, jnp.bfloat16),
        in_specs=[pl.BlockSpec(memory_space=pltpu.VMEM)] * 7,
        out_specs=pl.BlockSpec(memory_space=pltpu.VMEM),
        compiler_params=pltpu.CompilerParams(vmem_limit_bytes=SMALL_VMEM),
        name="fresh_columns",
    )(half, outer, sibling, remote, *moments)


def subtract_kernel(where, outer_q, outer_k, outer_v, own, remote, pair, *outs):
    outers = (outer_q, outer_k, outer_v)
    width = own.shape[1]
    deltas = (own, pair.at[:, pl.ds(0, width)], remote, pair.at[:, pl.ds(width, width)])
    for distance, delta in enumerate(deltas):
        block = lax.bitwise_xor(where[0], distance)
        start = 0
        for outer, out in zip(outers, outs):
            width = outer.shape[1] // len(deltas)
            columns = pl.ds(pl.multiple_of(block * width, width), width)
            out[:, columns] = outer[:, columns] - delta[:, start : start + width].astype(jnp.float32)
            start += width


def subtract(where, outers, own, remote, pair):
    return pl.pallas_call(
        subtract_kernel,
        out_shape=[jax.ShapeDtypeStruct(o.shape, o.dtype) for o in outers],
        in_specs=[pl.BlockSpec(memory_space=pltpu.SMEM)] + [pl.BlockSpec(memory_space=pltpu.VMEM)] * 6,
        out_specs=[pl.BlockSpec(memory_space=pltpu.VMEM)] * len(outers),
        compiler_params=pltpu.CompilerParams(vmem_limit_bytes=SMALL_VMEM),
        name="outer_minus_delta",
    )(where, *outers, own, remote, pair)


def place_kernel(count, pieces, where, *refs):
    sources, out, sems = refs[:count], refs[-2], refs[-1]
    copies = []
    for distance, source in enumerate(sources):
        block = lax.bitwise_xor(where[0], distance)
        left = 0
        for start, stride, width in pieces:
            at = pl.multiple_of(start + block * stride, 128)
            copies.append((source.at[:, pl.ds(left, width)], out.at[:, pl.ds(at, width)]))
            left += width
    fetch([a for a, _ in copies], [b for _, b in copies], sems)


def place(where, sources, pieces, columns, earlier, name):
    held = [] if earlier is None else [earlier]
    return pl.pallas_call(
        functools.partial(place_kernel, len(sources), pieces),
        out_shape=jax.ShapeDtypeStruct((sources[0].shape[0], columns), jnp.bfloat16),
        in_specs=[pl.BlockSpec(memory_space=pltpu.SMEM)]
        + [pl.BlockSpec(memory_space=pltpu.VMEM)] * len(sources)
        + [pl.BlockSpec(memory_space=pl.ANY)] * len(held),
        out_specs=pl.BlockSpec(memory_space=pl.ANY),
        scratch_shapes=[pltpu.SemaphoreType.DMA((len(sources) * len(pieces),))],
        input_output_aliases={1 + len(sources): 0} if held else {},
        compiler_params=pltpu.CompilerParams(vmem_limit_bytes=SMALL_VMEM),
        name=name,
    )(where, *sources, *held)


def per_device(
    tokens, inner_q, inner_k, inner_v, outer_q, outer_k, outer_v, moment_q, moment_k, value_momentum
):
    count = lax.axis_size("replica")
    n = lax.axis_size("fsdp")
    me = lax.axis_index("replica")
    row = lax.axis_index("fsdp")
    inners = (inner_q[0], inner_k[0], inner_v[0])
    outers = (outer_q, outer_k, outer_v)
    moments = (moment_q, moment_k, value_momentum)
    widths = [m.shape[1] for m in moments]
    rows = outer_q.shape[0]
    mine = tokens.shape[0]
    total_width = sum(widths)
    cut = total_width // 2
    streams = (cut, total_width - cut)
    LAG, LEAD = 0, 1

    where = me.astype(jnp.int32).reshape(1)
    block = jax.ShapeDtypeStruct((rows, total_width), jnp.float32)
    buffers = [pltpu.VMEM((rows, w), a.dtype) for a, w in zip((*inners, *outers), widths * 2)]

    def half(distance, name, where):
        kernel = functools.partial(half_kernel, distance)
        return columns_call(kernel, name, where, (*inners, *outers), [block] * 2, buffers)

    far_pack, near_pack = pack(where, inners, widths, (3, 1), "pack_inner")
    far_sibling = from_replica(far_pack, 1)
    near_sibling = from_replica(near_pack, 1)
    far_half, far_outer = half(2, "far_half", where)
    far = far_half + (far_outer - far_sibling.astype(jnp.float32))
    fars = [far[:, :cut].astype(jnp.bfloat16), far[:, cut:].astype(jnp.bfloat16)]
    remotes = [from_replica(f, 2) for f in fars]
    near_half, own_outer = half(0, "near_half", after(where, fars[LEAD]))

    tokens_1 = from_replica(after(tokens, fars[LEAD]), 1)
    near_tokens = jnp.concatenate([tokens, tokens_1], axis=0)
    parts = (near_half, own_outer, near_sibling)
    fresh = [
        fresh_columns(*parts, after(remotes[LAG], near_tokens), moments, 0, count),
        fresh_columns(*parts, remotes[LEAD], moments, cut, count),
    ]
    tokens_2 = from_replica(after(tokens, remotes[LEAD]), 2)

    def whole_step(*others):
        remote = jnp.concatenate([after(remotes[0], *others), remotes[1]], axis=1)
        return own_step(*parts, remote, moments, count)

    up = [(ring_member(p, n), ring_member((p + 1) % n, n)) for p in range(n)]
    down = [(b, a) for a, b in up]
    last = n // 2

    def product(lhs, steps, block):
        lanes = lax.dynamic_slice_in_dim(lhs, source_of(row, steps, n) * rows, rows, 1)
        return jnp.dot(lanes, block, preferred_element_type=jnp.float32)

    if n % 2 or not SHORTEST_RING <= n <= LONGEST_RING:
        gathered = [lax.all_gather(part, "fsdp", axis=0, tiled=True) for part in fresh]
        tokens_3 = from_replica(tokens_2, 1)
        far_tokens = jnp.concatenate([tokens_2, tokens_3], axis=0)
        delta, *new_moments = whole_step()
        delta_2 = from_replica(delta, 2)
        near_totals = [jnp.dot(near_tokens, g, preferred_element_type=jnp.float32) for g in gathered]
        far_totals = [jnp.dot(far_tokens, g, preferred_element_type=jnp.float32) for g in gathered]
    else:
        heads = [[part, part] for part in fresh]
        arrived = [[(0, part)] for part in fresh]
        near_totals = [product(near_tokens, 0, part) for part in fresh]
        far_totals = [None, None]

        def hop(stream, way, step, *others):
            heads[stream][way] = lax.ppermute(after(heads[stream][way], *others), "fsdp", (up, down)[way])
            arrived[stream].append((step if way == 0 else -step, heads[stream][way]))

        def add_near(stream, blocks):
            for block in blocks:
                near_totals[stream] += product(near_tokens, *block)

        def add_far(stream, blocks, *others):
            for steps, block in blocks:
                value = product(far_tokens, steps, after(block, *others) if others else block)
                far_totals[stream] = value if far_totals[stream] is None else far_totals[stream] + value

        def hold(stream, first, *others):
            arrived[stream][first:] = [(steps, after(block, *others)) for steps, block in arrived[stream][first:]]

        hop(LEAD, 0, 1)
        hop(LEAD, 1, 1)
        heads[LAG] = [after(block, *heads[LEAD]) for block in heads[LAG]]
        hop(LAG, 0, 1, near_totals[LAG])
        hop(LAG, 1, 1, near_totals[LAG])
        add_near(LEAD, arrived[LEAD][-2:])
        add_near(LAG, arrived[LAG][-2:])
        delta, *new_moments = whole_step(near_totals[LEAD])
        for step in range(2, last):
            for stream in (LEAD, LAG):
                hop(stream, 0, step, near_totals[stream])
                hop(stream, 1, step, near_totals[stream])
            if step < last - 1:
                add_near(LEAD, arrived[LEAD][-2:])
                add_near(LAG, arrived[LAG][-2:])
            if step == 2:
                tokens_2 = after(tokens_2, heads[LAG][0])
                tokens_3 = from_replica(tokens_2, 1)
                far_tokens = jnp.concatenate([tokens_2, tokens_3], axis=0)
                delta_2 = from_replica(after(delta, tokens_2), 2)
        add_near(LEAD, arrived[LEAD][-2:])
        hop(LEAD, 0, last, near_totals[LEAD])
        add_far(LEAD, arrived[LEAD][:-1])
        hold(LAG, -2, far_totals[LEAD])
        add_near(LAG, arrived[LAG][-2:])
        hop(LAG, 1, last, near_totals[LAG])
        hold(LEAD, -1, near_totals[LAG])
        add_near(LEAD, arrived[LEAD][-1:])
        add_far(LEAD, arrived[LEAD][-1:])
        hold(LAG, -1, near_totals[LEAD], delta_2)
        add_near(LAG, arrived[LAG][-1:])
        add_far(LAG, arrived[LAG], near_totals[LAG])

    held = [after(d, near_totals[LAG]) for d in (delta, delta_2)]
    pair = from_replica(jnp.concatenate(held, axis=1), 1)
    new_outers = subtract(where, outers, delta, delta_2, pair)

    base_k, base_v = count * widths[0], count * (widths[0] + widths[1])
    pieces = (
        ((0, widths[0], cut),),
        ((cut, widths[0], widths[0] - cut), (base_k, widths[1], widths[1]), (base_v, widths[2], widths[2])),
    )
    projected = None
    for stream, name in ((LEAD, "place_leading"), (LAG, "place_second")):
        near_out = near_totals[stream].astype(jnp.bfloat16)
        far_out = far_totals[stream].astype(jnp.bfloat16)
        sources = [
            near_out[:mine],
            from_replica(near_out[mine:], 1),
            from_replica(far_out[:mine], 2),
            from_replica(far_out[mine:], 3),
        ]
        if projected is not None:
            projected = after(projected, *new_outers)
        projected = place(where, sources, pieces[stream], count * total_width, projected, name)
    return projected, *new_outers, *new_moments


def solution(mesh):
    placed = (
        P(("replica", "fsdp"), None),
        P("replica", "fsdp", None),
        P("replica", "fsdp", None),
        P("replica", "fsdp", None),
        P("fsdp", None),
        P("fsdp", None),
        P("fsdp", None),
        P("fsdp", "replica"),
        P("fsdp", "replica"),
        P("fsdp", "replica"),
    )
    return jax.shard_map(
        per_device,
        mesh=mesh,
        in_specs=placed,
        out_specs=(
            P(("replica", "fsdp"), None),
            P("fsdp", None),
            P("fsdp", None),
            P("fsdp", None),
            P("fsdp", "replica"),
            P("fsdp", "replica"),
            P("fsdp", "replica"),
        ),
        check_vma=False,
    )
```

time: 321 us -> 76.1 us (0.24)
  waiting for transfers between devices: 262 us -> 25.3 us
  starting transfers between devices: 0.21 us -> 28.2 us
  other arithmetic: 14 us -> 0.21 us
  blocking collectives: 13.5 us -> 0 us
  between operations: 13.9 us -> 1.27 us
  Pallas kernels: 0 us -> 9.47 us
  local copies, waits for them, and re-layouts: 8.31 us -> 1.58 us
    all_gather x2 -> x0, waiting for transfers between devices: 192 us -> none  [the longest x1 177 us: per_device(): fresh = lax.all_gather(local_fresh, 'fsdp', axis=0, tiled=True)]
    reduce_scatter x3 -> x0, waiting for transfers between devices: 69.5 us -> none  [per_device(): lax.psum_scatter(differences, 'replica', scatter_dimension=1, tiled=True)]
    ppermute x0 -> x29, starting transfers between devices: none -> 28.2 us  [the longest x14 16.1 us: hop(): lax.ppermute(after(heads[stream][way], *others), 'fsdp', (up, down)[way])]
    ppermute x0 -> x29, waiting for transfers between devices: none -> 25.3 us  [the longest x14 12.9 us: hop(): lax.ppermute(after(heads[stream][way], *others), 'fsdp', (up, down)[way])]
    all_gather x2 -> x0, blocking collectives: 13.5 us -> none  [per_device(): lax.all_gather(tuple(owned_outer), 'replica', axis=1, tiled=True)]
    sub x6 -> x0, other arithmetic: 10.9 us -> none  [the longest x3 5.53 us: per_device(): own_slice - LEARN_RATE * (pseudo + MOMENTUM_BETA * new_moment)]
    pallas_call x0 -> x9, Pallas kernels: none -> 9.47 us  [the longest x3 4.15 us: columns_call(): pl.pallas_call(kernel, out_shape=shapes, in_specs=[pl.BlockSpec(memory_sp...]
    unnamed x30 -> x16, local copies, waits for them, and re-layouts: 8.31 us -> 1.23 us
  transfers between devices with their start and end apart: 5 -> 29, of which waited for: 5 -> 14; matrix products, arithmetic and copies ran while one was open for 2% -> 14% of each run, Pallas kernels for 0% -> 10%
where the time goes in v2:
time: 76.1 us; the launch traced here: 75.9 us
  starting transfers between devices  28.2 us (37%)
  waiting for transfers between devices  25.3 us (33%)
  matrix products  9.88 us (13%)
  Pallas kernels  9.47 us (12%)
  local copies, waits for them, and re-layouts  1.58 us (2%)
  between operations  1.27 us (2%)
    ppermute x14, starting transfers between devices, hop(): lax.ppermute(after(heads[stream][way], *others), 'fsdp', (up, down)[way])  16.1 us
    ppermute x14, waiting for transfers between devices, hop(): lax.ppermute(after(heads[stream][way], *others), 'fsdp', (up, down)[way])  12.9 us
    ppermute x15, waiting for transfers between devices, from_replica(): return lax.ppermute(x, 'replica', [(i, i ^ distance) for i in range(count)])  12.3 us
    ppermute x15, starting transfers between devices, from_replica(): return lax.ppermute(x, 'replica', [(i, i ^ distance) for i in range(count)])  12.1 us
    dot_general x32, matrix products, product(): return jnp.dot(lanes, block, preferred_element_type=jnp.float32)  9.88 us
    pallas_call x3, Pallas kernels, columns_call(): pl.pallas_call(kernel, out_shape=shapes, in_specs=[pl.BlockSpec(memory_sp...  4.15 us
    pallas_call x1, Pallas kernels, subtract(): pl.pallas_call(subtract_kernel, out_shape=[jax.ShapeDtypeStruct(o.shape,...  2.03 us
    pallas_call x2, Pallas kernels, place(): pl.pallas_call(functools.partial(place_kernel, len(sources), pieces), out...  1.87 us
  transfers between devices with their start and end apart: 29, of which 14 were waited for; matrix products, arithmetic and copies ran while one was open for 14% of the time, Pallas kernels for 10%

profile of v2, /device:TPU:0, one launch (start us, length us, event | category | flops | bytes accessed | tf_op | source)
XLA Modules:
  0.0 75.9 jit_solution(2755420058045758134)
XLA Ops:
  0.6 1.2 %pack_inner.1 = (bf16[256,768]{1,0:T(8,128)(2,1)S(1)}, bf16[256,768]{1,0:T(8,128)(2,1)S(1)}) custom-call(s32[1]{0:T(128)} %bitcast.where, bf16[256,2048]{1,0:T(8,128)(2,1)} %bitcast.36, bf16[256,512]{1,0:T(8,128)(2,1)} %bitcast.39, bf16[256,512]{1,0:T(8,128)(2,1)} %bitcast.42), custom_call_target="tpu_custom_call" | custom-call | tf_op jit(solution)/shard_map/pack_inner/pallas_call | solution.py:67
  1.8 0.5 collective-permute-start
  2.3 1.5 %far_half.1 = (f32[256,768]{1,0:T(8,128)S(1)}, f32[256,768]{1,0:T(8,128)S(1)}) custom-call(s32[1]{0:T(128)} %bitcast.where, bf16[256,2048]{1,0:T(8,128)(2,1)} %bitcast.37, bf16[256,512]{1,0:T(8,128)(2,1)} %bitcast.40, bf16[256,512]{1,0:T(8,128)(2,1)} %bitcast.43, f32[256,2048]{1,0:T(8,128)} %outer_q.1, f32[256,512]{1,0:T(8,128)} %outer_k.1, f32[256,512]{1,0:T(8,128)} %outer_v.1), custom_call_target="tpu_custom_call" | custom-call | tf_op jit(solution)/shard_map/far_half/pallas_call | solution.py:67
  4.0 1.0 %copy-done.6 = bf16[256,2048]{1,0:T(8,128)(2,1)S(1)} copy-done((bf16[256,2048]{1,0:T(8,128)(2,1)S(1)}, bf16[256,2048]{1,0:T(8,128)(2,1)}, u32[]{:S(2)}) %copy-start.6) | copy-done | bytes 1048600
  5.1 0.5 collective-permute-start.2
  5.5 2.5 %collective-permute-start.4 = (bf16[256,384]{1,0:T(8,128)(2,1)S(1)}, bf16[256,384]{1,0:T(8,128)(2,1)S(1)}, u32[]{:S(2)}, u32[]{:S(2)}) collective-permute-start(bf16[256,384]{1,0:T(8,128)(2,1)S(1)} %get-tuple-element.110), channel_id=1, source_target_pairs={{0,16},{8,24},{16,0},{24,8},{1,17},{9,25},{17,1},{25,9},{2,18},{10... | collective-permute-start | bytes 589832 | tf_op jit(solution)/shard_map/ppermute | solution.py:19
  8.2 1.5 %near_half.1 = (f32[256,768]{1,0:T(8,128)S(1)}, f32[256,768]{1,0:T(8,128)S(1)}) custom-call(s32[1]{0:T(128)} %bitcast.where, bf16[256,2048]{1,0:T(8,128)(2,1)} %bitcast.38, bf16[256,512]{1,0:T(8,128)(2,1)} %bitcast.41, bf16[256,512]{1,0:T(8,128)(2,1)} %bitcast.44, f32[256,2048]{1,0:T(8,128)} %outer_q.1, f32[256,512]{1,0:T(8,128)} %outer_k.1, f32[256,512]{1,0:T(8,128)} %outer_v.1), custom_call_target="tpu_custom_call" | custom-call | tf_op jit(solution)/shard_map/near_half/pallas_call | solution.py:67
  9.8 4.0 %collective-permute-done.4.remote = bf16[256,384]{1,0:T(8,128)(2,1)S(1)} collective-permute-done((bf16[256,384]{1,0:T(8,128)(2,1)S(1)}, bf16[256,384]{1,0:T(8,128)(2,1)S(1)}, u32[]{:S(2)}, u32[]{:S(2)}) %collective-permute-start.4) | collective-permute-done | bytes 196640 | tf_op jit(solution)/shard_map/ppermute | solution.py:19
  14.0 2.0 %collective-permute-start.6 = (bf16[256,384]{1,0:T(8,128)(2,1)S(1)}, bf16[256,384]{1,0:T(8,128)(2,1)S(1)}, u32[]{:S(2)}, u32[]{:S(2)}) collective-permute-start(bf16[256,384]{1,0:T(8,128)(2,1)S(1)} %fresh_columns.3), channel_id=1, source_target_pairs={{2,0},{4,2},{6,4},{7,6},{5,7},{3,5},{1,3},{0,1},{10,8},{12,10},{14... | collective-permute-start | bytes 589832 | tf_op jit(solution)/shard_map/ppermute | solution.py:286
  16.1 1.9 %collective-permute-start.12 = (bf16[256,2048]{1,0:T(8,128)(2,1)S(1)}, bf16[256,2048]{1,0:T(8,128)(2,1)S(1)}, u32[]{:S(2)}, u32[]{:S(2)}) collective-permute-start(bf16[256,2048]{1,0:T(8,128)(2,1)S(1)} %copy-done.6), channel_id=1, source_target_pairs={{0,16},{8,24},{16,0},{24,8},{1,17},{9,25},{17,1},{25,9},{2,18},{10... | collective-permute-start | bytes 3145736 | tf_op jit(solution)/shard_map/ppermute | solution.py:19
  18.3 2.3 %collective-permute-done.6 = bf16[256,384]{1,0:T(8,128)(2,1)S(1)} collective-permute-done((bf16[256,384]{1,0:T(8,128)(2,1)S(1)}, bf16[256,384]{1,0:T(8,128)(2,1)S(1)}, u32[]{:S(2)}, u32[]{:S(2)}) %collective-permute-start.6) | collective-permute-done | bytes 196640 | tf_op jit(solution)/shard_map/ppermute | solution.py:286
  20.5 1.3 %collective-permute-done.5 = bf16[256,384]{1,0:T(8,128)(2,1)S(1)} collective-permute-done((bf16[256,384]{1,0:T(8,128)(2,1)S(1)}, bf16[256,384]{1,0:T(8,128)(2,1)S(1)}, u32[]{:S(2)}, u32[]{:S(2)}) %collective-permute-start.5) | collective-permute-done | bytes 196640 | tf_op jit(solution)/shard_map/ppermute | solution.py:286
  22.1 1.6 %collective-permute-start.8 = (bf16[256,384]{1,0:T(8,128)(2,1)S(1)}, bf16[256,384]{1,0:T(8,128)(2,1)S(1)}, u32[]{:S(2)}, u32[]{:S(2)}) collective-permute-start(bf16[256,384]{1,0:T(8,128)(2,1)S(1)} %fresh_columns.2), channel_id=1, source_target_pairs={{2,0},{4,2},{6,4},{7,6},{5,7},{3,5},{1,3},{0,1},{10,8},{12,10},{14... | collective-permute-start | bytes 589832 | tf_op jit(solution)/shard_map/ppermute | solution.py:286
  23.8 0.4 collective-permute-start.7
  25.1 0.5 collective-permute-start.14
  25.6 1.6 %collective-permute-start.15 = (bf16[256,384]{1,0:T(8,128)(2,1)S(1)}, bf16[256,384]{1,0:T(8,128)(2,1)S(1)}, u32[]{:S(2)}, u32[]{:S(2)}) collective-permute-start(bf16[256,384]{1,0:T(8,128)(2,1)S(1)} %collective-permute-done.6), channel_id=1, source_target_pairs={{2,0},{4,2},{6,4},{7,6},{5,7},{3,5},{1,3},{0,1},{10,8},{12,10},{14... | collective-permute-start | bytes 589832 | tf_op jit(solution)/shard_map/ppermute | solution.py:286
  27.2 1.1 %own_step.1 = (bf16[256,768]{1,0:T(8,128)(2,1)S(1)}, f32[256,512]{1,0:T(8,128)}, f32[256,128]{1,0:T(8,128)}, f32[256,128]{1,0:T(8,128)}) custom-call(f32[256,768]{1,0:T(8,128)S(1)} %get-tuple-element.59.half, f32[256,768]{1,0:T(8,128)S(1)} %get-tuple-element.60.outer, bf16[256,768]{1,0:T(8,128)(2,1)S(1)} %collective-permute-done.2.sibling, ...), custom_call_target="tpu_custom_call" | custom-call | tf_op jit(solution)/shard_map/own_step/pallas_call | solution.py:126
  28.3 1.6 %collective-permute-done.8 = bf16[256,384]{1,0:T(8,128)(2,1)S(1)} collective-permute-done((bf16[256,384]{1,0:T(8,128)(2,1)S(1)}, bf16[256,384]{1,0:T(8,128)(2,1)S(1)}, u32[]{:S(2)}, u32[]{:S(2)}) %collective-permute-start.8) | collective-permute-done | bytes 196640 | tf_op jit(solution)/shard_map/ppermute | solution.py:286
  30.2 1.3 %collective-permute-done.7 = bf16[256,384]{1,0:T(8,128)(2,1)S(1)} collective-permute-done((bf16[256,384]{1,0:T(8,128)(2,1)S(1)}, bf16[256,384]{1,0:T(8,128)(2,1)S(1)}, u32[]{:S(2)}, u32[]{:S(2)}) %collective-permute-start.7) | collective-permute-done | bytes 196640 | tf_op jit(solution)/shard_map/ppermute | solution.py:286
  31.5 0.3 fusion.16
  31.9 0.5 collective-permute-start.9
  32.4 1.6 %collective-permute-start.10 = (bf16[256,384]{1,0:T(8,128)(2,1)S(1)}, bf16[256,384]{1,0:T(8,128)(2,1)S(1)}, u32[]{:S(2)}, u32[]{:S(2)}) collective-permute-start(bf16[256,384]{1,0:T(8,128)(2,1)S(1)} %collective-permute-done.8), channel_id=1, source_target_pairs={{2,0},{4,2},{6,4},{7,6},{5,7},{3,5},{1,3},{0,1},{10,8},{12,10},{14... | collective-permute-start | bytes 589832 | tf_op jit(solution)/shard_map/ppermute | solution.py:286
  34.4 1.3 %collective-permute-done.14 = bf16[256,384]{1,0:T(8,128)(2,1)S(1)} collective-permute-done((bf16[256,384]{1,0:T(8,128)(2,1)S(1)}, bf16[256,384]{1,0:T(8,128)(2,1)S(1)}, u32[]{:S(2)}, u32[]{:S(2)}) %collective-permute-start.14) | collective-permute-done | bytes 196640 | tf_op jit(solution)/shard_map/ppermute | solution.py:286
  36.1 0.5 collective-permute-start.16
  36.6 1.6 %collective-permute-start.17 = (bf16[256,384]{1,0:T(8,128)(2,1)S(1)}, bf16[256,384]{1,0:T(8,128)(2,1)S(1)}, u32[]{:S(2)}, u32[]{:S(2)}) collective-permute-start(bf16[256,384]{1,0:T(8,128)(2,1)S(1)} %collective-permute-done.15), channel_id=1, source_target_pairs={{2,0},{4,2},{6,4},{7,6},{5,7},{3,5},{1,3},{0,1},{10,8},{12,10},{14... | collective-permute-start | bytes 589832 | tf_op jit(solution)/shard_map/ppermute | solution.py:286
  38.1 2.1 %collective-permute-done.12 = bf16[256,2048]{1,0:T(8,128)(2,1)S(1)} collective-permute-done((bf16[256,2048]{1,0:T(8,128)(2,1)S(1)}, bf16[256,2048]{1,0:T(8,128)(2,1)S(1)}, u32[]{:S(2)}, u32[]{:S(2)}) %collective-permute-start.12) | collective-permute-done | bytes 1048608 | tf_op jit(solution)/shard_map/ppermute | solution.py:19
  40.6 0.3 fusion.15
  40.9 1.9 %collective-permute-start.11 = (bf16[256,384]{1,0:T(8,128)(2,1)S(1)}, bf16[256,384]{1,0:T(8,128)(2,1)S(1)}, u32[]{:S(2)}, u32[]{:S(2)}) collective-permute-start(bf16[256,384]{1,0:T(8,128)(2,1)S(1)} %collective-permute-done.9), channel_id=1, source_target_pairs={{0,2},{2,4},{4,6},{6,7},{7,5},{5,3},{3,1},{1,0},{8,10},{10,12},{12... | collective-permute-start | bytes 589832 | tf_op jit(solution)/shard_map/ppermute | solution.py:286
  43.0 1.7 %collective-permute-start.21 = (bf16[256,768]{1,0:T(8,128)(2,1)S(1)}, bf16[256,768]{1,0:T(8,128)(2,1)S(1)}, u32[]{:S(2)}, u32[]{:S(2)}) collective-permute-start(bf16[256,768]{1,0:T(8,128)(2,1)S(1)} %get-tuple-element.92.own), channel_id=1, source_target_pairs={{0,16},{8,24},{16,0},{24,8},{1,17},{9,25},{17,1},{25,9},{2,18},{10... | collective-permute-start | bytes 1179656 | tf_op jit(solution)/shard_map/ppermute | solution.py:19
  45.4 1.6 %collective-permute-start.20 = (bf16[256,384]{1,0:T(8,128)(2,1)S(1)}, bf16[256,384]{1,0:T(8,128)(2,1)S(1)}, u32[]{:S(2)}, u32[]{:S(2)}) collective-permute-start(bf16[256,384]{1,0:T(8,128)(2,1)S(1)} %collective-permute-done.16), channel_id=1, source_target_pairs={{0,2},{2,4},{4,6},{6,7},{7,5},{5,3},{3,1},{1,0},{8,10},{10,12},{12... | collective-permute-start | bytes 589832 | tf_op jit(solution)/shard_map/ppermute | solution.py:286
  49.0 0.4 fusion.14
  49.4 0.4 collective-permute-done.18
  50.1 0.3 fusion.7
  50.5 2.0 %collective-permute-done.20 = bf16[256,384]{1,0:T(8,128)(2,1)S(1)} collective-permute-done((bf16[256,384]{1,0:T(8,128)(2,1)S(1)}, bf16[256,384]{1,0:T(8,128)(2,1)S(1)}, u32[]{:S(2)}, u32[]{:S(2)}) %collective-permute-start.20) | collective-permute-done | bytes 196640 | tf_op jit(solution)/shard_map/ppermute | solution.py:286
  52.9 2.0 %collective-permute-start.19 = (bf16[256,384]{1,0:T(8,128)(2,1)S(1)}, bf16[256,384]{1,0:T(8,128)(2,1)S(1)}, u32[]{:S(2)}, u32[]{:S(2)}) collective-permute-start(bf16[256,384]{1,0:T(8,128)(2,1)S(1)} %collective-permute-done.18), channel_id=1, source_target_pairs={{2,0},{4,2},{6,4},{7,6},{5,7},{3,5},{1,3},{0,1},{10,8},{12,10},{14... | collective-permute-start | bytes 589832 | tf_op jit(solution)/shard_map/ppermute | solution.py:286
  54.8 0.5 collective-permute-start.27
  55.4 1.0 %collective-permute-start.26 = (bf16[256,384]{1,0:T(8,128)(2,1)S(1)}, bf16[256,384]{1,0:T(8,128)(2,1)S(1)}, u32[]{:S(2)}, u32[]{:S(2)}) collective-permute-start(bf16[256,384]{1,0:T(8,128)(2,1)S(1)} %get-tuple-element.102), channel_id=1, source_target_pairs={{0,16},{8,24},{16,0},{24,8},{1,17},{9,25},{17,1},{25,9},{2,18},{10... | collective-permute-start | bytes 589832 | tf_op jit(solution)/shard_map/ppermute | solution.py:19
  56.7 0.4 collective-permute-start.25
  57.1 2.4 %collective-permute-done.19 = bf16[256,384]{1,0:T(8,128)(2,1)S(1)} collective-permute-done((bf16[256,384]{1,0:T(8,128)(2,1)S(1)}, bf16[256,384]{1,0:T(8,128)(2,1)S(1)}, u32[]{:S(2)}, u32[]{:S(2)}) %collective-permute-start.19) | collective-permute-done | bytes 196640 | tf_op jit(solution)/shard_map/ppermute | solution.py:286
  62.2 0.6 collective-permute-start.28
  62.7 0.5 fusion.17
  63.3 1.5 %collective-permute-start.24 = (bf16[256,384]{1,0:T(8,128)(2,1)S(1)}, bf16[256,384]{1,0:T(8,128)(2,1)S(1)}, u32[]{:S(2)}, u32[]{:S(2)}) collective-permute-start(bf16[256,384]{1,0:T(8,128)(2,1)S(1)} %get-tuple-element.105), channel_id=1, source_target_pairs={{0,24},{8,16},{16,8},{24,0},{1,25},{9,17},{17,9},{25,1},{2,26},{10... | collective-permute-start | bytes 589832 | tf_op jit(solution)/shard_map/ppermute | solution.py:19
  64.8 1.5 %collective-permute-done.26.refs_2_ = bf16[256,384]{1,0:T(8,128)(2,1)S(1)} collective-permute-done((bf16[256,384]{1,0:T(8,128)(2,1)S(1)}, bf16[256,384]{1,0:T(8,128)(2,1)S(1)}, u32[]{:S(2)}, u32[]{:S(2)}) %collective-permute-start.26) | collective-permute-done | bytes 196640 | tf_op jit(solution)/shard_map/ppermute | solution.py:19
  66.3 0.8 %collective-permute-start.23 = (bf16[256,384]{1,0:T(8,128)(2,1)S(1)}, bf16[256,384]{1,0:T(8,128)(2,1)S(1)}, u32[]{:S(2)}, u32[]{:S(2)}) collective-permute-start(bf16[256,384]{1,0:T(8,128)(2,1)S(1)} %get-tuple-element.106), channel_id=1, source_target_pairs={{0,16},{8,24},{16,0},{24,8},{1,17},{9,25},{17,1},{25,9},{2,18},{10... | collective-permute-start | bytes 589832 | tf_op jit(solution)/shard_map/ppermute | solution.py:19
  67.1 1.0 %place_leading.1.refs_4_ = bf16[256,3072]{1,0:T(8,128)(2,1)} custom-call(s32[1]{0:T(128)} %bitcast.where, bf16[256,384]{1,0:T(8,128)(2,1)S(1)} %get-tuple-element.104.refs_0_, bf16[256,384]{1,0:T(8,128)(2,1)S(1)} %collective-permute-done.25.refs_1_, bf16[256,384]{1,0:T(8,128)(2,1)S(1)} %collective-permute-done.26.refs_2_, ...), custom_call_target="tpu_custom_call" | custom-call | tf_op jit(solution)/shard_map/place_leading/pallas_call | solution.py:201
  68.1 2.0 %outer_minus_delta.1 = (f32[256,2048]{1,0:T(8,128)}, f32[256,512]{1,0:T(8,128)}, f32[256,512]{1,0:T(8,128)}) custom-call(s32[1]{0:T(128)} %bitcast.where, f32[256,2048]{1,0:T(8,128)S(1)} %copy-done, f32[256,512]{1,0:T(8,128)S(1)} %copy-done.1, f32[256,512]{1,0:T(8,128)S(1)} %copy-done.2, bf16[256,768]{1,0:T(8,128)(2,1)S(1)} %get-tuple-element.92.own, ...), custom_call_target="tpu_custom_call" | custom-call | tf_op jit(solution)/shard_map/outer_minus_delta/pallas_call | solution.py:176
  70.3 4.5 %collective-permute-done.23.refs_2_ = bf16[256,384]{1,0:T(8,128)(2,1)S(1)} collective-permute-done((bf16[256,384]{1,0:T(8,128)(2,1)S(1)}, bf16[256,384]{1,0:T(8,128)(2,1)S(1)}, u32[]{:S(2)}, u32[]{:S(2)}) %collective-permute-start.23) | collective-permute-done | bytes 196640 | tf_op jit(solution)/shard_map/ppermute | solution.py:19
  74.8 0.9 %place_second.1 = bf16[256,3072]{1,0:T(8,128)(2,1)} custom-call(s32[1]{0:T(128)} %bitcast.where, bf16[256,384]{1,0:T(8,128)(2,1)S(1)} %get-tuple-element.108.refs_0_, bf16[256,384]{1,0:T(8,128)(2,1)S(1)} %collective-permute-done.22.refs_1_, bf16[256,384]{1,0:T(8,128)(2,1)S(1)} %collective-permute-done.23.refs_2_, ...), custom_call_target="tpu_custom_call", output_to_operand_aliasing={{}: (5, {})} | custom-call | tf_op jit(solution)/shard_map/place_second/pallas_call | solution.py:201
  (77 shorter events, 10.0 us)
Async XLA Ops:
  1.8 2.0 %collective-permute-start = (bf16[256,768]{1,0:T(8,128)(2,1)S(1)}, bf16[256,768]{1,0:T(8,128)(2,1)S(1)}, u32[]{:S(2)}, u32[]{:S(2)}) collective-permute-start(bf16[256,768]{1,0:T(8,128)(2,1)S(1)} %get-tuple-element.56), channel_id=1, source_target_pairs={{0,8},{8,0},{16,24},{24,16},{1,9},{9,1},{17,25},{25,17},{2,10},{10... | collective-permute-start | bytes 1179656 | tf_op jit(solution)/shard_map/ppermute | solution.py:19
  3.8 1.2 %copy-start.6 = (bf16[256,2048]{1,0:T(8,128)(2,1)S(1)}, bf16[256,2048]{1,0:T(8,128)(2,1)}, u32[]{:S(2)}) copy-start(bf16[256,2048]{1,0:T(8,128)(2,1)} %param.10) | copy-start | bytes 3145732
  5.0 13.0 %collective-permute-start.1 = (bf16[256,2048]{1,0:T(8,128)(2,1)S(1)}, bf16[256,2048]{1,0:T(8,128)(2,1)S(1)}, u32[]{:S(2)}, u32[]{:S(2)}) collective-permute-start(bf16[256,2048]{1,0:T(8,128)(2,1)S(1)} %copy-done.6), channel_id=1, source_target_pairs={{0,8},{8,0},{16,24},{24,16},{1,9},{9,1},{17,25},{25,17},{2,10},{10... | collective-permute-start | bytes 3145736 | tf_op jit(solution)/shard_map/ppermute | solution.py:19
  5.1 4.7 %collective-permute-start.2 = (bf16[256,768]{1,0:T(8,128)(2,1)S(1)}, bf16[256,768]{1,0:T(8,128)(2,1)S(1)}, u32[]{:S(2)}, u32[]{:S(2)}) collective-permute-start(bf16[256,768]{1,0:T(8,128)(2,1)S(1)} %get-tuple-element.61), channel_id=1, source_target_pairs={{0,8},{8,0},{16,24},{24,16},{1,9},{9,1},{17,25},{25,17},{2,10},{10... | collective-permute-start | bytes 1179656 | tf_op jit(solution)/shard_map/ppermute | solution.py:19
  5.5 8.3 %collective-permute-start.4 = (bf16[256,384]{1,0:T(8,128)(2,1)S(1)}, bf16[256,384]{1,0:T(8,128)(2,1)S(1)}, u32[]{:S(2)}, u32[]{:S(2)}) collective-permute-start(bf16[256,384]{1,0:T(8,128)(2,1)S(1)} %get-tuple-element.110), channel_id=1, source_target_pairs={{0,16},{8,24},{16,0},{24,8},{1,17},{9,25},{17,1},{25,9},{2,18},{10... | collective-permute-start | bytes 589832 | tf_op jit(solution)/shard_map/ppermute | solution.py:19
  8.1 5.7 %copy-start.3 = (f32[256,512]{1,0:T(8,128)S(1)}, f32[256,512]{1,0:T(8,128)}, u32[]{:S(2)}) copy-start(f32[256,512]{1,0:T(8,128)} %moment_q.5) | copy-start | bytes 1572868
  8.1 5.7 %copy-start.4 = (f32[256,128]{1,0:T(8,128)S(1)}, f32[256,128]{1,0:T(8,128)}, u32[]{:S(2)}) copy-start(f32[256,128]{1,0:T(8,128)} %moment_k.5) | copy-start | bytes 393220
  8.1 5.7 %copy-start.5 = (f32[256,128]{1,0:T(8,128)S(1)}, f32[256,128]{1,0:T(8,128)}, u32[]{:S(2)}) copy-start(f32[256,128]{1,0:T(8,128)} %moment_v.5) | copy-start | bytes 393220
  8.1 9.9 %collective-permute-start.3 = (bf16[256,384]{1,0:T(8,128)(2,1)S(1)}, bf16[256,384]{1,0:T(8,128)(2,1)S(1)}, u32[]{:S(2)}, u32[]{:S(2)}) collective-permute-start(bf16[256,384]{1,0:T(8,128)(2,1)S(1)} %get-tuple-element.109), channel_id=1, source_target_pairs={{0,16},{8,24},{16,0},{24,8},{1,17},{9,25},{17,1},{25,9},{2,18},{10... | collective-permute-start | bytes 589832 | tf_op jit(solution)/shard_map/ppermute | solution.py:19
  14.0 6.6 %collective-permute-start.6 = (bf16[256,384]{1,0:T(8,128)(2,1)S(1)}, bf16[256,384]{1,0:T(8,128)(2,1)S(1)}, u32[]{:S(2)}, u32[]{:S(2)}) collective-permute-start(bf16[256,384]{1,0:T(8,128)(2,1)S(1)} %fresh_columns.3), channel_id=1, source_target_pairs={{2,0},{4,2},{6,4},{7,6},{5,7},{3,5},{1,3},{0,1},{10,8},{12,10},{14... | collective-permute-start | bytes 589832 | tf_op jit(solution)/shard_map/ppermute | solution.py:286
  16.0 5.8 %collective-permute-start.5 = (bf16[256,384]{1,0:T(8,128)(2,1)S(1)}, bf16[256,384]{1,0:T(8,128)(2,1)S(1)}, u32[]{:S(2)}, u32[]{:S(2)}) collective-permute-start(bf16[256,384]{1,0:T(8,128)(2,1)S(1)} %fresh_columns.3), channel_id=1, source_target_pairs={{0,2},{2,4},{4,6},{6,7},{7,5},{5,3},{3,1},{1,0},{8,10},{10,12},{12... | collective-permute-start | bytes 589832 | tf_op jit(solution)/shard_map/ppermute | solution.py:286
  16.1 24.1 %collective-permute-start.12 = (bf16[256,2048]{1,0:T(8,128)(2,1)S(1)}, bf16[256,2048]{1,0:T(8,128)(2,1)S(1)}, u32[]{:S(2)}, u32[]{:S(2)}) collective-permute-start(bf16[256,2048]{1,0:T(8,128)(2,1)S(1)} %copy-done.6), channel_id=1, source_target_pairs={{0,16},{8,24},{16,0},{24,8},{1,17},{9,25},{17,1},{25,9},{2,18},{10... | collective-permute-start | bytes 3145736 | tf_op jit(solution)/shard_map/ppermute | solution.py:19
  22.1 7.8 %collective-permute-start.8 = (bf16[256,384]{1,0:T(8,128)(2,1)S(1)}, bf16[256,384]{1,0:T(8,128)(2,1)S(1)}, u32[]{:S(2)}, u32[]{:S(2)}) collective-permute-start(bf16[256,384]{1,0:T(8,128)(2,1)S(1)} %fresh_columns.2), channel_id=1, source_target_pairs={{2,0},{4,2},{6,4},{7,6},{5,7},{3,5},{1,3},{0,1},{10,8},{12,10},{14... | collective-permute-start | bytes 589832 | tf_op jit(solution)/shard_map/ppermute | solution.py:286
  23.8 7.8 %collective-permute-start.7 = (bf16[256,384]{1,0:T(8,128)(2,1)S(1)}, bf16[256,384]{1,0:T(8,128)(2,1)S(1)}, u32[]{:S(2)}, u32[]{:S(2)}) collective-permute-start(bf16[256,384]{1,0:T(8,128)(2,1)S(1)} %fresh_columns.2), channel_id=1, source_target_pairs={{0,2},{2,4},{4,6},{6,7},{7,5},{5,3},{3,1},{1,0},{8,10},{10,12},{12... | collective-permute-start | bytes 589832 | tf_op jit(solution)/shard_map/ppermute | solution.py:286
  25.1 10.6 %collective-permute-start.14 = (bf16[256,384]{1,0:T(8,128)(2,1)S(1)}, bf16[256,384]{1,0:T(8,128)(2,1)S(1)}, u32[]{:S(2)}, u32[]{:S(2)}) collective-permute-start(bf16[256,384]{1,0:T(8,128)(2,1)S(1)} %collective-permute-done.5), channel_id=1, source_target_pairs={{0,2},{2,4},{4,6},{6,7},{7,5},{5,3},{3,1},{1,0},{8,10},{10,12},{12... | collective-permute-start | bytes 589832 | tf_op jit(solution)/shard_map/ppermute | solution.py:286
  25.6 8.5 %collective-permute-start.15 = (bf16[256,384]{1,0:T(8,128)(2,1)S(1)}, bf16[256,384]{1,0:T(8,128)(2,1)S(1)}, u32[]{:S(2)}, u32[]{:S(2)}) collective-permute-start(bf16[256,384]{1,0:T(8,128)(2,1)S(1)} %collective-permute-done.6), channel_id=1, source_target_pairs={{2,0},{4,2},{6,4},{7,6},{5,7},{3,5},{1,3},{0,1},{10,8},{12,10},{14... | collective-permute-start | bytes 589832 | tf_op jit(solution)/shard_map/ppermute | solution.py:286
  31.9 8.4 %collective-permute-start.9 = (bf16[256,384]{1,0:T(8,128)(2,1)S(1)}, bf16[256,384]{1,0:T(8,128)(2,1)S(1)}, u32[]{:S(2)}, u32[]{:S(2)}) collective-permute-start(bf16[256,384]{1,0:T(8,128)(2,1)S(1)} %collective-permute-done.7), channel_id=1, source_target_pairs={{0,2},{2,4},{4,6},{6,7},{7,5},{5,3},{3,1},{1,0},{8,10},{10,12},{12... | collective-permute-start | bytes 589832 | tf_op jit(solution)/shard_map/ppermute | solution.py:286
  32.4 7.9 %collective-permute-start.10 = (bf16[256,384]{1,0:T(8,128)(2,1)S(1)}, bf16[256,384]{1,0:T(8,128)(2,1)S(1)}, u32[]{:S(2)}, u32[]{:S(2)}) collective-permute-start(bf16[256,384]{1,0:T(8,128)(2,1)S(1)} %collective-permute-done.8), channel_id=1, source_target_pairs={{2,0},{4,2},{6,4},{7,6},{5,7},{3,5},{1,3},{0,1},{10,8},{12,10},{14... | collective-permute-start | bytes 589832 | tf_op jit(solution)/shard_map/ppermute | solution.py:286
  36.1 9.0 %collective-permute-start.16 = (bf16[256,384]{1,0:T(8,128)(2,1)S(1)}, bf16[256,384]{1,0:T(8,128)(2,1)S(1)}, u32[]{:S(2)}, u32[]{:S(2)}) collective-permute-start(bf16[256,384]{1,0:T(8,128)(2,1)S(1)} %collective-permute-done.14), channel_id=1, source_target_pairs={{0,2},{2,4},{4,6},{6,7},{7,5},{5,3},{3,1},{1,0},{8,10},{10,12},{12... | collective-permute-start | bytes 589832 | tf_op jit(solution)/shard_map/ppermute | solution.py:286
  36.6 6.4 %collective-permute-start.17 = (bf16[256,384]{1,0:T(8,128)(2,1)S(1)}, bf16[256,384]{1,0:T(8,128)(2,1)S(1)}, u32[]{:S(2)}, u32[]{:S(2)}) collective-permute-start(bf16[256,384]{1,0:T(8,128)(2,1)S(1)} %collective-permute-done.15), channel_id=1, source_target_pairs={{2,0},{4,2},{6,4},{7,6},{5,7},{3,5},{1,3},{0,1},{10,8},{12,10},{14... | collective-permute-start | bytes 589832 | tf_op jit(solution)/shard_map/ppermute | solution.py:286
  40.3 6.8 %collective-permute-start.13 = (bf16[256,2048]{1,0:T(8,128)(2,1)S(1)}, bf16[256,2048]{1,0:T(8,128)(2,1)S(1)}, u32[]{:S(2)}, u32[]{:S(2)}) collective-permute-start(bf16[256,2048]{1,0:T(8,128)(2,1)S(1)} %collective-permute-done.12), channel_id=1, source_target_pairs={{0,8},{8,0},{16,24},{24,16},{1,9},{9,1},{17,25},{25,17},{2,10},{10... | collective-permute-start | bytes 3145736 | tf_op jit(solution)/shard_map/ppermute | solution.py:19
  40.9 8.9 %collective-permute-start.11 = (bf16[256,384]{1,0:T(8,128)(2,1)S(1)}, bf16[256,384]{1,0:T(8,128)(2,1)S(1)}, u32[]{:S(2)}, u32[]{:S(2)}) collective-permute-start(bf16[256,384]{1,0:T(8,128)(2,1)S(1)} %collective-permute-done.9), channel_id=1, source_target_pairs={{0,2},{2,4},{4,6},{6,7},{7,5},{5,3},{3,1},{1,0},{8,10},{10,12},{12... | collective-permute-start | bytes 589832 | tf_op jit(solution)/shard_map/ppermute | solution.py:286
  42.8 7.0 %collective-permute-start.18 = (bf16[256,384]{1,0:T(8,128)(2,1)S(1)}, bf16[256,384]{1,0:T(8,128)(2,1)S(1)}, u32[]{:S(2)}, u32[]{:S(2)}) collective-permute-start(bf16[256,384]{1,0:T(8,128)(2,1)S(1)} %collective-permute-done.10), channel_id=1, source_target_pairs={{2,0},{4,2},{6,4},{7,6},{5,7},{3,5},{1,3},{0,1},{10,8},{12,10},{14... | collective-permute-start | bytes 589832 | tf_op jit(solution)/shard_map/ppermute | solution.py:286
  43.0 14.1 %collective-permute-start.21 = (bf16[256,768]{1,0:T(8,128)(2,1)S(1)}, bf16[256,768]{1,0:T(8,128)(2,1)S(1)}, u32[]{:S(2)}, u32[]{:S(2)}) collective-permute-start(bf16[256,768]{1,0:T(8,128)(2,1)S(1)} %get-tuple-element.92.own), channel_id=1, source_target_pairs={{0,16},{8,24},{16,0},{24,8},{1,17},{9,25},{17,1},{25,9},{2,18},{10... | collective-permute-start | bytes 1179656 | tf_op jit(solution)/shard_map/ppermute | solution.py:19
  45.4 7.2 %collective-permute-start.20 = (bf16[256,384]{1,0:T(8,128)(2,1)S(1)}, bf16[256,384]{1,0:T(8,128)(2,1)S(1)}, u32[]{:S(2)}, u32[]{:S(2)}) collective-permute-start(bf16[256,384]{1,0:T(8,128)(2,1)S(1)} %collective-permute-done.16), channel_id=1, source_target_pairs={{0,2},{2,4},{4,6},{6,7},{7,5},{5,3},{3,1},{1,0},{8,10},{10,12},{12... | collective-permute-start | bytes 589832 | tf_op jit(solution)/shard_map/ppermute | solution.py:286
  52.9 6.7 %collective-permute-start.19 = (bf16[256,384]{1,0:T(8,128)(2,1)S(1)}, bf16[256,384]{1,0:T(8,128)(2,1)S(1)}, u32[]{:S(2)}, u32[]{:S(2)}) collective-permute-start(bf16[256,384]{1,0:T(8,128)(2,1)S(1)} %collective-permute-done.18), channel_id=1, source_target_pairs={{2,0},{4,2},{6,4},{7,6},{5,7},{3,5},{1,3},{0,1},{10,8},{12,10},{14... | collective-permute-start | bytes 589832 | tf_op jit(solution)/shard_map/ppermute | solution.py:286
  54.8 8.5 %collective-permute-start.27 = (bf16[256,384]{1,0:T(8,128)(2,1)S(1)}, bf16[256,384]{1,0:T(8,128)(2,1)S(1)}, u32[]{:S(2)}, u32[]{:S(2)}) collective-permute-start(bf16[256,384]{1,0:T(8,128)(2,1)S(1)} %get-tuple-element.101), channel_id=1, source_target_pairs={{0,24},{8,16},{16,8},{24,0},{1,25},{9,17},{17,9},{25,1},{2,26},{10... | collective-permute-start | bytes 589832 | tf_op jit(solution)/shard_map/ppermute | solution.py:19
  55.4 10.9 %collective-permute-start.26 = (bf16[256,384]{1,0:T(8,128)(2,1)S(1)}, bf16[256,384]{1,0:T(8,128)(2,1)S(1)}, u32[]{:S(2)}, u32[]{:S(2)}) collective-permute-start(bf16[256,384]{1,0:T(8,128)(2,1)S(1)} %get-tuple-element.102), channel_id=1, source_target_pairs={{0,16},{8,24},{16,0},{24,8},{1,17},{9,25},{17,1},{25,9},{2,18},{10... | collective-permute-start | bytes 589832 | tf_op jit(solution)/shard_map/ppermute | solution.py:19
  56.7 10.4 %collective-permute-start.25 = (bf16[256,384]{1,0:T(8,128)(2,1)S(1)}, bf16[256,384]{1,0:T(8,128)(2,1)S(1)}, u32[]{:S(2)}, u32[]{:S(2)}) collective-permute-start(bf16[256,384]{1,0:T(8,128)(2,1)S(1)} %get-tuple-element.103), channel_id=1, source_target_pairs={{0,8},{8,0},{16,24},{24,16},{1,9},{9,1},{17,25},{25,17},{2,10},{10... | collective-permute-start | bytes 589832 | tf_op jit(solution)/shard_map/ppermute | solution.py:19
  59.9 10.2 %collective-permute-start.22 = (bf16[256,384]{1,0:T(8,128)(2,1)S(1)}, bf16[256,384]{1,0:T(8,128)(2,1)S(1)}, u32[]{:S(2)}, u32[]{:S(2)}) collective-permute-start(bf16[256,384]{1,0:T(8,128)(2,1)S(1)} %get-tuple-element.107), channel_id=1, source_target_pairs={{0,8},{8,0},{16,24},{24,16},{1,9},{9,1},{17,25},{25,17},{2,10},{10... | collective-permute-start | bytes 589832 | tf_op jit(solution)/shard_map/ppermute | solution.py:19
  62.2 5.9 %collective-permute-start.28 = (bf16[256,1536]{1,0:T(8,128)(2,1)S(1)}, bf16[256,1536]{1,0:T(8,128)(2,1)S(1)}, u32[]{:S(2)}, u32[]{:S(2)}) collective-permute-start(bf16[256,1536]{1,0:T(8,128)(2,1)S(1)} %pad_maximum_fusion), channel_id=1, source_target_pairs={{0,8},{8,0},{16,24},{24,16},{1,9},{9,1},{17,25},{25,17},{2,10},{10... | collective-permute-start | bytes 2359304 | tf_op jit(solution)/shard_map/ppermute | solution.py:19
  63.2 4.8 %copy-start = (f32[256,2048]{1,0:T(8,128)S(1)}, f32[256,2048]{1,0:T(8,128)}, u32[]{:S(2)}) copy-start(f32[256,2048]{1,0:T(8,128)} %outer_q.1) | copy-start | bytes 6291460
  63.2 4.8 %copy-start.1 = (f32[256,512]{1,0:T(8,128)S(1)}, f32[256,512]{1,0:T(8,128)}, u32[]{:S(2)}) copy-start(f32[256,512]{1,0:T(8,128)} %outer_k.1) | copy-start | bytes 1572868
  63.2 4.8 %copy-start.2 = (f32[256,512]{1,0:T(8,128)S(1)}, f32[256,512]{1,0:T(8,128)}, u32[]{:S(2)}) copy-start(f32[256,512]{1,0:T(8,128)} %outer_v.1) | copy-start | bytes 1572868
  63.3 6.9 %collective-permute-start.24 = (bf16[256,384]{1,0:T(8,128)(2,1)S(1)}, bf16[256,384]{1,0:T(8,128)(2,1)S(1)}, u32[]{:S(2)}, u32[]{:S(2)}) collective-permute-start(bf16[256,384]{1,0:T(8,128)(2,1)S(1)} %get-tuple-element.105), channel_id=1, source_target_pairs={{0,24},{8,16},{16,8},{24,0},{1,25},{9,17},{17,9},{25,1},{2,26},{10... | collective-permute-start | bytes 589832 | tf_op jit(solution)/shard_map/ppermute | solution.py:19
  66.3 8.5 %collective-permute-start.23 = (bf16[256,384]{1,0:T(8,128)(2,1)S(1)}, bf16[256,384]{1,0:T(8,128)(2,1)S(1)}, u32[]{:S(2)}, u32[]{:S(2)}) collective-permute-start(bf16[256,384]{1,0:T(8,128)(2,1)S(1)} %get-tuple-element.106), channel_id=1, source_target_pairs={{0,16},{8,24},{16,0},{24,8},{1,17},{9,25},{17,1},{25,9},{2,18},{10... | collective-permute-start | bytes 589832 | tf_op jit(solution)/shard_map/ppermute | solution.py:19

commit v3 on v2

--- a/solution.py
+++ b/solution.py
@@ -247,7 +247,7 @@
     remotes = [from_replica(f, 2) for f in fars]
     near_half, own_outer = half(0, "near_half", after(where, fars[LEAD]))
 
-    tokens_1 = from_replica(after(tokens, fars[LEAD]), 1)
+    tokens_1 = from_replica(tokens, 1)
     near_tokens = jnp.concatenate([tokens, tokens_1], axis=0)
     parts = (near_half, own_outer, near_sibling)
     fresh = [
@@ -328,8 +328,9 @@
         add_near(LEAD, arrived[LEAD][-1:])
         add_far(LEAD, arrived[LEAD][-1:])
         hold(LAG, -1, near_totals[LEAD], delta_2)
+        add_far(LAG, arrived[LAG][:-1], near_totals[LEAD], far_totals[LEAD])
         add_near(LAG, arrived[LAG][-1:])
-        add_far(LAG, arrived[LAG], near_totals[LAG])
+        add_far(LAG, arrived[LAG][-1:], near_totals[LAG])
 
     held = [after(d, near_totals[LAG]) for d in (delta, delta_2)]
     pair = from_replica(jnp.concatenate(held, axis=1), 1)

time: 76.1 us -> 75.1 us (0.987)
  local copies, waits for them, and re-layouts: 1.58 us -> 0.62 us
    unnamed x16, local copies, waits for them, and re-layouts: 1.23 us -> 0.24 us
    ppermute x14, waiting for transfers between devices: 12.9 us -> 11.9 us  [hop(): lax.ppermute(after(heads[stream][way], *others), 'fsdp', (up, down)[way])]
  transfers between devices with their start and end apart: 29 -> 29, of which waited for: 14 -> 17; matrix products, arithmetic and copies ran while one was open for 14% -> 14% of each run, Pallas kernels for 10% -> 10%
where the time goes in v3:
time: 75.1 us; the launch traced here: 74.9 us
  starting transfers between devices  28.7 us (38%)
  waiting for transfers between devices  24.8 us (33%)
  matrix products  9.87 us (13%)
  Pallas kernels  9.4 us (13%)
  between operations  1.27 us (2%)
    ppermute x14, starting transfers between devices, hop(): lax.ppermute(after(heads[stream][way], *others), 'fsdp', (up, down)[way])  16.4 us
    ppermute x15, waiting for transfers between devices, from_replica(): return lax.ppermute(x, 'replica', [(i, i ^ distance) for i in range(count)])  12.9 us
    ppermute x15, starting transfers between devices, from_replica(): return lax.ppermute(x, 'replica', [(i, i ^ distance) for i in range(count)])  12.3 us
    ppermute x14, waiting for transfers between devices, hop(): lax.ppermute(after(heads[stream][way], *others), 'fsdp', (up, down)[way])  11.9 us
    dot_general x32, matrix products, product(): return jnp.dot(lanes, block, preferred_element_type=jnp.float32)  9.87 us
    pallas_call x3, Pallas kernels, columns_call(): pl.pallas_call(kernel, out_shape=shapes, in_specs=[pl.BlockSpec(memory_sp...  4.08 us
    pallas_call x1, Pallas kernels, subtract(): pl.pallas_call(subtract_kernel, out_shape=[jax.ShapeDtypeStruct(o.shape,...  2.03 us
    pallas_call x2, Pallas kernels, place(): pl.pallas_call(functools.partial(place_kernel, len(sources), pieces), out...  1.87 us
  transfers between devices with their start and end apart: 29, of which 17 were waited for; matrix products, arithmetic and copies ran while one was open for 14% of the time, Pallas kernels for 10%

profile of v3, /device:TPU:0, one launch (start us, length us, event | category | flops | bytes accessed | tf_op | source)
XLA Modules:
  0.0 74.9 jit_solution(3274691904874847407)
XLA Ops:
  0.6 1.2 %pack_inner.1 = (bf16[256,768]{1,0:T(8,128)(2,1)S(1)}, bf16[256,768]{1,0:T(8,128)(2,1)S(1)}) custom-call(s32[1]{0:T(128)} %bitcast.where, bf16[256,2048]{1,0:T(8,128)(2,1)} %bitcast.36, bf16[256,512]{1,0:T(8,128)(2,1)} %bitcast.39, bf16[256,512]{1,0:T(8,128)(2,1)} %bitcast.42), custom_call_target="tpu_custom_call" | custom-call | tf_op jit(solution)/shard_map/pack_inner/pallas_call | solution.py:67
  1.8 0.5 collective-permute-start.1
  2.4 0.4 collective-permute-start.2
  2.8 1.5 %far_half.1 = (f32[256,768]{1,0:T(8,128)S(1)}, f32[256,768]{1,0:T(8,128)S(1)}) custom-call(s32[1]{0:T(128)} %bitcast.where, bf16[256,2048]{1,0:T(8,128)(2,1)} %bitcast.37, bf16[256,512]{1,0:T(8,128)(2,1)} %bitcast.40, bf16[256,512]{1,0:T(8,128)(2,1)} %bitcast.43, f32[256,2048]{1,0:T(8,128)} %outer_q.1, f32[256,512]{1,0:T(8,128)} %outer_k.1, f32[256,512]{1,0:T(8,128)} %outer_v.1), custom_call_target="tpu_custom_call" | custom-call | tf_op jit(solution)/shard_map/far_half/pallas_call | solution.py:67
  4.5 2.6 %collective-permute-start.4 = (bf16[256,384]{1,0:T(8,128)(2,1)S(1)}, bf16[256,384]{1,0:T(8,128)(2,1)S(1)}, u32[]{:S(2)}, u32[]{:S(2)}) collective-permute-start(bf16[256,384]{1,0:T(8,128)(2,1)S(1)} %get-tuple-element.108), channel_id=1, source_target_pairs={{0,16},{8,24},{16,0},{24,8},{1,17},{9,25},{17,1},{25,9},{2,18},{10... | collective-permute-start | bytes 589832 | tf_op jit(solution)/shard_map/ppermute | solution.py:19
  7.3 1.0 %collective-permute-start.3 = (bf16[256,384]{1,0:T(8,128)(2,1)S(1)}, bf16[256,384]{1,0:T(8,128)(2,1)S(1)}, u32[]{:S(2)}, u32[]{:S(2)}) collective-permute-start(bf16[256,384]{1,0:T(8,128)(2,1)S(1)} %get-tuple-element.107), channel_id=1, source_target_pairs={{0,16},{8,24},{16,0},{24,8},{1,17},{9,25},{17,1},{25,9},{2,18},{10... | collective-permute-start | bytes 589832 | tf_op jit(solution)/shard_map/ppermute | solution.py:19
  8.3 1.5 %near_half.1 = (f32[256,768]{1,0:T(8,128)S(1)}, f32[256,768]{1,0:T(8,128)S(1)}) custom-call(s32[1]{0:T(128)} %bitcast.where, bf16[256,2048]{1,0:T(8,128)(2,1)} %bitcast.38, bf16[256,512]{1,0:T(8,128)(2,1)} %bitcast.41, bf16[256,512]{1,0:T(8,128)(2,1)} %bitcast.44, f32[256,2048]{1,0:T(8,128)} %outer_q.1, f32[256,512]{1,0:T(8,128)} %outer_k.1, f32[256,512]{1,0:T(8,128)} %outer_v.1), custom_call_target="tpu_custom_call" | custom-call | tf_op jit(solution)/shard_map/near_half/pallas_call | solution.py:67
  9.8 3.1 %collective-permute-done.4.remote = bf16[256,384]{1,0:T(8,128)(2,1)S(1)} collective-permute-done((bf16[256,384]{1,0:T(8,128)(2,1)S(1)}, bf16[256,384]{1,0:T(8,128)(2,1)S(1)}, u32[]{:S(2)}, u32[]{:S(2)}) %collective-permute-start.4) | collective-permute-done | bytes 196640 | tf_op jit(solution)/shard_map/ppermute | solution.py:19
  13.1 2.0 %collective-permute-start.6 = (bf16[256,384]{1,0:T(8,128)(2,1)S(1)}, bf16[256,384]{1,0:T(8,128)(2,1)S(1)}, u32[]{:S(2)}, u32[]{:S(2)}) collective-permute-start(bf16[256,384]{1,0:T(8,128)(2,1)S(1)} %fresh_columns.3), channel_id=1, source_target_pairs={{2,0},{4,2},{6,4},{7,6},{5,7},{3,5},{1,3},{0,1},{10,8},{12,10},{14... | collective-permute-start | bytes 589832 | tf_op jit(solution)/shard_map/ppermute | solution.py:286
  15.3 1.9 %collective-permute-start.12 = (bf16[256,2048]{1,0:T(8,128)(2,1)S(1)}, bf16[256,2048]{1,0:T(8,128)(2,1)S(1)}, u32[]{:S(2)}, u32[]{:S(2)}) collective-permute-start(bf16[256,2048]{1,0:T(8,128)(2,1)S(1)} %copy-done.6), channel_id=1, source_target_pairs={{0,16},{8,24},{16,0},{24,8},{1,17},{9,25},{17,1},{25,9},{2,18},{10... | collective-permute-start | bytes 3145736 | tf_op jit(solution)/shard_map/ppermute | solution.py:19
  17.4 2.2 %collective-permute-done.6 = bf16[256,384]{1,0:T(8,128)(2,1)S(1)} collective-permute-done((bf16[256,384]{1,0:T(8,128)(2,1)S(1)}, bf16[256,384]{1,0:T(8,128)(2,1)S(1)}, u32[]{:S(2)}, u32[]{:S(2)}) %collective-permute-start.6) | collective-permute-done | bytes 196640 | tf_op jit(solution)/shard_map/ppermute | solution.py:286
  19.6 1.3 %collective-permute-done.5 = bf16[256,384]{1,0:T(8,128)(2,1)S(1)} collective-permute-done((bf16[256,384]{1,0:T(8,128)(2,1)S(1)}, bf16[256,384]{1,0:T(8,128)(2,1)S(1)}, u32[]{:S(2)}, u32[]{:S(2)}) %collective-permute-start.5) | collective-permute-done | bytes 196640 | tf_op jit(solution)/shard_map/ppermute | solution.py:286
  21.2 1.6 %collective-permute-start.8 = (bf16[256,384]{1,0:T(8,128)(2,1)S(1)}, bf16[256,384]{1,0:T(8,128)(2,1)S(1)}, u32[]{:S(2)}, u32[]{:S(2)}) collective-permute-start(bf16[256,384]{1,0:T(8,128)(2,1)S(1)} %fresh_columns.2), channel_id=1, source_target_pairs={{2,0},{4,2},{6,4},{7,6},{5,7},{3,5},{1,3},{0,1},{10,8},{12,10},{14... | collective-permute-start | bytes 589832 | tf_op jit(solution)/shard_map/ppermute | solution.py:286
  22.8 0.4 collective-permute-start.7
  24.1 0.5 collective-permute-start.14
  24.6 1.6 %collective-permute-start.15 = (bf16[256,384]{1,0:T(8,128)(2,1)S(1)}, bf16[256,384]{1,0:T(8,128)(2,1)S(1)}, u32[]{:S(2)}, u32[]{:S(2)}) collective-permute-start(bf16[256,384]{1,0:T(8,128)(2,1)S(1)} %collective-permute-done.6), channel_id=1, source_target_pairs={{2,0},{4,2},{6,4},{7,6},{5,7},{3,5},{1,3},{0,1},{10,8},{12,10},{14... | collective-permute-start | bytes 589832 | tf_op jit(solution)/shard_map/ppermute | solution.py:286
  26.3 1.1 %own_step.1 = (bf16[256,768]{1,0:T(8,128)(2,1)S(1)}, f32[256,512]{1,0:T(8,128)}, f32[256,128]{1,0:T(8,128)}, f32[256,128]{1,0:T(8,128)}) custom-call(f32[256,768]{1,0:T(8,128)S(1)} %get-tuple-element.57.half, f32[256,768]{1,0:T(8,128)S(1)} %get-tuple-element.58.outer, bf16[256,768]{1,0:T(8,128)(2,1)S(1)} %collective-permute-done.2.sibling, ...), custom_call_target="tpu_custom_call" | custom-call | tf_op jit(solution)/shard_map/own_step/pallas_call | solution.py:126
  27.3 1.7 %collective-permute-done.8 = bf16[256,384]{1,0:T(8,128)(2,1)S(1)} collective-permute-done((bf16[256,384]{1,0:T(8,128)(2,1)S(1)}, bf16[256,384]{1,0:T(8,128)(2,1)S(1)}, u32[]{:S(2)}, u32[]{:S(2)}) %collective-permute-start.8) | collective-permute-done | bytes 196640 | tf_op jit(solution)/shard_map/ppermute | solution.py:286
  29.3 1.2 %collective-permute-done.7 = bf16[256,384]{1,0:T(8,128)(2,1)S(1)} collective-permute-done((bf16[256,384]{1,0:T(8,128)(2,1)S(1)}, bf16[256,384]{1,0:T(8,128)(2,1)S(1)}, u32[]{:S(2)}, u32[]{:S(2)}) %collective-permute-start.7) | collective-permute-done | bytes 196640 | tf_op jit(solution)/shard_map/ppermute | solution.py:286
  30.5 0.3 fusion.16
  30.8 0.5 collective-permute-start.9
  31.3 1.6 %collective-permute-start.10 = (bf16[256,384]{1,0:T(8,128)(2,1)S(1)}, bf16[256,384]{1,0:T(8,128)(2,1)S(1)}, u32[]{:S(2)}, u32[]{:S(2)}) collective-permute-start(bf16[256,384]{1,0:T(8,128)(2,1)S(1)} %collective-permute-done.8), channel_id=1, source_target_pairs={{2,0},{4,2},{6,4},{7,6},{5,7},{3,5},{1,3},{0,1},{10,8},{12,10},{14... | collective-permute-start | bytes 589832 | tf_op jit(solution)/shard_map/ppermute | solution.py:286
  33.5 1.2 %collective-permute-done.14 = bf16[256,384]{1,0:T(8,128)(2,1)S(1)} collective-permute-done((bf16[256,384]{1,0:T(8,128)(2,1)S(1)}, bf16[256,384]{1,0:T(8,128)(2,1)S(1)}, u32[]{:S(2)}, u32[]{:S(2)}) %collective-permute-start.14) | collective-permute-done | bytes 196640 | tf_op jit(solution)/shard_map/ppermute | solution.py:286
  35.0 0.5 collective-permute-start.16
  35.5 1.6 %collective-permute-start.17 = (bf16[256,384]{1,0:T(8,128)(2,1)S(1)}, bf16[256,384]{1,0:T(8,128)(2,1)S(1)}, u32[]{:S(2)}, u32[]{:S(2)}) collective-permute-start(bf16[256,384]{1,0:T(8,128)(2,1)S(1)} %collective-permute-done.15), channel_id=1, source_target_pairs={{2,0},{4,2},{6,4},{7,6},{5,7},{3,5},{1,3},{0,1},{10,8},{12,10},{14... | collective-permute-start | bytes 589832 | tf_op jit(solution)/shard_map/ppermute | solution.py:286
  37.9 1.5 %collective-permute-done.12 = bf16[256,2048]{1,0:T(8,128)(2,1)S(1)} collective-permute-done((bf16[256,2048]{1,0:T(8,128)(2,1)S(1)}, bf16[256,2048]{1,0:T(8,128)(2,1)S(1)}, u32[]{:S(2)}, u32[]{:S(2)}) %collective-permute-start.12) | collective-permute-done | bytes 1048608 | tf_op jit(solution)/shard_map/ppermute | solution.py:19
  39.7 1.9 %collective-permute-start.11 = (bf16[256,384]{1,0:T(8,128)(2,1)S(1)}, bf16[256,384]{1,0:T(8,128)(2,1)S(1)}, u32[]{:S(2)}, u32[]{:S(2)}) collective-permute-start(bf16[256,384]{1,0:T(8,128)(2,1)S(1)} %collective-permute-done.9), channel_id=1, source_target_pairs={{0,2},{2,4},{4,6},{6,7},{7,5},{5,3},{3,1},{1,0},{8,10},{10,12},{12... | collective-permute-start | bytes 589832 | tf_op jit(solution)/shard_map/ppermute | solution.py:286
  42.4 1.9 %collective-permute-start.20 = (bf16[256,384]{1,0:T(8,128)(2,1)S(1)}, bf16[256,384]{1,0:T(8,128)(2,1)S(1)}, u32[]{:S(2)}, u32[]{:S(2)}) collective-permute-start(bf16[256,384]{1,0:T(8,128)(2,1)S(1)} %collective-permute-done.16), channel_id=1, source_target_pairs={{0,2},{2,4},{4,6},{6,7},{7,5},{5,3},{3,1},{1,0},{8,10},{10,12},{12... | collective-permute-start | bytes 589832 | tf_op jit(solution)/shard_map/ppermute | solution.py:286
  44.3 1.5 %collective-permute-start.21 = (bf16[256,768]{1,0:T(8,128)(2,1)S(1)}, bf16[256,768]{1,0:T(8,128)(2,1)S(1)}, u32[]{:S(2)}, u32[]{:S(2)}) collective-permute-start(bf16[256,768]{1,0:T(8,128)(2,1)S(1)} %get-tuple-element.90.own), channel_id=1, source_target_pairs={{0,16},{8,24},{16,0},{24,8},{1,17},{9,25},{17,1},{25,9},{2,18},{10... | collective-permute-start | bytes 1179656 | tf_op jit(solution)/shard_map/ppermute | solution.py:19
  47.8 0.4 fusion.14
  48.2 0.4 collective-permute-done.18
  48.9 0.3 fusion.7
  49.2 2.0 %collective-permute-done.20 = bf16[256,384]{1,0:T(8,128)(2,1)S(1)} collective-permute-done((bf16[256,384]{1,0:T(8,128)(2,1)S(1)}, bf16[256,384]{1,0:T(8,128)(2,1)S(1)}, u32[]{:S(2)}, u32[]{:S(2)}) %collective-permute-start.20) | collective-permute-done | bytes 196640 | tf_op jit(solution)/shard_map/ppermute | solution.py:286
  52.0 2.0 %collective-permute-start.19 = (bf16[256,384]{1,0:T(8,128)(2,1)S(1)}, bf16[256,384]{1,0:T(8,128)(2,1)S(1)}, u32[]{:S(2)}, u32[]{:S(2)}) collective-permute-start(bf16[256,384]{1,0:T(8,128)(2,1)S(1)} %collective-permute-done.18), channel_id=1, source_target_pairs={{2,0},{4,2},{6,4},{7,6},{5,7},{3,5},{1,3},{0,1},{10,8},{12,10},{14... | collective-permute-start | bytes 589832 | tf_op jit(solution)/shard_map/ppermute | solution.py:286
  54.0 0.5 collective-permute-start.27
  54.5 1.0 %collective-permute-start.26 = (bf16[256,384]{1,0:T(8,128)(2,1)S(1)}, bf16[256,384]{1,0:T(8,128)(2,1)S(1)}, u32[]{:S(2)}, u32[]{:S(2)}) collective-permute-start(bf16[256,384]{1,0:T(8,128)(2,1)S(1)} %get-tuple-element.100), channel_id=1, source_target_pairs={{0,16},{8,24},{16,0},{24,8},{1,17},{9,25},{17,1},{25,9},{2,18},{10... | collective-permute-start | bytes 589832 | tf_op jit(solution)/shard_map/ppermute | solution.py:19
  55.5 0.3 collective-permute-start.25
  57.6 1.2 %collective-permute-done.19 = bf16[256,384]{1,0:T(8,128)(2,1)S(1)} collective-permute-done((bf16[256,384]{1,0:T(8,128)(2,1)S(1)}, bf16[256,384]{1,0:T(8,128)(2,1)S(1)}, u32[]{:S(2)}, u32[]{:S(2)}) %collective-permute-start.19) | collective-permute-done | bytes 196640 | tf_op jit(solution)/shard_map/ppermute | solution.py:286
  59.6 0.6 collective-permute-start.28
  60.2 0.5 fusion.17
  60.7 0.4 collective-permute-done.27.refs_3_
  61.1 1.0 %collective-permute-start.24 = (bf16[256,384]{1,0:T(8,128)(2,1)S(1)}, bf16[256,384]{1,0:T(8,128)(2,1)S(1)}, u32[]{:S(2)}, u32[]{:S(2)}) collective-permute-start(bf16[256,384]{1,0:T(8,128)(2,1)S(1)} %get-tuple-element.103), channel_id=1, source_target_pairs={{0,24},{8,16},{16,8},{24,0},{1,25},{9,17},{17,9},{25,1},{2,26},{10... | collective-permute-start | bytes 589832 | tf_op jit(solution)/shard_map/ppermute | solution.py:19
  62.1 3.3 %collective-permute-done.26.refs_2_ = bf16[256,384]{1,0:T(8,128)(2,1)S(1)} collective-permute-done((bf16[256,384]{1,0:T(8,128)(2,1)S(1)}, bf16[256,384]{1,0:T(8,128)(2,1)S(1)}, u32[]{:S(2)}, u32[]{:S(2)}) %collective-permute-start.26) | collective-permute-done | bytes 196640 | tf_op jit(solution)/shard_map/ppermute | solution.py:19
  65.4 0.8 %collective-permute-start.23 = (bf16[256,384]{1,0:T(8,128)(2,1)S(1)}, bf16[256,384]{1,0:T(8,128)(2,1)S(1)}, u32[]{:S(2)}, u32[]{:S(2)}) collective-permute-start(bf16[256,384]{1,0:T(8,128)(2,1)S(1)} %get-tuple-element.104), channel_id=1, source_target_pairs={{0,16},{8,24},{16,0},{24,8},{1,17},{9,25},{17,1},{25,9},{2,18},{10... | collective-permute-start | bytes 589832 | tf_op jit(solution)/shard_map/ppermute | solution.py:19
  66.2 1.0 %place_leading.1.refs_4_ = bf16[256,3072]{1,0:T(8,128)(2,1)} custom-call(s32[1]{0:T(128)} %bitcast.where, bf16[256,384]{1,0:T(8,128)(2,1)S(1)} %get-tuple-element.102.refs_0_, bf16[256,384]{1,0:T(8,128)(2,1)S(1)} %collective-permute-done.25.refs_1_, bf16[256,384]{1,0:T(8,128)(2,1)S(1)} %collective-permute-done.26.refs_2_, ...), custom_call_target="tpu_custom_call" | custom-call | tf_op jit(solution)/shard_map/place_leading/pallas_call | solution.py:201
  67.2 2.0 %outer_minus_delta.1 = (f32[256,2048]{1,0:T(8,128)}, f32[256,512]{1,0:T(8,128)}, f32[256,512]{1,0:T(8,128)}) custom-call(s32[1]{0:T(128)} %bitcast.where, f32[256,2048]{1,0:T(8,128)S(1)} %copy-done, f32[256,512]{1,0:T(8,128)S(1)} %copy-done.1, f32[256,512]{1,0:T(8,128)S(1)} %copy-done.2, bf16[256,768]{1,0:T(8,128)(2,1)S(1)} %get-tuple-element.90.own, ...), custom_call_target="tpu_custom_call" | custom-call | tf_op jit(solution)/shard_map/outer_minus_delta/pallas_call | solution.py:176
  69.5 4.3 %collective-permute-done.23.refs_2_ = bf16[256,384]{1,0:T(8,128)(2,1)S(1)} collective-permute-done((bf16[256,384]{1,0:T(8,128)(2,1)S(1)}, bf16[256,384]{1,0:T(8,128)(2,1)S(1)}, u32[]{:S(2)}, u32[]{:S(2)}) %collective-permute-start.23) | collective-permute-done | bytes 196640 | tf_op jit(solution)/shard_map/ppermute | solution.py:19
  73.8 0.9 %place_second.1 = bf16[256,3072]{1,0:T(8,128)(2,1)} custom-call(s32[1]{0:T(128)} %bitcast.where, bf16[256,384]{1,0:T(8,128)(2,1)S(1)} %get-tuple-element.106.refs_0_, bf16[256,384]{1,0:T(8,128)(2,1)S(1)} %collective-permute-done.22.refs_1_, bf16[256,384]{1,0:T(8,128)(2,1)S(1)} %collective-permute-done.23.refs_2_, ...), custom_call_target="tpu_custom_call", output_to_operand_aliasing={{}: (5, {})} | custom-call | tf_op jit(solution)/shard_map/place_second/pallas_call | solution.py:201
  (77 shorter events, 11.1 us)
Async XLA Ops:
  1.8 2.5 %collective-permute-start.1 = (bf16[256,768]{1,0:T(8,128)(2,1)S(1)}, bf16[256,768]{1,0:T(8,128)(2,1)S(1)}, u32[]{:S(2)}, u32[]{:S(2)}) collective-permute-start(bf16[256,768]{1,0:T(8,128)(2,1)S(1)} %get-tuple-element.55), channel_id=1, source_target_pairs={{0,8},{8,0},{16,24},{24,16},{1,9},{9,1},{17,25},{25,17},{2,10},{10... | collective-permute-start | bytes 1179656 | tf_op jit(solution)/shard_map/ppermute | solution.py:19
  2.3 14.8 %collective-permute-start = (bf16[256,2048]{1,0:T(8,128)(2,1)}, bf16[256,2048]{1,0:T(8,128)(2,1)S(1)}, u32[]{:S(2)}, u32[]{:S(2)}) collective-permute-start(bf16[256,2048]{1,0:T(8,128)(2,1)} %param.10), channel_id=1, source_target_pairs={{0,8},{8,0},{16,24},{24,16},{1,9},{9,1},{17,25},{25,17},{2,10},{10... | collective-permute-start | bytes 3145736 | tf_op jit(solution)/shard_map/ppermute | solution.py:19
  2.4 7.4 %collective-permute-start.2 = (bf16[256,768]{1,0:T(8,128)(2,1)S(1)}, bf16[256,768]{1,0:T(8,128)(2,1)S(1)}, u32[]{:S(2)}, u32[]{:S(2)}) collective-permute-start(bf16[256,768]{1,0:T(8,128)(2,1)S(1)} %get-tuple-element.59), channel_id=1, source_target_pairs={{0,8},{8,0},{16,24},{24,16},{1,9},{9,1},{17,25},{25,17},{2,10},{10... | collective-permute-start | bytes 1179656 | tf_op jit(solution)/shard_map/ppermute | solution.py:19
  4.3 2.9 %copy-start.6 = (bf16[256,2048]{1,0:T(8,128)(2,1)S(1)}, bf16[256,2048]{1,0:T(8,128)(2,1)}, u32[]{:S(2)}) copy-start(bf16[256,2048]{1,0:T(8,128)(2,1)} %param.10) | copy-start | bytes 3145732
  4.5 8.4 %collective-permute-start.4 = (bf16[256,384]{1,0:T(8,128)(2,1)S(1)}, bf16[256,384]{1,0:T(8,128)(2,1)S(1)}, u32[]{:S(2)}, u32[]{:S(2)}) collective-permute-start(bf16[256,384]{1,0:T(8,128)(2,1)S(1)} %get-tuple-element.108), channel_id=1, source_target_pairs={{0,16},{8,24},{16,0},{24,8},{1,17},{9,25},{17,1},{25,9},{2,18},{10... | collective-permute-start | bytes 589832 | tf_op jit(solution)/shard_map/ppermute | solution.py:19
  7.3 5.6 %copy-start.3 = (f32[256,512]{1,0:T(8,128)S(1)}, f32[256,512]{1,0:T(8,128)}, u32[]{:S(2)}) copy-start(f32[256,512]{1,0:T(8,128)} %moment_q.5) | copy-start | bytes 1572868
  7.3 5.6 %copy-start.4 = (f32[256,128]{1,0:T(8,128)S(1)}, f32[256,128]{1,0:T(8,128)}, u32[]{:S(2)}) copy-start(f32[256,128]{1,0:T(8,128)} %moment_k.5) | copy-start | bytes 393220
  7.3 5.6 %copy-start.5 = (f32[256,128]{1,0:T(8,128)S(1)}, f32[256,128]{1,0:T(8,128)}, u32[]{:S(2)}) copy-start(f32[256,128]{1,0:T(8,128)} %moment_v.5) | copy-start | bytes 393220
  7.3 9.9 %collective-permute-start.3 = (bf16[256,384]{1,0:T(8,128)(2,1)S(1)}, bf16[256,384]{1,0:T(8,128)(2,1)S(1)}, u32[]{:S(2)}, u32[]{:S(2)}) collective-permute-start(bf16[256,384]{1,0:T(8,128)(2,1)S(1)} %get-tuple-element.107), channel_id=1, source_target_pairs={{0,16},{8,24},{16,0},{24,8},{1,17},{9,25},{17,1},{25,9},{2,18},{10... | collective-permute-start | bytes 589832 | tf_op jit(solution)/shard_map/ppermute | solution.py:19
  13.1 6.5 %collective-permute-start.6 = (bf16[256,384]{1,0:T(8,128)(2,1)S(1)}, bf16[256,384]{1,0:T(8,128)(2,1)S(1)}, u32[]{:S(2)}, u32[]{:S(2)}) collective-permute-start(bf16[256,384]{1,0:T(8,128)(2,1)S(1)} %fresh_columns.3), channel_id=1, source_target_pairs={{2,0},{4,2},{6,4},{7,6},{5,7},{3,5},{1,3},{0,1},{10,8},{12,10},{14... | collective-permute-start | bytes 589832 | tf_op jit(solution)/shard_map/ppermute | solution.py:286
  15.1 5.7 %collective-permute-start.5 = (bf16[256,384]{1,0:T(8,128)(2,1)S(1)}, bf16[256,384]{1,0:T(8,128)(2,1)S(1)}, u32[]{:S(2)}, u32[]{:S(2)}) collective-permute-start(bf16[256,384]{1,0:T(8,128)(2,1)S(1)} %fresh_columns.3), channel_id=1, source_target_pairs={{0,2},{2,4},{4,6},{6,7},{7,5},{5,3},{3,1},{1,0},{8,10},{10,12},{12... | collective-permute-start | bytes 589832 | tf_op jit(solution)/shard_map/ppermute | solution.py:286
  15.3 24.1 %collective-permute-start.12 = (bf16[256,2048]{1,0:T(8,128)(2,1)S(1)}, bf16[256,2048]{1,0:T(8,128)(2,1)S(1)}, u32[]{:S(2)}, u32[]{:S(2)}) collective-permute-start(bf16[256,2048]{1,0:T(8,128)(2,1)S(1)} %copy-done.6), channel_id=1, source_target_pairs={{0,16},{8,24},{16,0},{24,8},{1,17},{9,25},{17,1},{25,9},{2,18},{10... | collective-permute-start | bytes 3145736 | tf_op jit(solution)/shard_map/ppermute | solution.py:19
  21.2 7.8 %collective-permute-start.8 = (bf16[256,384]{1,0:T(8,128)(2,1)S(1)}, bf16[256,384]{1,0:T(8,128)(2,1)S(1)}, u32[]{:S(2)}, u32[]{:S(2)}) collective-permute-start(bf16[256,384]{1,0:T(8,128)(2,1)S(1)} %fresh_columns.2), channel_id=1, source_target_pairs={{2,0},{4,2},{6,4},{7,6},{5,7},{3,5},{1,3},{0,1},{10,8},{12,10},{14... | collective-permute-start | bytes 589832 | tf_op jit(solution)/shard_map/ppermute | solution.py:286
  22.8 7.7 %collective-permute-start.7 = (bf16[256,384]{1,0:T(8,128)(2,1)S(1)}, bf16[256,384]{1,0:T(8,128)(2,1)S(1)}, u32[]{:S(2)}, u32[]{:S(2)}) collective-permute-start(bf16[256,384]{1,0:T(8,128)(2,1)S(1)} %fresh_columns.2), channel_id=1, source_target_pairs={{0,2},{2,4},{4,6},{6,7},{7,5},{5,3},{3,1},{1,0},{8,10},{10,12},{12... | collective-permute-start | bytes 589832 | tf_op jit(solution)/shard_map/ppermute | solution.py:286
  24.1 10.5 %collective-permute-start.14 = (bf16[256,384]{1,0:T(8,128)(2,1)S(1)}, bf16[256,384]{1,0:T(8,128)(2,1)S(1)}, u32[]{:S(2)}, u32[]{:S(2)}) collective-permute-start(bf16[256,384]{1,0:T(8,128)(2,1)S(1)} %collective-permute-done.5), channel_id=1, source_target_pairs={{0,2},{2,4},{4,6},{6,7},{7,5},{5,3},{3,1},{1,0},{8,10},{10,12},{12... | collective-permute-start | bytes 589832 | tf_op jit(solution)/shard_map/ppermute | solution.py:286
  24.6 8.6 %collective-permute-start.15 = (bf16[256,384]{1,0:T(8,128)(2,1)S(1)}, bf16[256,384]{1,0:T(8,128)(2,1)S(1)}, u32[]{:S(2)}, u32[]{:S(2)}) collective-permute-start(bf16[256,384]{1,0:T(8,128)(2,1)S(1)} %collective-permute-done.6), channel_id=1, source_target_pairs={{2,0},{4,2},{6,4},{7,6},{5,7},{3,5},{1,3},{0,1},{10,8},{12,10},{14... | collective-permute-start | bytes 589832 | tf_op jit(solution)/shard_map/ppermute | solution.py:286
  30.8 7.0 %collective-permute-start.9 = (bf16[256,384]{1,0:T(8,128)(2,1)S(1)}, bf16[256,384]{1,0:T(8,128)(2,1)S(1)}, u32[]{:S(2)}, u32[]{:S(2)}) collective-permute-start(bf16[256,384]{1,0:T(8,128)(2,1)S(1)} %collective-permute-done.7), channel_id=1, source_target_pairs={{0,2},{2,4},{4,6},{6,7},{7,5},{5,3},{3,1},{1,0},{8,10},{10,12},{12... | collective-permute-start | bytes 589832 | tf_op jit(solution)/shard_map/ppermute | solution.py:286
  31.3 6.0 %collective-permute-start.10 = (bf16[256,384]{1,0:T(8,128)(2,1)S(1)}, bf16[256,384]{1,0:T(8,128)(2,1)S(1)}, u32[]{:S(2)}, u32[]{:S(2)}) collective-permute-start(bf16[256,384]{1,0:T(8,128)(2,1)S(1)} %collective-permute-done.8), channel_id=1, source_target_pairs={{2,0},{4,2},{6,4},{7,6},{5,7},{3,5},{1,3},{0,1},{10,8},{12,10},{14... | collective-permute-start | bytes 589832 | tf_op jit(solution)/shard_map/ppermute | solution.py:286
  35.0 7.0 %collective-permute-start.16 = (bf16[256,384]{1,0:T(8,128)(2,1)S(1)}, bf16[256,384]{1,0:T(8,128)(2,1)S(1)}, u32[]{:S(2)}, u32[]{:S(2)}) collective-permute-start(bf16[256,384]{1,0:T(8,128)(2,1)S(1)} %collective-permute-done.14), channel_id=1, source_target_pairs={{0,2},{2,4},{4,6},{6,7},{7,5},{5,3},{3,1},{1,0},{8,10},{10,12},{12... | collective-permute-start | bytes 589832 | tf_op jit(solution)/shard_map/ppermute | solution.py:286
  35.5 6.2 %collective-permute-start.17 = (bf16[256,384]{1,0:T(8,128)(2,1)S(1)}, bf16[256,384]{1,0:T(8,128)(2,1)S(1)}, u32[]{:S(2)}, u32[]{:S(2)}) collective-permute-start(bf16[256,384]{1,0:T(8,128)(2,1)S(1)} %collective-permute-done.15), channel_id=1, source_target_pairs={{2,0},{4,2},{6,4},{7,6},{5,7},{3,5},{1,3},{0,1},{10,8},{12,10},{14... | collective-permute-start | bytes 589832 | tf_op jit(solution)/shard_map/ppermute | solution.py:286
  39.3 6.5 %collective-permute-start.13 = (bf16[256,2048]{1,0:T(8,128)(2,1)S(1)}, bf16[256,2048]{1,0:T(8,128)(2,1)S(1)}, u32[]{:S(2)}, u32[]{:S(2)}) collective-permute-start(bf16[256,2048]{1,0:T(8,128)(2,1)S(1)} %collective-permute-done.12), channel_id=1, source_target_pairs={{0,8},{8,0},{16,24},{24,16},{1,9},{9,1},{17,25},{25,17},{2,10},{10... | collective-permute-start | bytes 3145736 | tf_op jit(solution)/shard_map/ppermute | solution.py:19
  39.7 8.9 %collective-permute-start.11 = (bf16[256,384]{1,0:T(8,128)(2,1)S(1)}, bf16[256,384]{1,0:T(8,128)(2,1)S(1)}, u32[]{:S(2)}, u32[]{:S(2)}) collective-permute-start(bf16[256,384]{1,0:T(8,128)(2,1)S(1)} %collective-permute-done.9), channel_id=1, source_target_pairs={{0,2},{2,4},{4,6},{6,7},{7,5},{5,3},{3,1},{1,0},{8,10},{10,12},{12... | collective-permute-start | bytes 589832 | tf_op jit(solution)/shard_map/ppermute | solution.py:286
  41.6 7.0 %collective-permute-start.18 = (bf16[256,384]{1,0:T(8,128)(2,1)S(1)}, bf16[256,384]{1,0:T(8,128)(2,1)S(1)}, u32[]{:S(2)}, u32[]{:S(2)}) collective-permute-start(bf16[256,384]{1,0:T(8,128)(2,1)S(1)} %collective-permute-done.10), channel_id=1, source_target_pairs={{2,0},{4,2},{6,4},{7,6},{5,7},{3,5},{1,3},{0,1},{10,8},{12,10},{14... | collective-permute-start | bytes 589832 | tf_op jit(solution)/shard_map/ppermute | solution.py:286
  42.4 8.9 %collective-permute-start.20 = (bf16[256,384]{1,0:T(8,128)(2,1)S(1)}, bf16[256,384]{1,0:T(8,128)(2,1)S(1)}, u32[]{:S(2)}, u32[]{:S(2)}) collective-permute-start(bf16[256,384]{1,0:T(8,128)(2,1)S(1)} %collective-permute-done.16), channel_id=1, source_target_pairs={{0,2},{2,4},{4,6},{6,7},{7,5},{5,3},{3,1},{1,0},{8,10},{10,12},{12... | collective-permute-start | bytes 589832 | tf_op jit(solution)/shard_map/ppermute | solution.py:286
  44.3 13.4 %collective-permute-start.21 = (bf16[256,768]{1,0:T(8,128)(2,1)S(1)}, bf16[256,768]{1,0:T(8,128)(2,1)S(1)}, u32[]{:S(2)}, u32[]{:S(2)}) collective-permute-start(bf16[256,768]{1,0:T(8,128)(2,1)S(1)} %get-tuple-element.90.own), channel_id=1, source_target_pairs={{0,16},{8,24},{16,0},{24,8},{1,17},{9,25},{17,1},{25,9},{2,18},{10... | collective-permute-start | bytes 1179656 | tf_op jit(solution)/shard_map/ppermute | solution.py:19
  52.0 6.8 %collective-permute-start.19 = (bf16[256,384]{1,0:T(8,128)(2,1)S(1)}, bf16[256,384]{1,0:T(8,128)(2,1)S(1)}, u32[]{:S(2)}, u32[]{:S(2)}) collective-permute-start(bf16[256,384]{1,0:T(8,128)(2,1)S(1)} %collective-permute-done.18), channel_id=1, source_target_pairs={{2,0},{4,2},{6,4},{7,6},{5,7},{3,5},{1,3},{0,1},{10,8},{12,10},{14... | collective-permute-start | bytes 589832 | tf_op jit(solution)/shard_map/ppermute | solution.py:286
  54.0 7.2 %collective-permute-start.27 = (bf16[256,384]{1,0:T(8,128)(2,1)S(1)}, bf16[256,384]{1,0:T(8,128)(2,1)S(1)}, u32[]{:S(2)}, u32[]{:S(2)}) collective-permute-start(bf16[256,384]{1,0:T(8,128)(2,1)S(1)} %get-tuple-element.99), channel_id=1, source_target_pairs={{0,24},{8,16},{16,8},{24,0},{1,25},{9,17},{17,9},{25,1},{2,26},{10... | collective-permute-start | bytes 589832 | tf_op jit(solution)/shard_map/ppermute | solution.py:19
  54.5 10.9 %collective-permute-start.26 = (bf16[256,384]{1,0:T(8,128)(2,1)S(1)}, bf16[256,384]{1,0:T(8,128)(2,1)S(1)}, u32[]{:S(2)}, u32[]{:S(2)}) collective-permute-start(bf16[256,384]{1,0:T(8,128)(2,1)S(1)} %get-tuple-element.100), channel_id=1, source_target_pairs={{0,16},{8,24},{16,0},{24,8},{1,17},{9,25},{17,1},{25,9},{2,18},{10... | collective-permute-start | bytes 589832 | tf_op jit(solution)/shard_map/ppermute | solution.py:19
  55.5 10.7 %collective-permute-start.25 = (bf16[256,384]{1,0:T(8,128)(2,1)S(1)}, bf16[256,384]{1,0:T(8,128)(2,1)S(1)}, u32[]{:S(2)}, u32[]{:S(2)}) collective-permute-start(bf16[256,384]{1,0:T(8,128)(2,1)S(1)} %get-tuple-element.101), channel_id=1, source_target_pairs={{0,8},{8,0},{16,24},{24,16},{1,9},{9,1},{17,25},{25,17},{2,10},{10... | collective-permute-start | bytes 589832 | tf_op jit(solution)/shard_map/ppermute | solution.py:19
  59.2 10.1 %collective-permute-start.22 = (bf16[256,384]{1,0:T(8,128)(2,1)S(1)}, bf16[256,384]{1,0:T(8,128)(2,1)S(1)}, u32[]{:S(2)}, u32[]{:S(2)}) collective-permute-start(bf16[256,384]{1,0:T(8,128)(2,1)S(1)} %get-tuple-element.105), channel_id=1, source_target_pairs={{0,8},{8,0},{16,24},{24,16},{1,9},{9,1},{17,25},{25,17},{2,10},{10... | collective-permute-start | bytes 589832 | tf_op jit(solution)/shard_map/ppermute | solution.py:19
  59.6 7.6 %collective-permute-start.28 = (bf16[256,1536]{1,0:T(8,128)(2,1)S(1)}, bf16[256,1536]{1,0:T(8,128)(2,1)S(1)}, u32[]{:S(2)}, u32[]{:S(2)}) collective-permute-start(bf16[256,1536]{1,0:T(8,128)(2,1)S(1)} %pad_maximum_fusion), channel_id=1, source_target_pairs={{0,8},{8,0},{16,24},{24,16},{1,9},{9,1},{17,25},{25,17},{2,10},{10... | collective-permute-start | bytes 2359304 | tf_op jit(solution)/shard_map/ppermute | solution.py:19
  60.7 6.5 %copy-start = (f32[256,2048]{1,0:T(8,128)S(1)}, f32[256,2048]{1,0:T(8,128)}, u32[]{:S(2)}) copy-start(f32[256,2048]{1,0:T(8,128)} %outer_q.1) | copy-start | bytes 6291460
  60.7 6.5 %copy-start.1 = (f32[256,512]{1,0:T(8,128)S(1)}, f32[256,512]{1,0:T(8,128)}, u32[]{:S(2)}) copy-start(f32[256,512]{1,0:T(8,128)} %outer_k.1) | copy-start | bytes 1572868
  60.7 6.5 %copy-start.2 = (f32[256,512]{1,0:T(8,128)S(1)}, f32[256,512]{1,0:T(8,128)}, u32[]{:S(2)}) copy-start(f32[256,512]{1,0:T(8,128)} %outer_v.1) | copy-start | bytes 1572868
  61.1 8.4 %collective-permute-start.24 = (bf16[256,384]{1,0:T(8,128)(2,1)S(1)}, bf16[256,384]{1,0:T(8,128)(2,1)S(1)}, u32[]{:S(2)}, u32[]{:S(2)}) collective-permute-start(bf16[256,384]{1,0:T(8,128)(2,1)S(1)} %get-tuple-element.103), channel_id=1, source_target_pairs={{0,24},{8,16},{16,8},{24,0},{1,25},{9,17},{17,9},{25,1},{2,26},{10... | collective-permute-start | bytes 589832 | tf_op jit(solution)/shard_map/ppermute | solution.py:19
  65.4 8.4 %collective-permute-start.23 = (bf16[256,384]{1,0:T(8,128)(2,1)S(1)}, bf16[256,384]{1,0:T(8,128)(2,1)S(1)}, u32[]{:S(2)}, u32[]{:S(2)}) collective-permute-start(bf16[256,384]{1,0:T(8,128)(2,1)S(1)} %get-tuple-element.104), channel_id=1, source_target_pairs={{0,16},{8,24},{16,0},{24,8},{1,17},{9,25},{17,1},{25,9},{2,18},{10... | collective-permute-start | bytes 589832 | tf_op jit(solution)/shard_map/ppermute | solution.py:19

commit v4 on v3

--- a/solution.py
+++ b/solution.py
@@ -264,10 +264,11 @@
     down = [(b, a) for a, b in up]
     last = n // 2
 
-    def product(lhs, steps, block):
-        lanes = lax.dynamic_slice_in_dim(lhs, source_of(row, steps, n) * rows, rows, 1)
+    def product(lhs, steps, first, block):
+        lanes = lax.dynamic_slice_in_dim(lhs, source_of(row, steps, n) * rows + first, block.shape[0], 1)
         return jnp.dot(lanes, block, preferred_element_type=jnp.float32)
 
+    near_outs, from_sibling = [None, None], [None, None]
     if n % 2 or not SHORTEST_RING <= n <= LONGEST_RING:
         gathered = [lax.all_gather(part, "fsdp", axis=0, tiled=True) for part in fresh]
         tokens_3 = from_replica(tokens_2, 1)
@@ -278,25 +279,31 @@
         far_totals = [jnp.dot(far_tokens, g, preferred_element_type=jnp.float32) for g in gathered]
     else:
         heads = [[part, part] for part in fresh]
-        arrived = [[(0, part)] for part in fresh]
-        near_totals = [product(near_tokens, 0, part) for part in fresh]
+        arrived = [[(0, 0, part)] for part in fresh]
+        near_totals = [product(near_tokens, 0, 0, part) for part in fresh]
         far_totals = [None, None]
 
         def hop(stream, way, step, *others):
             heads[stream][way] = lax.ppermute(after(heads[stream][way], *others), "fsdp", (up, down)[way])
-            arrived[stream].append((step if way == 0 else -step, heads[stream][way]))
+            arrived[stream].append((step if way == 0 else -step, 0, heads[stream][way]))
+
+        def last_hop(stream, *others):
+            for way, first, stop in ((0, 0, rows // 2), (1, rows // 2, rows)):
+                part = after(heads[stream][way], *others)[first:stop]
+                block = lax.ppermute(part, "fsdp", (up, down)[way])
+                arrived[stream].append((last if way == 0 else -last, first, block))
 
         def add_near(stream, blocks):
             for block in blocks:
                 near_totals[stream] += product(near_tokens, *block)
 
         def add_far(stream, blocks, *others):
-            for steps, block in blocks:
-                value = product(far_tokens, steps, after(block, *others) if others else block)
+            for steps, top, block in blocks:
+                value = product(far_tokens, steps, top, after(block, *others) if others else block)
                 far_totals[stream] = value if far_totals[stream] is None else far_totals[stream] + value
 
         def hold(stream, first, *others):
-            arrived[stream][first:] = [(steps, after(block, *others)) for steps, block in arrived[stream][first:]]
+            arrived[stream][first:] = [(steps, top, after(b, *others)) for steps, top, b in arrived[stream][first:]]
 
         hop(LEAD, 0, 1)
         hop(LEAD, 1, 1)
@@ -319,18 +326,20 @@
                 far_tokens = jnp.concatenate([tokens_2, tokens_3], axis=0)
                 delta_2 = from_replica(after(delta, tokens_2), 2)
         add_near(LEAD, arrived[LEAD][-2:])
-        hop(LEAD, 0, last, near_totals[LEAD])
-        add_far(LEAD, arrived[LEAD][:-1])
+        last_hop(LEAD, near_totals[LEAD])
+        add_far(LEAD, arrived[LEAD][:-2])
         hold(LAG, -2, far_totals[LEAD])
         add_near(LAG, arrived[LAG][-2:])
-        hop(LAG, 1, last, near_totals[LAG])
-        hold(LEAD, -1, near_totals[LAG])
-        add_near(LEAD, arrived[LEAD][-1:])
-        add_far(LEAD, arrived[LEAD][-1:])
-        hold(LAG, -1, near_totals[LEAD], delta_2)
-        add_far(LAG, arrived[LAG][:-1], near_totals[LEAD], far_totals[LEAD])
-        add_near(LAG, arrived[LAG][-1:])
-        add_far(LAG, arrived[LAG][-1:], near_totals[LAG])
+        hold(LEAD, -2, near_totals[LAG])
+        add_near(LEAD, arrived[LEAD][-2:])
+        add_far(LEAD, arrived[LEAD][-2:])
+        near_outs[LEAD] = near_totals[LEAD].astype(jnp.bfloat16)
+        from_sibling[LEAD] = from_replica(near_outs[LEAD][mine:], 1)
+        last_hop(LAG, near_totals[LAG], from_sibling[LEAD])
+        hold(LAG, -2, near_totals[LEAD], delta_2)
+        add_far(LAG, arrived[LAG][:-2], from_sibling[LEAD], far_totals[LEAD])
+        add_near(LAG, arrived[LAG][-2:])
+        add_far(LAG, arrived[LAG][-2:], near_totals[LAG])
 
     held = [after(d, near_totals[LAG]) for d in (delta, delta_2)]
     pair = from_replica(jnp.concatenate(held, axis=1), 1)
@@ -343,11 +352,13 @@
     )
     projected = None
     for stream, name in ((LEAD, "place_leading"), (LAG, "place_second")):
-        near_out = near_totals[stream].astype(jnp.bfloat16)
+        if near_outs[stream] is None:
+            near_outs[stream] = near_totals[stream].astype(jnp.bfloat16)
+            from_sibling[stream] = from_replica(near_outs[stream][mine:], 1)
         far_out = far_totals[stream].astype(jnp.bfloat16)
         sources = [
-            near_out[:mine],
-            from_replica(near_out[mine:], 1),
+            near_outs[stream][:mine],
+            from_sibling[stream],
             from_replica(far_out[:mine], 2),
             from_replica(far_out[mine:], 3),
         ]

time: 75.1 us -> 74.2 us (0.988)
  waiting for transfers between devices: 24.8 us -> 22 us
  starting transfers between devices: 28.7 us -> 29.7 us
  matrix products: 9.87 us -> 10.7 us
    ppermute x0 -> x4, starting transfers between devices: none -> 4.16 us  [last_hop(): block = lax.ppermute(part, 'fsdp', (up, down)[way])]
    ppermute x14 -> x12, starting transfers between devices: 16.4 us -> 12.5 us  [hop(): lax.ppermute(after(heads[stream][way], *others), 'fsdp', (up, down)[way])]
    ppermute x14 -> x12, waiting for transfers between devices: 11.9 us -> 8.85 us  [hop(): lax.ppermute(after(heads[stream][way], *others), 'fsdp', (up, down)[way])]
    ppermute x0 -> x4, waiting for transfers between devices: none -> 1.85 us  [last_hop(): block = lax.ppermute(part, 'fsdp', (up, down)[way])]
    ppermute x15, waiting for transfers between devices: 12.9 us -> 11.3 us  [from_replica(): return lax.ppermute(x, 'replica', [(i, i ^ distance) for i in range(count)])]
    dot_general x32 -> x36, matrix products: 9.87 us -> 10.7 us  [product(): return jnp.dot(lanes, block, preferred_element_type=jnp.float32)]
  transfers between devices with their start and end apart: 29 -> 31, of which waited for: 17 -> 17; matrix products, arithmetic and copies ran while one was open for 14% -> 16% of each run, Pallas kernels for 10% -> 10%
where the time goes in v4:
time: 74.2 us; the launch traced here: 74 us
  starting transfers between devices  29.7 us (40%)
  waiting for transfers between devices  22 us (30%)
  matrix products  10.7 us (14%)
  Pallas kernels  9.4 us (13%)
  between operations  1.35 us (2%)
    ppermute x15, starting transfers between devices, from_replica(): return lax.ppermute(x, 'replica', [(i, i ^ distance) for i in range(count)])  13 us
    ppermute x12, starting transfers between devices, hop(): lax.ppermute(after(heads[stream][way], *others), 'fsdp', (up, down)[way])  12.5 us
    ppermute x15, waiting for transfers between devices, from_replica(): return lax.ppermute(x, 'replica', [(i, i ^ distance) for i in range(count)])  11.3 us
    dot_general x36, matrix products, product(): return jnp.dot(lanes, block, preferred_element_type=jnp.float32)  10.7 us
    ppermute x12, waiting for transfers between devices, hop(): lax.ppermute(after(heads[stream][way], *others), 'fsdp', (up, down)[way])  8.85 us
    ppermute x4, starting transfers between devices, last_hop(): block = lax.ppermute(part, 'fsdp', (up, down)[way])  4.16 us
    pallas_call x3, Pallas kernels, columns_call(): pl.pallas_call(kernel, out_shape=shapes, in_specs=[pl.BlockSpec(memory_sp...  4.08 us
    pallas_call x1, Pallas kernels, subtract(): pl.pallas_call(subtract_kernel, out_shape=[jax.ShapeDtypeStruct(o.shape,...  2.03 us
  transfers between devices with their start and end apart: 31, of which 17 were waited for; matrix products, arithmetic and copies ran while one was open for 16% of the time, Pallas kernels for 10%

profile of v4, /device:TPU:0, one launch (start us, length us, event | category | flops | bytes accessed | tf_op | source)
XLA Modules:
  0.0 74.0 jit_solution(12648872079822193636)
XLA Ops:
  0.6 1.2 %pack_inner.1 = (bf16[256,768]{1,0:T(8,128)(2,1)S(1)}, bf16[256,768]{1,0:T(8,128)(2,1)S(1)}) custom-call(s32[1]{0:T(128)} %bitcast.where, bf16[256,2048]{1,0:T(8,128)(2,1)} %bitcast.40, bf16[256,512]{1,0:T(8,128)(2,1)} %bitcast.43, bf16[256,512]{1,0:T(8,128)(2,1)} %bitcast.46), custom_call_target="tpu_custom_call" | custom-call | tf_op jit(solution)/shard_map/pack_inner/pallas_call | solution.py:67
  1.8 0.5 collective-permute-start.1
  2.4 0.4 collective-permute-start.2
  2.8 1.5 %far_half.1 = (f32[256,768]{1,0:T(8,128)S(1)}, f32[256,768]{1,0:T(8,128)S(1)}) custom-call(s32[1]{0:T(128)} %bitcast.where, bf16[256,2048]{1,0:T(8,128)(2,1)} %bitcast.41, bf16[256,512]{1,0:T(8,128)(2,1)} %bitcast.44, bf16[256,512]{1,0:T(8,128)(2,1)} %bitcast.47, f32[256,2048]{1,0:T(8,128)} %outer_q.1, f32[256,512]{1,0:T(8,128)} %outer_k.1, f32[256,512]{1,0:T(8,128)} %outer_v.1), custom_call_target="tpu_custom_call" | custom-call | tf_op jit(solution)/shard_map/far_half/pallas_call | solution.py:67
  4.5 2.6 %collective-permute-start.4 = (bf16[256,384]{1,0:T(8,128)(2,1)S(1)}, bf16[256,384]{1,0:T(8,128)(2,1)S(1)}, u32[]{:S(2)}, u32[]{:S(2)}) collective-permute-start(bf16[256,384]{1,0:T(8,128)(2,1)S(1)} %get-tuple-element.118), channel_id=1, source_target_pairs={{0,16},{8,24},{16,0},{24,8},{1,17},{9,25},{17,1},{25,9},{2,18},{10... | collective-permute-start | bytes 589832 | tf_op jit(solution)/shard_map/ppermute | solution.py:19
  7.3 1.0 %collective-permute-start.3 = (bf16[256,384]{1,0:T(8,128)(2,1)S(1)}, bf16[256,384]{1,0:T(8,128)(2,1)S(1)}, u32[]{:S(2)}, u32[]{:S(2)}) collective-permute-start(bf16[256,384]{1,0:T(8,128)(2,1)S(1)} %get-tuple-element.117), channel_id=1, source_target_pairs={{0,16},{8,24},{16,0},{24,8},{1,17},{9,25},{17,1},{25,9},{2,18},{10... | collective-permute-start | bytes 589832 | tf_op jit(solution)/shard_map/ppermute | solution.py:19
  8.3 1.5 %near_half.1 = (f32[256,768]{1,0:T(8,128)S(1)}, f32[256,768]{1,0:T(8,128)S(1)}) custom-call(s32[1]{0:T(128)} %bitcast.where, bf16[256,2048]{1,0:T(8,128)(2,1)} %bitcast.42, bf16[256,512]{1,0:T(8,128)(2,1)} %bitcast.45, bf16[256,512]{1,0:T(8,128)(2,1)} %bitcast.48, f32[256,2048]{1,0:T(8,128)} %outer_q.1, f32[256,512]{1,0:T(8,128)} %outer_k.1, f32[256,512]{1,0:T(8,128)} %outer_v.1), custom_call_target="tpu_custom_call" | custom-call | tf_op jit(solution)/shard_map/near_half/pallas_call | solution.py:67
  9.8 3.1 %collective-permute-done.4.remote = bf16[256,384]{1,0:T(8,128)(2,1)S(1)} collective-permute-done((bf16[256,384]{1,0:T(8,128)(2,1)S(1)}, bf16[256,384]{1,0:T(8,128)(2,1)S(1)}, u32[]{:S(2)}, u32[]{:S(2)}) %collective-permute-start.4) | collective-permute-done | bytes 196640 | tf_op jit(solution)/shard_map/ppermute | solution.py:19
  13.1 2.0 %collective-permute-start.6 = (bf16[256,384]{1,0:T(8,128)(2,1)S(1)}, bf16[256,384]{1,0:T(8,128)(2,1)S(1)}, u32[]{:S(2)}, u32[]{:S(2)}) collective-permute-start(bf16[256,384]{1,0:T(8,128)(2,1)S(1)} %fresh_columns.3), channel_id=1, source_target_pairs={{2,0},{4,2},{6,4},{7,6},{5,7},{3,5},{1,3},{0,1},{10,8},{12,10},{14... | collective-permute-start | bytes 589832 | tf_op jit(solution)/shard_map/ppermute | solution.py:287
  15.3 1.9 %collective-permute-start.12 = (bf16[256,2048]{1,0:T(8,128)(2,1)S(1)}, bf16[256,2048]{1,0:T(8,128)(2,1)S(1)}, u32[]{:S(2)}, u32[]{:S(2)}) collective-permute-start(bf16[256,2048]{1,0:T(8,128)(2,1)S(1)} %copy-done.6), channel_id=1, source_target_pairs={{0,16},{8,24},{16,0},{24,8},{1,17},{9,25},{17,1},{25,9},{2,18},{10... | collective-permute-start | bytes 3145736 | tf_op jit(solution)/shard_map/ppermute | solution.py:19
  17.4 2.2 %collective-permute-done.6 = bf16[256,384]{1,0:T(8,128)(2,1)S(1)} collective-permute-done((bf16[256,384]{1,0:T(8,128)(2,1)S(1)}, bf16[256,384]{1,0:T(8,128)(2,1)S(1)}, u32[]{:S(2)}, u32[]{:S(2)}) %collective-permute-start.6) | collective-permute-done | bytes 196640 | tf_op jit(solution)/shard_map/ppermute | solution.py:287
  19.6 1.3 %collective-permute-done.5 = bf16[256,384]{1,0:T(8,128)(2,1)S(1)} collective-permute-done((bf16[256,384]{1,0:T(8,128)(2,1)S(1)}, bf16[256,384]{1,0:T(8,128)(2,1)S(1)}, u32[]{:S(2)}, u32[]{:S(2)}) %collective-permute-start.5) | collective-permute-done | bytes 196640 | tf_op jit(solution)/shard_map/ppermute | solution.py:287
  21.2 1.6 %collective-permute-start.8 = (bf16[256,384]{1,0:T(8,128)(2,1)S(1)}, bf16[256,384]{1,0:T(8,128)(2,1)S(1)}, u32[]{:S(2)}, u32[]{:S(2)}) collective-permute-start(bf16[256,384]{1,0:T(8,128)(2,1)S(1)} %fresh_columns.2), channel_id=1, source_target_pairs={{2,0},{4,2},{6,4},{7,6},{5,7},{3,5},{1,3},{0,1},{10,8},{12,10},{14... | collective-permute-start | bytes 589832 | tf_op jit(solution)/shard_map/ppermute | solution.py:287
  22.8 0.4 collective-permute-start.7
  24.1 0.5 collective-permute-start.14
  24.6 1.6 %collective-permute-start.15 = (bf16[256,384]{1,0:T(8,128)(2,1)S(1)}, bf16[256,384]{1,0:T(8,128)(2,1)S(1)}, u32[]{:S(2)}, u32[]{:S(2)}) collective-permute-start(bf16[256,384]{1,0:T(8,128)(2,1)S(1)} %collective-permute-done.6), channel_id=1, source_target_pairs={{2,0},{4,2},{6,4},{7,6},{5,7},{3,5},{1,3},{0,1},{10,8},{12,10},{14... | collective-permute-start | bytes 589832 | tf_op jit(solution)/shard_map/ppermute | solution.py:287
  26.3 1.1 %own_step.1 = (bf16[256,768]{1,0:T(8,128)(2,1)S(1)}, f32[256,512]{1,0:T(8,128)}, f32[256,128]{1,0:T(8,128)}, f32[256,128]{1,0:T(8,128)}) custom-call(f32[256,768]{1,0:T(8,128)S(1)} %get-tuple-element.62.half, f32[256,768]{1,0:T(8,128)S(1)} %get-tuple-element.63.outer, bf16[256,768]{1,0:T(8,128)(2,1)S(1)} %collective-permute-done.2.sibling, ...), custom_call_target="tpu_custom_call" | custom-call | tf_op jit(solution)/shard_map/own_step/pallas_call | solution.py:126
  27.3 1.7 %collective-permute-done.8 = bf16[256,384]{1,0:T(8,128)(2,1)S(1)} collective-permute-done((bf16[256,384]{1,0:T(8,128)(2,1)S(1)}, bf16[256,384]{1,0:T(8,128)(2,1)S(1)}, u32[]{:S(2)}, u32[]{:S(2)}) %collective-permute-start.8) | collective-permute-done | bytes 196640 | tf_op jit(solution)/shard_map/ppermute | solution.py:287
  29.3 1.2 %collective-permute-done.7 = bf16[256,384]{1,0:T(8,128)(2,1)S(1)} collective-permute-done((bf16[256,384]{1,0:T(8,128)(2,1)S(1)}, bf16[256,384]{1,0:T(8,128)(2,1)S(1)}, u32[]{:S(2)}, u32[]{:S(2)}) %collective-permute-start.7) | collective-permute-done | bytes 196640 | tf_op jit(solution)/shard_map/ppermute | solution.py:287
  30.5 0.3 fusion.20
  30.8 0.5 collective-permute-start.9
  31.3 1.6 %collective-permute-start.10 = (bf16[256,384]{1,0:T(8,128)(2,1)S(1)}, bf16[256,384]{1,0:T(8,128)(2,1)S(1)}, u32[]{:S(2)}, u32[]{:S(2)}) collective-permute-start(bf16[256,384]{1,0:T(8,128)(2,1)S(1)} %collective-permute-done.8), channel_id=1, source_target_pairs={{2,0},{4,2},{6,4},{7,6},{5,7},{3,5},{1,3},{0,1},{10,8},{12,10},{14... | collective-permute-start | bytes 589832 | tf_op jit(solution)/shard_map/ppermute | solution.py:287
  33.5 1.2 %collective-permute-done.14 = bf16[256,384]{1,0:T(8,128)(2,1)S(1)} collective-permute-done((bf16[256,384]{1,0:T(8,128)(2,1)S(1)}, bf16[256,384]{1,0:T(8,128)(2,1)S(1)}, u32[]{:S(2)}, u32[]{:S(2)}) %collective-permute-start.14) | collective-permute-done | bytes 196640 | tf_op jit(solution)/shard_map/ppermute | solution.py:287
  35.0 0.5 collective-permute-start.16
  35.5 1.6 %collective-permute-start.17 = (bf16[256,384]{1,0:T(8,128)(2,1)S(1)}, bf16[256,384]{1,0:T(8,128)(2,1)S(1)}, u32[]{:S(2)}, u32[]{:S(2)}) collective-permute-start(bf16[256,384]{1,0:T(8,128)(2,1)S(1)} %collective-permute-done.15), channel_id=1, source_target_pairs={{2,0},{4,2},{6,4},{7,6},{5,7},{3,5},{1,3},{0,1},{10,8},{12,10},{14... | collective-permute-start | bytes 589832 | tf_op jit(solution)/shard_map/ppermute | solution.py:287
  37.9 1.5 %collective-permute-done.12 = bf16[256,2048]{1,0:T(8,128)(2,1)S(1)} collective-permute-done((bf16[256,2048]{1,0:T(8,128)(2,1)S(1)}, bf16[256,2048]{1,0:T(8,128)(2,1)S(1)}, u32[]{:S(2)}, u32[]{:S(2)}) %collective-permute-start.12) | collective-permute-done | bytes 1048608 | tf_op jit(solution)/shard_map/ppermute | solution.py:19
  39.3 0.3 fusion.19
  39.7 1.9 %collective-permute-start.11 = (bf16[256,384]{1,0:T(8,128)(2,1)S(1)}, bf16[256,384]{1,0:T(8,128)(2,1)S(1)}, u32[]{:S(2)}, u32[]{:S(2)}) collective-permute-start(bf16[256,384]{1,0:T(8,128)(2,1)S(1)} %collective-permute-done.9), channel_id=1, source_target_pairs={{0,2},{2,4},{4,6},{6,7},{7,5},{5,3},{3,1},{1,0},{8,10},{10,12},{12... | collective-permute-start | bytes 589832 | tf_op jit(solution)/shard_map/ppermute | solution.py:287
  42.4 1.8 %collective-permute-start.20 = (bf16[128,384]{1,0:T(8,128)(2,1)S(1)}, bf16[128,384]{1,0:T(8,128)(2,1)S(1)}, u32[]{:S(2)}, u32[]{:S(2)}) collective-permute-start(bf16[128,384]{1,0:T(8,128)(2,1)S(1)} %slice.47), channel_id=1, source_target_pairs={{2,0},{4,2},{6,4},{7,6},{5,7},{3,5},{1,3},{0,1},{10,8},{12,10},{14... | collective-permute-start | bytes 294920 | tf_op jit(solution)/shard_map/ppermute | solution.py:293
  44.6 1.8 %collective-permute-start.23 = (bf16[256,768]{1,0:T(8,128)(2,1)S(1)}, bf16[256,768]{1,0:T(8,128)(2,1)S(1)}, u32[]{:S(2)}, u32[]{:S(2)}) collective-permute-start(bf16[256,768]{1,0:T(8,128)(2,1)S(1)} %get-tuple-element.100.own), channel_id=1, source_target_pairs={{0,16},{8,24},{16,0},{24,8},{1,17},{9,25},{17,1},{25,9},{2,18},{10... | collective-permute-start | bytes 1179656 | tf_op jit(solution)/shard_map/ppermute | solution.py:19
  48.3 0.4 fusion.18
  48.7 0.6 collective-permute-done.18
  49.9 0.8 %collective-permute-done.20 = bf16[128,384]{1,0:T(8,128)(2,1)S(1)} collective-permute-done((bf16[128,384]{1,0:T(8,128)(2,1)S(1)}, bf16[128,384]{1,0:T(8,128)(2,1)S(1)}, u32[]{:S(2)}, u32[]{:S(2)}) %collective-permute-start.20) | collective-permute-done | bytes 98336 | tf_op jit(solution)/shard_map/ppermute | solution.py:293
  51.9 1.6 %collective-permute-start.29 = (bf16[256,384]{1,0:T(8,128)(2,1)S(1)}, bf16[256,384]{1,0:T(8,128)(2,1)S(1)}, u32[]{:S(2)}, u32[]{:S(2)}) collective-permute-start(bf16[256,384]{1,0:T(8,128)(2,1)S(1)} %get-tuple-element.109), channel_id=1, source_target_pairs={{0,24},{8,16},{16,8},{24,0},{1,25},{9,17},{17,9},{25,1},{2,26},{10... | collective-permute-start | bytes 589832 | tf_op jit(solution)/shard_map/ppermute | solution.py:19
  53.6 0.5 collective-permute-start.28
  54.2 0.3 collective-permute-start.24
  54.5 1.7 %collective-permute-start.22 = (bf16[128,384]{1,0:T(8,128)(2,1)S(1)}, bf16[128,384]{1,0:T(8,128)(2,1)S(1)}, u32[]{:S(2)}, u32[]{:S(2)}) collective-permute-start(bf16[128,384]{1,0:T(8,128)(2,1)S(1)} %slice.49), channel_id=1, source_target_pairs={{0,2},{2,4},{4,6},{6,7},{7,5},{5,3},{3,1},{1,0},{8,10},{10,12},{12... | collective-permute-start | bytes 294920 | tf_op jit(solution)/shard_map/ppermute | solution.py:293
  58.0 0.8 %collective-permute-done.24 = bf16[128,384]{1,0:T(8,128)(2,1)S(1)} collective-permute-done((bf16[128,384]{1,0:T(8,128)(2,1)S(1)}, bf16[128,384]{1,0:T(8,128)(2,1)S(1)}, u32[]{:S(2)}, u32[]{:S(2)}) %collective-permute-start.24) | collective-permute-done | bytes 98336 | tf_op jit(solution)/shard_map/ppermute | solution.py:293
  60.3 0.6 collective-permute-start.30
  60.9 0.5 fusion.21
  61.5 1.3 %collective-permute-start.27 = (bf16[256,384]{1,0:T(8,128)(2,1)S(1)}, bf16[256,384]{1,0:T(8,128)(2,1)S(1)}, u32[]{:S(2)}, u32[]{:S(2)}) collective-permute-start(bf16[256,384]{1,0:T(8,128)(2,1)S(1)} %get-tuple-element.113), channel_id=1, source_target_pairs={{0,24},{8,16},{16,8},{24,0},{1,25},{9,17},{17,9},{25,1},{2,26},{10... | collective-permute-start | bytes 589832 | tf_op jit(solution)/shard_map/ppermute | solution.py:19
  62.8 0.5 collective-permute-start.26
  63.3 0.4 collective-permute-done.28.refs_2_
  63.6 1.0 %place_leading.1.refs_4_ = bf16[256,3072]{1,0:T(8,128)(2,1)} custom-call(s32[1]{0:T(128)} %bitcast.where, bf16[256,384]{1,0:T(8,128)(2,1)S(1)} %get-tuple-element.111.refs_0_, bf16[256,384]{1,0:T(8,128)(2,1)S(1)} %collective-permute-done.21.refs_1_, bf16[256,384]{1,0:T(8,128)(2,1)S(1)} %collective-permute-done.28.refs_2_, ...), custom_call_target="tpu_custom_call" | custom-call | tf_op jit(solution)/shard_map/place_leading/pallas_call | solution.py:201
  64.7 2.0 %outer_minus_delta.1 = (f32[256,2048]{1,0:T(8,128)}, f32[256,512]{1,0:T(8,128)}, f32[256,512]{1,0:T(8,128)}) custom-call(s32[1]{0:T(128)} %bitcast.where, f32[256,2048]{1,0:T(8,128)S(1)} %copy-done, f32[256,512]{1,0:T(8,128)S(1)} %copy-done.1, f32[256,512]{1,0:T(8,128)S(1)} %copy-done.2, bf16[256,768]{1,0:T(8,128)(2,1)S(1)} %get-tuple-element.100.own, ...), custom_call_target="tpu_custom_call" | custom-call | tf_op jit(solution)/shard_map/outer_minus_delta/pallas_call | solution.py:176
  66.7 1.9 %collective-permute-done.27.refs_3_ = bf16[256,384]{1,0:T(8,128)(2,1)S(1)} collective-permute-done((bf16[256,384]{1,0:T(8,128)(2,1)S(1)}, bf16[256,384]{1,0:T(8,128)(2,1)S(1)}, u32[]{:S(2)}, u32[]{:S(2)}) %collective-permute-start.27) | collective-permute-done | bytes 196640 | tf_op jit(solution)/shard_map/ppermute | solution.py:19
  68.6 4.4 %collective-permute-done.26.refs_2_ = bf16[256,384]{1,0:T(8,128)(2,1)S(1)} collective-permute-done((bf16[256,384]{1,0:T(8,128)(2,1)S(1)}, bf16[256,384]{1,0:T(8,128)(2,1)S(1)}, u32[]{:S(2)}, u32[]{:S(2)}) %collective-permute-start.26) | collective-permute-done | bytes 196640 | tf_op jit(solution)/shard_map/ppermute | solution.py:19
  73.0 0.9 %place_second.1 = bf16[256,3072]{1,0:T(8,128)(2,1)} custom-call(s32[1]{0:T(128)} %bitcast.where, bf16[256,384]{1,0:T(8,128)(2,1)S(1)} %get-tuple-element.116.refs_0_, bf16[256,384]{1,0:T(8,128)(2,1)S(1)} %collective-permute-done.25.refs_1_, bf16[256,384]{1,0:T(8,128)(2,1)S(1)} %collective-permute-done.26.refs_2_, ...), custom_call_target="tpu_custom_call", output_to_operand_aliasing={{}: (5, {})} | custom-call | tf_op jit(solution)/shard_map/place_second/pallas_call | solution.py:201
  (89 shorter events, 12.2 us)
Async XLA Ops:
  1.8 2.5 %collective-permute-start.1 = (bf16[256,768]{1,0:T(8,128)(2,1)S(1)}, bf16[256,768]{1,0:T(8,128)(2,1)S(1)}, u32[]{:S(2)}, u32[]{:S(2)}) collective-permute-start(bf16[256,768]{1,0:T(8,128)(2,1)S(1)} %get-tuple-element.60), channel_id=1, source_target_pairs={{0,8},{8,0},{16,24},{24,16},{1,9},{9,1},{17,25},{25,17},{2,10},{10... | collective-permute-start | bytes 1179656 | tf_op jit(solution)/shard_map/ppermute | solution.py:19
  2.3 14.8 %collective-permute-start = (bf16[256,2048]{1,0:T(8,128)(2,1)}, bf16[256,2048]{1,0:T(8,128)(2,1)S(1)}, u32[]{:S(2)}, u32[]{:S(2)}) collective-permute-start(bf16[256,2048]{1,0:T(8,128)(2,1)} %param.10), channel_id=1, source_target_pairs={{0,8},{8,0},{16,24},{24,16},{1,9},{9,1},{17,25},{25,17},{2,10},{10... | collective-permute-start | bytes 3145736 | tf_op jit(solution)/shard_map/ppermute | solution.py:19
  2.4 7.4 %collective-permute-start.2 = (bf16[256,768]{1,0:T(8,128)(2,1)S(1)}, bf16[256,768]{1,0:T(8,128)(2,1)S(1)}, u32[]{:S(2)}, u32[]{:S(2)}) collective-permute-start(bf16[256,768]{1,0:T(8,128)(2,1)S(1)} %get-tuple-element.64), channel_id=1, source_target_pairs={{0,8},{8,0},{16,24},{24,16},{1,9},{9,1},{17,25},{25,17},{2,10},{10... | collective-permute-start | bytes 1179656 | tf_op jit(solution)/shard_map/ppermute | solution.py:19
  4.3 2.9 %copy-start.6 = (bf16[256,2048]{1,0:T(8,128)(2,1)S(1)}, bf16[256,2048]{1,0:T(8,128)(2,1)}, u32[]{:S(2)}) copy-start(bf16[256,2048]{1,0:T(8,128)(2,1)} %param.10) | copy-start | bytes 3145732
  4.5 8.4 %collective-permute-start.4 = (bf16[256,384]{1,0:T(8,128)(2,1)S(1)}, bf16[256,384]{1,0:T(8,128)(2,1)S(1)}, u32[]{:S(2)}, u32[]{:S(2)}) collective-permute-start(bf16[256,384]{1,0:T(8,128)(2,1)S(1)} %get-tuple-element.118), channel_id=1, source_target_pairs={{0,16},{8,24},{16,0},{24,8},{1,17},{9,25},{17,1},{25,9},{2,18},{10... | collective-permute-start | bytes 589832 | tf_op jit(solution)/shard_map/ppermute | solution.py:19
  7.3 5.6 %copy-start.3 = (f32[256,512]{1,0:T(8,128)S(1)}, f32[256,512]{1,0:T(8,128)}, u32[]{:S(2)}) copy-start(f32[256,512]{1,0:T(8,128)} %moment_q.5) | copy-start | bytes 1572868
  7.3 5.6 %copy-start.4 = (f32[256,128]{1,0:T(8,128)S(1)}, f32[256,128]{1,0:T(8,128)}, u32[]{:S(2)}) copy-start(f32[256,128]{1,0:T(8,128)} %moment_k.5) | copy-start | bytes 393220
  7.3 5.6 %copy-start.5 = (f32[256,128]{1,0:T(8,128)S(1)}, f32[256,128]{1,0:T(8,128)}, u32[]{:S(2)}) copy-start(f32[256,128]{1,0:T(8,128)} %moment_v.5) | copy-start | bytes 393220
  7.3 9.9 %collective-permute-start.3 = (bf16[256,384]{1,0:T(8,128)(2,1)S(1)}, bf16[256,384]{1,0:T(8,128)(2,1)S(1)}, u32[]{:S(2)}, u32[]{:S(2)}) collective-permute-start(bf16[256,384]{1,0:T(8,128)(2,1)S(1)} %get-tuple-element.117), channel_id=1, source_target_pairs={{0,16},{8,24},{16,0},{24,8},{1,17},{9,25},{17,1},{25,9},{2,18},{10... | collective-permute-start | bytes 589832 | tf_op jit(solution)/shard_map/ppermute | solution.py:19
  13.1 6.5 %collective-permute-start.6 = (bf16[256,384]{1,0:T(8,128)(2,1)S(1)}, bf16[256,384]{1,0:T(8,128)(2,1)S(1)}, u32[]{:S(2)}, u32[]{:S(2)}) collective-permute-start(bf16[256,384]{1,0:T(8,128)(2,1)S(1)} %fresh_columns.3), channel_id=1, source_target_pairs={{2,0},{4,2},{6,4},{7,6},{5,7},{3,5},{1,3},{0,1},{10,8},{12,10},{14... | collective-permute-start | bytes 589832 | tf_op jit(solution)/shard_map/ppermute | solution.py:287
  15.1 5.7 %collective-permute-start.5 = (bf16[256,384]{1,0:T(8,128)(2,1)S(1)}, bf16[256,384]{1,0:T(8,128)(2,1)S(1)}, u32[]{:S(2)}, u32[]{:S(2)}) collective-permute-start(bf16[256,384]{1,0:T(8,128)(2,1)S(1)} %fresh_columns.3), channel_id=1, source_target_pairs={{0,2},{2,4},{4,6},{6,7},{7,5},{5,3},{3,1},{1,0},{8,10},{10,12},{12... | collective-permute-start | bytes 589832 | tf_op jit(solution)/shard_map/ppermute | solution.py:287
  15.3 24.1 %collective-permute-start.12 = (bf16[256,2048]{1,0:T(8,128)(2,1)S(1)}, bf16[256,2048]{1,0:T(8,128)(2,1)S(1)}, u32[]{:S(2)}, u32[]{:S(2)}) collective-permute-start(bf16[256,2048]{1,0:T(8,128)(2,1)S(1)} %copy-done.6), channel_id=1, source_target_pairs={{0,16},{8,24},{16,0},{24,8},{1,17},{9,25},{17,1},{25,9},{2,18},{10... | collective-permute-start | bytes 3145736 | tf_op jit(solution)/shard_map/ppermute | solution.py:19
  21.2 7.8 %collective-permute-start.8 = (bf16[256,384]{1,0:T(8,128)(2,1)S(1)}, bf16[256,384]{1,0:T(8,128)(2,1)S(1)}, u32[]{:S(2)}, u32[]{:S(2)}) collective-permute-start(bf16[256,384]{1,0:T(8,128)(2,1)S(1)} %fresh_columns.2), channel_id=1, source_target_pairs={{2,0},{4,2},{6,4},{7,6},{5,7},{3,5},{1,3},{0,1},{10,8},{12,10},{14... | collective-permute-start | bytes 589832 | tf_op jit(solution)/shard_map/ppermute | solution.py:287
  22.8 7.7 %collective-permute-start.7 = (bf16[256,384]{1,0:T(8,128)(2,1)S(1)}, bf16[256,384]{1,0:T(8,128)(2,1)S(1)}, u32[]{:S(2)}, u32[]{:S(2)}) collective-permute-start(bf16[256,384]{1,0:T(8,128)(2,1)S(1)} %fresh_columns.2), channel_id=1, source_target_pairs={{0,2},{2,4},{4,6},{6,7},{7,5},{5,3},{3,1},{1,0},{8,10},{10,12},{12... | collective-permute-start | bytes 589832 | tf_op jit(solution)/shard_map/ppermute | solution.py:287
  24.1 10.5 %collective-permute-start.14 = (bf16[256,384]{1,0:T(8,128)(2,1)S(1)}, bf16[256,384]{1,0:T(8,128)(2,1)S(1)}, u32[]{:S(2)}, u32[]{:S(2)}) collective-permute-start(bf16[256,384]{1,0:T(8,128)(2,1)S(1)} %collective-permute-done.5), channel_id=1, source_target_pairs={{0,2},{2,4},{4,6},{6,7},{7,5},{5,3},{3,1},{1,0},{8,10},{10,12},{12... | collective-permute-start | bytes 589832 | tf_op jit(solution)/shard_map/ppermute | solution.py:287
  24.6 8.6 %collective-permute-start.15 = (bf16[256,384]{1,0:T(8,128)(2,1)S(1)}, bf16[256,384]{1,0:T(8,128)(2,1)S(1)}, u32[]{:S(2)}, u32[]{:S(2)}) collective-permute-start(bf16[256,384]{1,0:T(8,128)(2,1)S(1)} %collective-permute-done.6), channel_id=1, source_target_pairs={{2,0},{4,2},{6,4},{7,6},{5,7},{3,5},{1,3},{0,1},{10,8},{12,10},{14... | collective-permute-start | bytes 589832 | tf_op jit(solution)/shard_map/ppermute | solution.py:287
  30.8 7.0 %collective-permute-start.9 = (bf16[256,384]{1,0:T(8,128)(2,1)S(1)}, bf16[256,384]{1,0:T(8,128)(2,1)S(1)}, u32[]{:S(2)}, u32[]{:S(2)}) collective-permute-start(bf16[256,384]{1,0:T(8,128)(2,1)S(1)} %collective-permute-done.7), channel_id=1, source_target_pairs={{0,2},{2,4},{4,6},{6,7},{7,5},{5,3},{3,1},{1,0},{8,10},{10,12},{12... | collective-permute-start | bytes 589832 | tf_op jit(solution)/shard_map/ppermute | solution.py:287
  31.3 6.0 %collective-permute-start.10 = (bf16[256,384]{1,0:T(8,128)(2,1)S(1)}, bf16[256,384]{1,0:T(8,128)(2,1)S(1)}, u32[]{:S(2)}, u32[]{:S(2)}) collective-permute-start(bf16[256,384]{1,0:T(8,128)(2,1)S(1)} %collective-permute-done.8), channel_id=1, source_target_pairs={{2,0},{4,2},{6,4},{7,6},{5,7},{3,5},{1,3},{0,1},{10,8},{12,10},{14... | collective-permute-start | bytes 589832 | tf_op jit(solution)/shard_map/ppermute | solution.py:287
  35.0 7.0 %collective-permute-start.16 = (bf16[256,384]{1,0:T(8,128)(2,1)S(1)}, bf16[256,384]{1,0:T(8,128)(2,1)S(1)}, u32[]{:S(2)}, u32[]{:S(2)}) collective-permute-start(bf16[256,384]{1,0:T(8,128)(2,1)S(1)} %collective-permute-done.14), channel_id=1, source_target_pairs={{0,2},{2,4},{4,6},{6,7},{7,5},{5,3},{3,1},{1,0},{8,10},{10,12},{12... | collective-permute-start | bytes 589832 | tf_op jit(solution)/shard_map/ppermute | solution.py:287
  35.5 6.2 %collective-permute-start.17 = (bf16[256,384]{1,0:T(8,128)(2,1)S(1)}, bf16[256,384]{1,0:T(8,128)(2,1)S(1)}, u32[]{:S(2)}, u32[]{:S(2)}) collective-permute-start(bf16[256,384]{1,0:T(8,128)(2,1)S(1)} %collective-permute-done.15), channel_id=1, source_target_pairs={{2,0},{4,2},{6,4},{7,6},{5,7},{3,5},{1,3},{0,1},{10,8},{12,10},{14... | collective-permute-start | bytes 589832 | tf_op jit(solution)/shard_map/ppermute | solution.py:287
  39.3 5.2 %collective-permute-start.13 = (bf16[256,2048]{1,0:T(8,128)(2,1)S(1)}, bf16[256,2048]{1,0:T(8,128)(2,1)S(1)}, u32[]{:S(2)}, u32[]{:S(2)}) collective-permute-start(bf16[256,2048]{1,0:T(8,128)(2,1)S(1)} %collective-permute-done.12), channel_id=1, source_target_pairs={{0,8},{8,0},{16,24},{24,16},{1,9},{9,1},{17,25},{25,17},{2,10},{10... | collective-permute-start | bytes 3145736 | tf_op jit(solution)/shard_map/ppermute | solution.py:19
  39.7 9.6 %collective-permute-start.11 = (bf16[256,384]{1,0:T(8,128)(2,1)S(1)}, bf16[256,384]{1,0:T(8,128)(2,1)S(1)}, u32[]{:S(2)}, u32[]{:S(2)}) collective-permute-start(bf16[256,384]{1,0:T(8,128)(2,1)S(1)} %collective-permute-done.9), channel_id=1, source_target_pairs={{0,2},{2,4},{4,6},{6,7},{7,5},{5,3},{3,1},{1,0},{8,10},{10,12},{12... | collective-permute-start | bytes 589832 | tf_op jit(solution)/shard_map/ppermute | solution.py:287
  41.6 7.7 %collective-permute-start.18 = (bf16[256,384]{1,0:T(8,128)(2,1)S(1)}, bf16[256,384]{1,0:T(8,128)(2,1)S(1)}, u32[]{:S(2)}, u32[]{:S(2)}) collective-permute-start(bf16[256,384]{1,0:T(8,128)(2,1)S(1)} %collective-permute-done.10), channel_id=1, source_target_pairs={{2,0},{4,2},{6,4},{7,6},{5,7},{3,5},{1,3},{0,1},{10,8},{12,10},{14... | collective-permute-start | bytes 589832 | tf_op jit(solution)/shard_map/ppermute | solution.py:287
  42.4 8.3 %collective-permute-start.20 = (bf16[128,384]{1,0:T(8,128)(2,1)S(1)}, bf16[128,384]{1,0:T(8,128)(2,1)S(1)}, u32[]{:S(2)}, u32[]{:S(2)}) collective-permute-start(bf16[128,384]{1,0:T(8,128)(2,1)S(1)} %slice.47), channel_id=1, source_target_pairs={{2,0},{4,2},{6,4},{7,6},{5,7},{3,5},{1,3},{0,1},{10,8},{12,10},{14... | collective-permute-start | bytes 294920 | tf_op jit(solution)/shard_map/ppermute | solution.py:293
  44.2 7.0 %collective-permute-start.19 = (bf16[128,384]{1,0:T(8,128)(2,1)S(1)}, bf16[128,384]{1,0:T(8,128)(2,1)S(1)}, u32[]{:S(2)}, u32[]{:S(2)}) collective-permute-start(bf16[128,384]{1,0:T(8,128)(2,1)S(1)} %slice.46), channel_id=1, source_target_pairs={{0,2},{2,4},{4,6},{6,7},{7,5},{5,3},{3,1},{1,0},{8,10},{10,12},{12... | collective-permute-start | bytes 294920 | tf_op jit(solution)/shard_map/ppermute | solution.py:293
  44.6 13.4 %collective-permute-start.23 = (bf16[256,768]{1,0:T(8,128)(2,1)S(1)}, bf16[256,768]{1,0:T(8,128)(2,1)S(1)}, u32[]{:S(2)}, u32[]{:S(2)}) collective-permute-start(bf16[256,768]{1,0:T(8,128)(2,1)S(1)} %get-tuple-element.100.own), channel_id=1, source_target_pairs={{0,16},{8,24},{16,0},{24,8},{1,17},{9,25},{17,1},{25,9},{2,18},{10... | collective-permute-start | bytes 1179656 | tf_op jit(solution)/shard_map/ppermute | solution.py:19
  51.8 2.3 %collective-permute-start.21 = (bf16[256,384]{1,0:T(8,128)(2,1)S(1)}, bf16[256,384]{1,0:T(8,128)(2,1)S(1)}, u32[]{:S(2)}, u32[]{:S(2)}) collective-permute-start(bf16[256,384]{1,0:T(8,128)(2,1)S(1)} %get-tuple-element.112), channel_id=1, source_target_pairs={{0,8},{8,0},{16,24},{24,16},{1,9},{9,1},{17,25},{25,17},{2,10},{10... | collective-permute-start | bytes 589832 | tf_op jit(solution)/shard_map/ppermute | solution.py:19
  51.9 10.9 %collective-permute-start.29 = (bf16[256,384]{1,0:T(8,128)(2,1)S(1)}, bf16[256,384]{1,0:T(8,128)(2,1)S(1)}, u32[]{:S(2)}, u32[]{:S(2)}) collective-permute-start(bf16[256,384]{1,0:T(8,128)(2,1)S(1)} %get-tuple-element.109), channel_id=1, source_target_pairs={{0,24},{8,16},{16,8},{24,0},{1,25},{9,17},{17,9},{25,1},{2,26},{10... | collective-permute-start | bytes 589832 | tf_op jit(solution)/shard_map/ppermute | solution.py:19
  53.6 10.1 %collective-permute-start.28 = (bf16[256,384]{1,0:T(8,128)(2,1)S(1)}, bf16[256,384]{1,0:T(8,128)(2,1)S(1)}, u32[]{:S(2)}, u32[]{:S(2)}) collective-permute-start(bf16[256,384]{1,0:T(8,128)(2,1)S(1)} %get-tuple-element.110), channel_id=1, source_target_pairs={{0,16},{8,24},{16,0},{24,8},{1,17},{9,25},{17,1},{25,9},{2,18},{10... | collective-permute-start | bytes 589832 | tf_op jit(solution)/shard_map/ppermute | solution.py:19
  54.2 4.7 %collective-permute-start.24 = (bf16[128,384]{1,0:T(8,128)(2,1)S(1)}, bf16[128,384]{1,0:T(8,128)(2,1)S(1)}, u32[]{:S(2)}, u32[]{:S(2)}) collective-permute-start(bf16[128,384]{1,0:T(8,128)(2,1)S(1)} %slice.50), channel_id=1, source_target_pairs={{2,0},{4,2},{6,4},{7,6},{5,7},{3,5},{1,3},{0,1},{10,8},{12,10},{14... | collective-permute-start | bytes 294920 | tf_op jit(solution)/shard_map/ppermute | solution.py:293
  54.5 4.6 %collective-permute-start.22 = (bf16[128,384]{1,0:T(8,128)(2,1)S(1)}, bf16[128,384]{1,0:T(8,128)(2,1)S(1)}, u32[]{:S(2)}, u32[]{:S(2)}) collective-permute-start(bf16[128,384]{1,0:T(8,128)(2,1)S(1)} %slice.49), channel_id=1, source_target_pairs={{0,2},{2,4},{4,6},{6,7},{7,5},{5,3},{3,1},{1,0},{8,10},{10,12},{12... | collective-permute-start | bytes 294920 | tf_op jit(solution)/shard_map/ppermute | solution.py:293
  59.7 7.0 %collective-permute-start.25 = (bf16[256,384]{1,0:T(8,128)(2,1)S(1)}, bf16[256,384]{1,0:T(8,128)(2,1)S(1)}, u32[]{:S(2)}, u32[]{:S(2)}) collective-permute-start(bf16[256,384]{1,0:T(8,128)(2,1)S(1)} %get-tuple-element.115), channel_id=1, source_target_pairs={{0,8},{8,0},{16,24},{24,16},{1,9},{9,1},{17,25},{25,17},{2,10},{10... | collective-permute-start | bytes 589832 | tf_op jit(solution)/shard_map/ppermute | solution.py:19
  60.3 4.3 %collective-permute-start.30 = (bf16[256,1536]{1,0:T(8,128)(2,1)S(1)}, bf16[256,1536]{1,0:T(8,128)(2,1)S(1)}, u32[]{:S(2)}, u32[]{:S(2)}) collective-permute-start(bf16[256,1536]{1,0:T(8,128)(2,1)S(1)} %pad_maximum_fusion), channel_id=1, source_target_pairs={{0,8},{8,0},{16,24},{24,16},{1,9},{9,1},{17,25},{25,17},{2,10},{10... | collective-permute-start | bytes 2359304 | tf_op jit(solution)/shard_map/ppermute | solution.py:19
  61.4 3.2 %copy-start = (f32[256,2048]{1,0:T(8,128)S(1)}, f32[256,2048]{1,0:T(8,128)}, u32[]{:S(2)}) copy-start(f32[256,2048]{1,0:T(8,128)} %outer_q.1) | copy-start | bytes 6291460
  61.4 3.2 %copy-start.1 = (f32[256,512]{1,0:T(8,128)S(1)}, f32[256,512]{1,0:T(8,128)}, u32[]{:S(2)}) copy-start(f32[256,512]{1,0:T(8,128)} %outer_k.1) | copy-start | bytes 1572868
  61.4 3.2 %copy-start.2 = (f32[256,512]{1,0:T(8,128)S(1)}, f32[256,512]{1,0:T(8,128)}, u32[]{:S(2)}) copy-start(f32[256,512]{1,0:T(8,128)} %outer_v.1) | copy-start | bytes 1572868
  61.5 7.1 %collective-permute-start.27 = (bf16[256,384]{1,0:T(8,128)(2,1)S(1)}, bf16[256,384]{1,0:T(8,128)(2,1)S(1)}, u32[]{:S(2)}, u32[]{:S(2)}) collective-permute-start(bf16[256,384]{1,0:T(8,128)(2,1)S(1)} %get-tuple-element.113), channel_id=1, source_target_pairs={{0,24},{8,16},{16,8},{24,0},{1,25},{9,17},{17,9},{25,1},{2,26},{10... | collective-permute-start | bytes 589832 | tf_op jit(solution)/shard_map/ppermute | solution.py:19
  62.8 10.1 %collective-permute-start.26 = (bf16[256,384]{1,0:T(8,128)(2,1)S(1)}, bf16[256,384]{1,0:T(8,128)(2,1)S(1)}, u32[]{:S(2)}, u32[]{:S(2)}) collective-permute-start(bf16[256,384]{1,0:T(8,128)(2,1)S(1)} %get-tuple-element.114), channel_id=1, source_target_pairs={{0,16},{8,24},{16,0},{24,8},{1,17},{9,25},{17,1},{25,9},{2,18},{10... | collective-permute-start | bytes 589832 | tf_op jit(solution)/shard_map/ppermute | solution.py:19

commit v5 on v4

--- a/solution.py
+++ b/solution.py
@@ -9,7 +9,7 @@
 
 LEARN_RATE = 0.7
 MOMENTUM_BETA = 0.9
-SMALL_VMEM = 20 * 1024 * 1024
+SMALL_VMEM = 14 * 1024 * 1024
 SHORTEST_RING = 8
 LONGEST_RING = 16
 

time: 74.2 us -> 74.3 us (level)
  no operation moved by 1% of the time
where the time goes in v5:
time: 74.3 us; the launch traced here: 74.1 us
  starting transfers between devices  29.7 us (40%)
  waiting for transfers between devices  22 us (30%)
  matrix products  10.8 us (15%)
  Pallas kernels  9.35 us (13%)
  between operations  1.36 us (2%)
    ppermute x15, starting transfers between devices, from_replica(): return lax.ppermute(x, 'replica', [(i, i ^ distance) for i in range(count)])  13 us
    ppermute x12, starting transfers between devices, hop(): lax.ppermute(after(heads[stream][way], *others), 'fsdp', (up, down)[way])  12.5 us
    ppermute x15, waiting for transfers between devices, from_replica(): return lax.ppermute(x, 'replica', [(i, i ^ distance) for i in range(count)])  11.3 us
    dot_general x36, matrix products, product(): return jnp.dot(lanes, block, preferred_element_type=jnp.float32)  10.8 us
    ppermute x12, waiting for transfers between devices, hop(): lax.ppermute(after(heads[stream][way], *others), 'fsdp', (up, down)[way])  8.81 us
    ppermute x4, starting transfers between devices, last_hop(): block = lax.ppermute(part, 'fsdp', (up, down)[way])  4.16 us
    pallas_call x3, Pallas kernels, columns_call(): pl.pallas_call(kernel, out_shape=shapes, in_specs=[pl.BlockSpec(memory_sp...  4.08 us
    pallas_call x1, Pallas kernels, subtract(): pl.pallas_call(subtract_kernel, out_shape=[jax.ShapeDtypeStruct(o.shape,...  2.01 us
  transfers between devices with their start and end apart: 31, of which 17 were waited for; matrix products, arithmetic and copies ran while one was open for 16% of the time, Pallas kernels for 10%

profile of v5, /device:TPU:0, one launch (start us, length us, event | category | flops | bytes accessed | tf_op | source)
XLA Modules:
  0.0 74.1 jit_solution(17635012973953069463)
XLA Ops:
  0.6 1.2 %pack_inner.1 = (bf16[256,768]{1,0:T(8,128)(2,1)S(1)}, bf16[256,768]{1,0:T(8,128)(2,1)S(1)}) custom-call(s32[1]{0:T(128)} %bitcast.where, bf16[256,2048]{1,0:T(8,128)(2,1)} %bitcast.40, bf16[256,512]{1,0:T(8,128)(2,1)} %bitcast.43, bf16[256,512]{1,0:T(8,128)(2,1)} %bitcast.46), custom_call_target="tpu_custom_call" | custom-call | tf_op jit(solution)/shard_map/pack_inner/pallas_call | solution.py:67
  1.8 0.5 collective-permute-start.1
  2.4 0.4 collective-permute-start.2
  2.8 1.5 %far_half.1 = (f32[256,768]{1,0:T(8,128)S(1)}, f32[256,768]{1,0:T(8,128)S(1)}) custom-call(s32[1]{0:T(128)} %bitcast.where, bf16[256,2048]{1,0:T(8,128)(2,1)} %bitcast.41, bf16[256,512]{1,0:T(8,128)(2,1)} %bitcast.44, bf16[256,512]{1,0:T(8,128)(2,1)} %bitcast.47, f32[256,2048]{1,0:T(8,128)} %outer_q.1, f32[256,512]{1,0:T(8,128)} %outer_k.1, f32[256,512]{1,0:T(8,128)} %outer_v.1), custom_call_target="tpu_custom_call" | custom-call | tf_op jit(solution)/shard_map/far_half/pallas_call | solution.py:67
  4.5 2.6 %collective-permute-start.4 = (bf16[256,384]{1,0:T(8,128)(2,1)S(1)}, bf16[256,384]{1,0:T(8,128)(2,1)S(1)}, u32[]{:S(2)}, u32[]{:S(2)}) collective-permute-start(bf16[256,384]{1,0:T(8,128)(2,1)S(1)} %get-tuple-element.118), channel_id=1, source_target_pairs={{0,16},{8,24},{16,0},{24,8},{1,17},{9,25},{17,1},{25,9},{2,18},{10... | collective-permute-start | bytes 589832 | tf_op jit(solution)/shard_map/ppermute | solution.py:19
  7.3 1.0 %collective-permute-start.3 = (bf16[256,384]{1,0:T(8,128)(2,1)S(1)}, bf16[256,384]{1,0:T(8,128)(2,1)S(1)}, u32[]{:S(2)}, u32[]{:S(2)}) collective-permute-start(bf16[256,384]{1,0:T(8,128)(2,1)S(1)} %get-tuple-element.117), channel_id=1, source_target_pairs={{0,16},{8,24},{16,0},{24,8},{1,17},{9,25},{17,1},{25,9},{2,18},{10... | collective-permute-start | bytes 589832 | tf_op jit(solution)/shard_map/ppermute | solution.py:19
  8.3 1.5 %near_half.1 = (f32[256,768]{1,0:T(8,128)S(1)}, f32[256,768]{1,0:T(8,128)S(1)}) custom-call(s32[1]{0:T(128)} %bitcast.where, bf16[256,2048]{1,0:T(8,128)(2,1)} %bitcast.42, bf16[256,512]{1,0:T(8,128)(2,1)} %bitcast.45, bf16[256,512]{1,0:T(8,128)(2,1)} %bitcast.48, f32[256,2048]{1,0:T(8,128)} %outer_q.1, f32[256,512]{1,0:T(8,128)} %outer_k.1, f32[256,512]{1,0:T(8,128)} %outer_v.1), custom_call_target="tpu_custom_call" | custom-call | tf_op jit(solution)/shard_map/near_half/pallas_call | solution.py:67
  9.8 3.1 %collective-permute-done.4.remote = bf16[256,384]{1,0:T(8,128)(2,1)S(1)} collective-permute-done((bf16[256,384]{1,0:T(8,128)(2,1)S(1)}, bf16[256,384]{1,0:T(8,128)(2,1)S(1)}, u32[]{:S(2)}, u32[]{:S(2)}) %collective-permute-start.4) | collective-permute-done | bytes 196640 | tf_op jit(solution)/shard_map/ppermute | solution.py:19
  13.1 2.0 %collective-permute-start.6 = (bf16[256,384]{1,0:T(8,128)(2,1)S(1)}, bf16[256,384]{1,0:T(8,128)(2,1)S(1)}, u32[]{:S(2)}, u32[]{:S(2)}) collective-permute-start(bf16[256,384]{1,0:T(8,128)(2,1)S(1)} %fresh_columns.3), channel_id=1, source_target_pairs={{2,0},{4,2},{6,4},{7,6},{5,7},{3,5},{1,3},{0,1},{10,8},{12,10},{14... | collective-permute-start | bytes 589832 | tf_op jit(solution)/shard_map/ppermute | solution.py:287
  15.3 1.9 %collective-permute-start.12 = (bf16[256,2048]{1,0:T(8,128)(2,1)S(1)}, bf16[256,2048]{1,0:T(8,128)(2,1)S(1)}, u32[]{:S(2)}, u32[]{:S(2)}) collective-permute-start(bf16[256,2048]{1,0:T(8,128)(2,1)S(1)} %copy-done.6), channel_id=1, source_target_pairs={{0,16},{8,24},{16,0},{24,8},{1,17},{9,25},{17,1},{25,9},{2,18},{10... | collective-permute-start | bytes 3145736 | tf_op jit(solution)/shard_map/ppermute | solution.py:19
  17.4 2.2 %collective-permute-done.6 = bf16[256,384]{1,0:T(8,128)(2,1)S(1)} collective-permute-done((bf16[256,384]{1,0:T(8,128)(2,1)S(1)}, bf16[256,384]{1,0:T(8,128)(2,1)S(1)}, u32[]{:S(2)}, u32[]{:S(2)}) %collective-permute-start.6) | collective-permute-done | bytes 196640 | tf_op jit(solution)/shard_map/ppermute | solution.py:287
  19.6 1.3 %collective-permute-done.5 = bf16[256,384]{1,0:T(8,128)(2,1)S(1)} collective-permute-done((bf16[256,384]{1,0:T(8,128)(2,1)S(1)}, bf16[256,384]{1,0:T(8,128)(2,1)S(1)}, u32[]{:S(2)}, u32[]{:S(2)}) %collective-permute-start.5) | collective-permute-done | bytes 196640 | tf_op jit(solution)/shard_map/ppermute | solution.py:287
  21.2 1.6 %collective-permute-start.8 = (bf16[256,384]{1,0:T(8,128)(2,1)S(1)}, bf16[256,384]{1,0:T(8,128)(2,1)S(1)}, u32[]{:S(2)}, u32[]{:S(2)}) collective-permute-start(bf16[256,384]{1,0:T(8,128)(2,1)S(1)} %fresh_columns.2), channel_id=1, source_target_pairs={{2,0},{4,2},{6,4},{7,6},{5,7},{3,5},{1,3},{0,1},{10,8},{12,10},{14... | collective-permute-start | bytes 589832 | tf_op jit(solution)/shard_map/ppermute | solution.py:287
  22.8 0.4 collective-permute-start.7
  24.1 0.5 collective-permute-start.14
  24.6 1.6 %collective-permute-start.15 = (bf16[256,384]{1,0:T(8,128)(2,1)S(1)}, bf16[256,384]{1,0:T(8,128)(2,1)S(1)}, u32[]{:S(2)}, u32[]{:S(2)}) collective-permute-start(bf16[256,384]{1,0:T(8,128)(2,1)S(1)} %collective-permute-done.6), channel_id=1, source_target_pairs={{2,0},{4,2},{6,4},{7,6},{5,7},{3,5},{1,3},{0,1},{10,8},{12,10},{14... | collective-permute-start | bytes 589832 | tf_op jit(solution)/shard_map/ppermute | solution.py:287
  26.3 1.0 %own_step.1 = (bf16[256,768]{1,0:T(8,128)(2,1)S(1)}, f32[256,512]{1,0:T(8,128)}, f32[256,128]{1,0:T(8,128)}, f32[256,128]{1,0:T(8,128)}) custom-call(f32[256,768]{1,0:T(8,128)S(1)} %get-tuple-element.62.half, f32[256,768]{1,0:T(8,128)S(1)} %get-tuple-element.63.outer, bf16[256,768]{1,0:T(8,128)(2,1)S(1)} %collective-permute-done.2.sibling, ...), custom_call_target="tpu_custom_call" | custom-call | tf_op jit(solution)/shard_map/own_step/pallas_call | solution.py:126
  27.3 1.7 %collective-permute-done.8 = bf16[256,384]{1,0:T(8,128)(2,1)S(1)} collective-permute-done((bf16[256,384]{1,0:T(8,128)(2,1)S(1)}, bf16[256,384]{1,0:T(8,128)(2,1)S(1)}, u32[]{:S(2)}, u32[]{:S(2)}) %collective-permute-start.8) | collective-permute-done | bytes 196640 | tf_op jit(solution)/shard_map/ppermute | solution.py:287
  29.3 1.2 %collective-permute-done.7 = bf16[256,384]{1,0:T(8,128)(2,1)S(1)} collective-permute-done((bf16[256,384]{1,0:T(8,128)(2,1)S(1)}, bf16[256,384]{1,0:T(8,128)(2,1)S(1)}, u32[]{:S(2)}, u32[]{:S(2)}) %collective-permute-start.7) | collective-permute-done | bytes 196640 | tf_op jit(solution)/shard_map/ppermute | solution.py:287
  30.8 0.5 collective-permute-start.9
  31.3 1.6 %collective-permute-start.10 = (bf16[256,384]{1,0:T(8,128)(2,1)S(1)}, bf16[256,384]{1,0:T(8,128)(2,1)S(1)}, u32[]{:S(2)}, u32[]{:S(2)}) collective-permute-start(bf16[256,384]{1,0:T(8,128)(2,1)S(1)} %collective-permute-done.8), channel_id=1, source_target_pairs={{2,0},{4,2},{6,4},{7,6},{5,7},{3,5},{1,3},{0,1},{10,8},{12,10},{14... | collective-permute-start | bytes 589832 | tf_op jit(solution)/shard_map/ppermute | solution.py:287
  33.5 1.2 %collective-permute-done.14 = bf16[256,384]{1,0:T(8,128)(2,1)S(1)} collective-permute-done((bf16[256,384]{1,0:T(8,128)(2,1)S(1)}, bf16[256,384]{1,0:T(8,128)(2,1)S(1)}, u32[]{:S(2)}, u32[]{:S(2)}) %collective-permute-start.14) | collective-permute-done | bytes 196640 | tf_op jit(solution)/shard_map/ppermute | solution.py:287
  35.0 0.5 collective-permute-start.16
  35.5 1.6 %collective-permute-start.17 = (bf16[256,384]{1,0:T(8,128)(2,1)S(1)}, bf16[256,384]{1,0:T(8,128)(2,1)S(1)}, u32[]{:S(2)}, u32[]{:S(2)}) collective-permute-start(bf16[256,384]{1,0:T(8,128)(2,1)S(1)} %collective-permute-done.15), channel_id=1, source_target_pairs={{2,0},{4,2},{6,4},{7,6},{5,7},{3,5},{1,3},{0,1},{10,8},{12,10},{14... | collective-permute-start | bytes 589832 | tf_op jit(solution)/shard_map/ppermute | solution.py:287
  37.9 1.5 %collective-permute-done.12 = bf16[256,2048]{1,0:T(8,128)(2,1)S(1)} collective-permute-done((bf16[256,2048]{1,0:T(8,128)(2,1)S(1)}, bf16[256,2048]{1,0:T(8,128)(2,1)S(1)}, u32[]{:S(2)}, u32[]{:S(2)}) %collective-permute-start.12) | collective-permute-done | bytes 1048608 | tf_op jit(solution)/shard_map/ppermute | solution.py:19
  39.3 0.3 fusion.19
  39.7 1.9 %collective-permute-start.11 = (bf16[256,384]{1,0:T(8,128)(2,1)S(1)}, bf16[256,384]{1,0:T(8,128)(2,1)S(1)}, u32[]{:S(2)}, u32[]{:S(2)}) collective-permute-start(bf16[256,384]{1,0:T(8,128)(2,1)S(1)} %collective-permute-done.9), channel_id=1, source_target_pairs={{0,2},{2,4},{4,6},{6,7},{7,5},{5,3},{3,1},{1,0},{8,10},{10,12},{12... | collective-permute-start | bytes 589832 | tf_op jit(solution)/shard_map/ppermute | solution.py:287
  42.5 1.8 %collective-permute-start.20 = (bf16[128,384]{1,0:T(8,128)(2,1)S(1)}, bf16[128,384]{1,0:T(8,128)(2,1)S(1)}, u32[]{:S(2)}, u32[]{:S(2)}) collective-permute-start(bf16[128,384]{1,0:T(8,128)(2,1)S(1)} %slice.47), channel_id=1, source_target_pairs={{2,0},{4,2},{6,4},{7,6},{5,7},{3,5},{1,3},{0,1},{10,8},{12,10},{14... | collective-permute-start | bytes 294920 | tf_op jit(solution)/shard_map/ppermute | solution.py:293
  44.7 1.8 %collective-permute-start.23 = (bf16[256,768]{1,0:T(8,128)(2,1)S(1)}, bf16[256,768]{1,0:T(8,128)(2,1)S(1)}, u32[]{:S(2)}, u32[]{:S(2)}) collective-permute-start(bf16[256,768]{1,0:T(8,128)(2,1)S(1)} %get-tuple-element.100.own), channel_id=1, source_target_pairs={{0,16},{8,24},{16,0},{24,8},{1,17},{9,25},{17,1},{25,9},{2,18},{10... | collective-permute-start | bytes 1179656 | tf_op jit(solution)/shard_map/ppermute | solution.py:19
  48.4 0.5 fusion.18
  48.9 0.5 collective-permute-done.18
  50.0 0.7 %collective-permute-done.20 = bf16[128,384]{1,0:T(8,128)(2,1)S(1)} collective-permute-done((bf16[128,384]{1,0:T(8,128)(2,1)S(1)}, bf16[128,384]{1,0:T(8,128)(2,1)S(1)}, u32[]{:S(2)}, u32[]{:S(2)}) %collective-permute-start.20) | collective-permute-done | bytes 98336 | tf_op jit(solution)/shard_map/ppermute | solution.py:293
  51.9 1.6 %collective-permute-start.29 = (bf16[256,384]{1,0:T(8,128)(2,1)S(1)}, bf16[256,384]{1,0:T(8,128)(2,1)S(1)}, u32[]{:S(2)}, u32[]{:S(2)}) collective-permute-start(bf16[256,384]{1,0:T(8,128)(2,1)S(1)} %get-tuple-element.109), channel_id=1, source_target_pairs={{0,24},{8,16},{16,8},{24,0},{1,25},{9,17},{17,9},{25,1},{2,26},{10... | collective-permute-start | bytes 589832 | tf_op jit(solution)/shard_map/ppermute | solution.py:19
  53.6 0.5 collective-permute-start.28
  54.2 0.4 collective-permute-start.24
  54.6 1.7 %collective-permute-start.22 = (bf16[128,384]{1,0:T(8,128)(2,1)S(1)}, bf16[128,384]{1,0:T(8,128)(2,1)S(1)}, u32[]{:S(2)}, u32[]{:S(2)}) collective-permute-start(bf16[128,384]{1,0:T(8,128)(2,1)S(1)} %slice.49), channel_id=1, source_target_pairs={{0,2},{2,4},{4,6},{6,7},{7,5},{5,3},{3,1},{1,0},{8,10},{10,12},{12... | collective-permute-start | bytes 294920 | tf_op jit(solution)/shard_map/ppermute | solution.py:293
  58.0 0.8 %collective-permute-done.24 = bf16[128,384]{1,0:T(8,128)(2,1)S(1)} collective-permute-done((bf16[128,384]{1,0:T(8,128)(2,1)S(1)}, bf16[128,384]{1,0:T(8,128)(2,1)S(1)}, u32[]{:S(2)}, u32[]{:S(2)}) %collective-permute-start.24) | collective-permute-done | bytes 98336 | tf_op jit(solution)/shard_map/ppermute | solution.py:293
  58.8 0.4 collective-permute-done.22
  60.4 0.6 collective-permute-start.30
  60.9 0.6 fusion.21
  61.6 1.3 %collective-permute-start.27 = (bf16[256,384]{1,0:T(8,128)(2,1)S(1)}, bf16[256,384]{1,0:T(8,128)(2,1)S(1)}, u32[]{:S(2)}, u32[]{:S(2)}) collective-permute-start(bf16[256,384]{1,0:T(8,128)(2,1)S(1)} %get-tuple-element.113), channel_id=1, source_target_pairs={{0,24},{8,16},{16,8},{24,0},{1,25},{9,17},{17,9},{25,1},{2,26},{10... | collective-permute-start | bytes 589832 | tf_op jit(solution)/shard_map/ppermute | solution.py:19
  62.9 0.5 collective-permute-start.26
  63.3 0.4 collective-permute-done.28.refs_2_
  63.7 1.0 %place_leading.1.refs_4_ = bf16[256,3072]{1,0:T(8,128)(2,1)} custom-call(s32[1]{0:T(128)} %bitcast.where, bf16[256,384]{1,0:T(8,128)(2,1)S(1)} %get-tuple-element.111.refs_0_, bf16[256,384]{1,0:T(8,128)(2,1)S(1)} %collective-permute-done.21.refs_1_, bf16[256,384]{1,0:T(8,128)(2,1)S(1)} %collective-permute-done.28.refs_2_, ...), custom_call_target="tpu_custom_call" | custom-call | tf_op jit(solution)/shard_map/place_leading/pallas_call | solution.py:201
  64.7 2.0 %outer_minus_delta.1 = (f32[256,2048]{1,0:T(8,128)}, f32[256,512]{1,0:T(8,128)}, f32[256,512]{1,0:T(8,128)}) custom-call(s32[1]{0:T(128)} %bitcast.where, f32[256,2048]{1,0:T(8,128)S(1)} %copy-done, f32[256,512]{1,0:T(8,128)S(1)} %copy-done.1, f32[256,512]{1,0:T(8,128)S(1)} %copy-done.2, bf16[256,768]{1,0:T(8,128)(2,1)S(1)} %get-tuple-element.100.own, ...), custom_call_target="tpu_custom_call" | custom-call | tf_op jit(solution)/shard_map/outer_minus_delta/pallas_call | solution.py:176
  66.8 1.9 %collective-permute-done.27.refs_3_ = bf16[256,384]{1,0:T(8,128)(2,1)S(1)} collective-permute-done((bf16[256,384]{1,0:T(8,128)(2,1)S(1)}, bf16[256,384]{1,0:T(8,128)(2,1)S(1)}, u32[]{:S(2)}, u32[]{:S(2)}) %collective-permute-start.27) | collective-permute-done | bytes 196640 | tf_op jit(solution)/shard_map/ppermute | solution.py:19
  68.6 4.4 %collective-permute-done.26.refs_2_ = bf16[256,384]{1,0:T(8,128)(2,1)S(1)} collective-permute-done((bf16[256,384]{1,0:T(8,128)(2,1)S(1)}, bf16[256,384]{1,0:T(8,128)(2,1)S(1)}, u32[]{:S(2)}, u32[]{:S(2)}) %collective-permute-start.26) | collective-permute-done | bytes 196640 | tf_op jit(solution)/shard_map/ppermute | solution.py:19
  73.1 0.9 %place_second.1 = bf16[256,3072]{1,0:T(8,128)(2,1)} custom-call(s32[1]{0:T(128)} %bitcast.where, bf16[256,384]{1,0:T(8,128)(2,1)S(1)} %get-tuple-element.116.refs_0_, bf16[256,384]{1,0:T(8,128)(2,1)S(1)} %collective-permute-done.25.refs_1_, bf16[256,384]{1,0:T(8,128)(2,1)S(1)} %collective-permute-done.26.refs_2_, ...), custom_call_target="tpu_custom_call", output_to_operand_aliasing={{}: (5, {})} | custom-call | tf_op jit(solution)/shard_map/place_second/pallas_call | solution.py:201
  (89 shorter events, 12.3 us)
Async XLA Ops:
  1.8 2.5 %collective-permute-start.1 = (bf16[256,768]{1,0:T(8,128)(2,1)S(1)}, bf16[256,768]{1,0:T(8,128)(2,1)S(1)}, u32[]{:S(2)}, u32[]{:S(2)}) collective-permute-start(bf16[256,768]{1,0:T(8,128)(2,1)S(1)} %get-tuple-element.60), channel_id=1, source_target_pairs={{0,8},{8,0},{16,24},{24,16},{1,9},{9,1},{17,25},{25,17},{2,10},{10... | collective-permute-start | bytes 1179656 | tf_op jit(solution)/shard_map/ppermute | solution.py:19
  2.3 14.8 %collective-permute-start = (bf16[256,2048]{1,0:T(8,128)(2,1)}, bf16[256,2048]{1,0:T(8,128)(2,1)S(1)}, u32[]{:S(2)}, u32[]{:S(2)}) collective-permute-start(bf16[256,2048]{1,0:T(8,128)(2,1)} %param.10), channel_id=1, source_target_pairs={{0,8},{8,0},{16,24},{24,16},{1,9},{9,1},{17,25},{25,17},{2,10},{10... | collective-permute-start | bytes 3145736 | tf_op jit(solution)/shard_map/ppermute | solution.py:19
  2.4 7.4 %collective-permute-start.2 = (bf16[256,768]{1,0:T(8,128)(2,1)S(1)}, bf16[256,768]{1,0:T(8,128)(2,1)S(1)}, u32[]{:S(2)}, u32[]{:S(2)}) collective-permute-start(bf16[256,768]{1,0:T(8,128)(2,1)S(1)} %get-tuple-element.64), channel_id=1, source_target_pairs={{0,8},{8,0},{16,24},{24,16},{1,9},{9,1},{17,25},{25,17},{2,10},{10... | collective-permute-start | bytes 1179656 | tf_op jit(solution)/shard_map/ppermute | solution.py:19
  4.3 2.9 %copy-start.6 = (bf16[256,2048]{1,0:T(8,128)(2,1)S(1)}, bf16[256,2048]{1,0:T(8,128)(2,1)}, u32[]{:S(2)}) copy-start(bf16[256,2048]{1,0:T(8,128)(2,1)} %param.10) | copy-start | bytes 3145732
  4.5 8.4 %collective-permute-start.4 = (bf16[256,384]{1,0:T(8,128)(2,1)S(1)}, bf16[256,384]{1,0:T(8,128)(2,1)S(1)}, u32[]{:S(2)}, u32[]{:S(2)}) collective-permute-start(bf16[256,384]{1,0:T(8,128)(2,1)S(1)} %get-tuple-element.118), channel_id=1, source_target_pairs={{0,16},{8,24},{16,0},{24,8},{1,17},{9,25},{17,1},{25,9},{2,18},{10... | collective-permute-start | bytes 589832 | tf_op jit(solution)/shard_map/ppermute | solution.py:19
  7.3 5.6 %copy-start.3 = (f32[256,512]{1,0:T(8,128)S(1)}, f32[256,512]{1,0:T(8,128)}, u32[]{:S(2)}) copy-start(f32[256,512]{1,0:T(8,128)} %moment_q.5) | copy-start | bytes 1572868
  7.3 5.6 %copy-start.4 = (f32[256,128]{1,0:T(8,128)S(1)}, f32[256,128]{1,0:T(8,128)}, u32[]{:S(2)}) copy-start(f32[256,128]{1,0:T(8,128)} %moment_k.5) | copy-start | bytes 393220
  7.3 5.6 %copy-start.5 = (f32[256,128]{1,0:T(8,128)S(1)}, f32[256,128]{1,0:T(8,128)}, u32[]{:S(2)}) copy-start(f32[256,128]{1,0:T(8,128)} %moment_v.5) | copy-start | bytes 393220
  7.3 9.9 %collective-permute-start.3 = (bf16[256,384]{1,0:T(8,128)(2,1)S(1)}, bf16[256,384]{1,0:T(8,128)(2,1)S(1)}, u32[]{:S(2)}, u32[]{:S(2)}) collective-permute-start(bf16[256,384]{1,0:T(8,128)(2,1)S(1)} %get-tuple-element.117), channel_id=1, source_target_pairs={{0,16},{8,24},{16,0},{24,8},{1,17},{9,25},{17,1},{25,9},{2,18},{10... | collective-permute-start | bytes 589832 | tf_op jit(solution)/shard_map/ppermute | solution.py:19
  13.1 6.5 %collective-permute-start.6 = (bf16[256,384]{1,0:T(8,128)(2,1)S(1)}, bf16[256,384]{1,0:T(8,128)(2,1)S(1)}, u32[]{:S(2)}, u32[]{:S(2)}) collective-permute-start(bf16[256,384]{1,0:T(8,128)(2,1)S(1)} %fresh_columns.3), channel_id=1, source_target_pairs={{2,0},{4,2},{6,4},{7,6},{5,7},{3,5},{1,3},{0,1},{10,8},{12,10},{14... | collective-permute-start | bytes 589832 | tf_op jit(solution)/shard_map/ppermute | solution.py:287
  15.1 5.7 %collective-permute-start.5 = (bf16[256,384]{1,0:T(8,128)(2,1)S(1)}, bf16[256,384]{1,0:T(8,128)(2,1)S(1)}, u32[]{:S(2)}, u32[]{:S(2)}) collective-permute-start(bf16[256,384]{1,0:T(8,128)(2,1)S(1)} %fresh_columns.3), channel_id=1, source_target_pairs={{0,2},{2,4},{4,6},{6,7},{7,5},{5,3},{3,1},{1,0},{8,10},{10,12},{12... | collective-permute-start | bytes 589832 | tf_op jit(solution)/shard_map/ppermute | solution.py:287
  15.3 24.1 %collective-permute-start.12 = (bf16[256,2048]{1,0:T(8,128)(2,1)S(1)}, bf16[256,2048]{1,0:T(8,128)(2,1)S(1)}, u32[]{:S(2)}, u32[]{:S(2)}) collective-permute-start(bf16[256,2048]{1,0:T(8,128)(2,1)S(1)} %copy-done.6), channel_id=1, source_target_pairs={{0,16},{8,24},{16,0},{24,8},{1,17},{9,25},{17,1},{25,9},{2,18},{10... | collective-permute-start | bytes 3145736 | tf_op jit(solution)/shard_map/ppermute | solution.py:19
  21.2 7.8 %collective-permute-start.8 = (bf16[256,384]{1,0:T(8,128)(2,1)S(1)}, bf16[256,384]{1,0:T(8,128)(2,1)S(1)}, u32[]{:S(2)}, u32[]{:S(2)}) collective-permute-start(bf16[256,384]{1,0:T(8,128)(2,1)S(1)} %fresh_columns.2), channel_id=1, source_target_pairs={{2,0},{4,2},{6,4},{7,6},{5,7},{3,5},{1,3},{0,1},{10,8},{12,10},{14... | collective-permute-start | bytes 589832 | tf_op jit(solution)/shard_map/ppermute | solution.py:287
  22.8 7.7 %collective-permute-start.7 = (bf16[256,384]{1,0:T(8,128)(2,1)S(1)}, bf16[256,384]{1,0:T(8,128)(2,1)S(1)}, u32[]{:S(2)}, u32[]{:S(2)}) collective-permute-start(bf16[256,384]{1,0:T(8,128)(2,1)S(1)} %fresh_columns.2), channel_id=1, source_target_pairs={{0,2},{2,4},{4,6},{6,7},{7,5},{5,3},{3,1},{1,0},{8,10},{10,12},{12... | collective-permute-start | bytes 589832 | tf_op jit(solution)/shard_map/ppermute | solution.py:287
  24.1 10.6 %collective-permute-start.14 = (bf16[256,384]{1,0:T(8,128)(2,1)S(1)}, bf16[256,384]{1,0:T(8,128)(2,1)S(1)}, u32[]{:S(2)}, u32[]{:S(2)}) collective-permute-start(bf16[256,384]{1,0:T(8,128)(2,1)S(1)} %collective-permute-done.5), channel_id=1, source_target_pairs={{0,2},{2,4},{4,6},{6,7},{7,5},{5,3},{3,1},{1,0},{8,10},{10,12},{12... | collective-permute-start | bytes 589832 | tf_op jit(solution)/shard_map/ppermute | solution.py:287
  24.6 8.6 %collective-permute-start.15 = (bf16[256,384]{1,0:T(8,128)(2,1)S(1)}, bf16[256,384]{1,0:T(8,128)(2,1)S(1)}, u32[]{:S(2)}, u32[]{:S(2)}) collective-permute-start(bf16[256,384]{1,0:T(8,128)(2,1)S(1)} %collective-permute-done.6), channel_id=1, source_target_pairs={{2,0},{4,2},{6,4},{7,6},{5,7},{3,5},{1,3},{0,1},{10,8},{12,10},{14... | collective-permute-start | bytes 589832 | tf_op jit(solution)/shard_map/ppermute | solution.py:287
  30.8 7.0 %collective-permute-start.9 = (bf16[256,384]{1,0:T(8,128)(2,1)S(1)}, bf16[256,384]{1,0:T(8,128)(2,1)S(1)}, u32[]{:S(2)}, u32[]{:S(2)}) collective-permute-start(bf16[256,384]{1,0:T(8,128)(2,1)S(1)} %collective-permute-done.7), channel_id=1, source_target_pairs={{0,2},{2,4},{4,6},{6,7},{7,5},{5,3},{3,1},{1,0},{8,10},{10,12},{12... | collective-permute-start | bytes 589832 | tf_op jit(solution)/shard_map/ppermute | solution.py:287
  31.3 6.0 %collective-permute-start.10 = (bf16[256,384]{1,0:T(8,128)(2,1)S(1)}, bf16[256,384]{1,0:T(8,128)(2,1)S(1)}, u32[]{:S(2)}, u32[]{:S(2)}) collective-permute-start(bf16[256,384]{1,0:T(8,128)(2,1)S(1)} %collective-permute-done.8), channel_id=1, source_target_pairs={{2,0},{4,2},{6,4},{7,6},{5,7},{3,5},{1,3},{0,1},{10,8},{12,10},{14... | collective-permute-start | bytes 589832 | tf_op jit(solution)/shard_map/ppermute | solution.py:287
  35.0 7.1 %collective-permute-start.16 = (bf16[256,384]{1,0:T(8,128)(2,1)S(1)}, bf16[256,384]{1,0:T(8,128)(2,1)S(1)}, u32[]{:S(2)}, u32[]{:S(2)}) collective-permute-start(bf16[256,384]{1,0:T(8,128)(2,1)S(1)} %collective-permute-done.14), channel_id=1, source_target_pairs={{0,2},{2,4},{4,6},{6,7},{7,5},{5,3},{3,1},{1,0},{8,10},{10,12},{12... | collective-permute-start | bytes 589832 | tf_op jit(solution)/shard_map/ppermute | solution.py:287
  35.5 6.2 %collective-permute-start.17 = (bf16[256,384]{1,0:T(8,128)(2,1)S(1)}, bf16[256,384]{1,0:T(8,128)(2,1)S(1)}, u32[]{:S(2)}, u32[]{:S(2)}) collective-permute-start(bf16[256,384]{1,0:T(8,128)(2,1)S(1)} %collective-permute-done.15), channel_id=1, source_target_pairs={{2,0},{4,2},{6,4},{7,6},{5,7},{3,5},{1,3},{0,1},{10,8},{12,10},{14... | collective-permute-start | bytes 589832 | tf_op jit(solution)/shard_map/ppermute | solution.py:287
  39.3 5.3 %collective-permute-start.13 = (bf16[256,2048]{1,0:T(8,128)(2,1)S(1)}, bf16[256,2048]{1,0:T(8,128)(2,1)S(1)}, u32[]{:S(2)}, u32[]{:S(2)}) collective-permute-start(bf16[256,2048]{1,0:T(8,128)(2,1)S(1)} %collective-permute-done.12), channel_id=1, source_target_pairs={{0,8},{8,0},{16,24},{24,16},{1,9},{9,1},{17,25},{25,17},{2,10},{10... | collective-permute-start | bytes 3145736 | tf_op jit(solution)/shard_map/ppermute | solution.py:19
  39.7 9.6 %collective-permute-start.11 = (bf16[256,384]{1,0:T(8,128)(2,1)S(1)}, bf16[256,384]{1,0:T(8,128)(2,1)S(1)}, u32[]{:S(2)}, u32[]{:S(2)}) collective-permute-start(bf16[256,384]{1,0:T(8,128)(2,1)S(1)} %collective-permute-done.9), channel_id=1, source_target_pairs={{0,2},{2,4},{4,6},{6,7},{7,5},{5,3},{3,1},{1,0},{8,10},{10,12},{12... | collective-permute-start | bytes 589832 | tf_op jit(solution)/shard_map/ppermute | solution.py:287
  41.6 7.7 %collective-permute-start.18 = (bf16[256,384]{1,0:T(8,128)(2,1)S(1)}, bf16[256,384]{1,0:T(8,128)(2,1)S(1)}, u32[]{:S(2)}, u32[]{:S(2)}) collective-permute-start(bf16[256,384]{1,0:T(8,128)(2,1)S(1)} %collective-permute-done.10), channel_id=1, source_target_pairs={{2,0},{4,2},{6,4},{7,6},{5,7},{3,5},{1,3},{0,1},{10,8},{12,10},{14... | collective-permute-start | bytes 589832 | tf_op jit(solution)/shard_map/ppermute | solution.py:287
  42.5 8.2 %collective-permute-start.20 = (bf16[128,384]{1,0:T(8,128)(2,1)S(1)}, bf16[128,384]{1,0:T(8,128)(2,1)S(1)}, u32[]{:S(2)}, u32[]{:S(2)}) collective-permute-start(bf16[128,384]{1,0:T(8,128)(2,1)S(1)} %slice.47), channel_id=1, source_target_pairs={{2,0},{4,2},{6,4},{7,6},{5,7},{3,5},{1,3},{0,1},{10,8},{12,10},{14... | collective-permute-start | bytes 294920 | tf_op jit(solution)/shard_map/ppermute | solution.py:293
  44.3 6.9 %collective-permute-start.19 = (bf16[128,384]{1,0:T(8,128)(2,1)S(1)}, bf16[128,384]{1,0:T(8,128)(2,1)S(1)}, u32[]{:S(2)}, u32[]{:S(2)}) collective-permute-start(bf16[128,384]{1,0:T(8,128)(2,1)S(1)} %slice.46), channel_id=1, source_target_pairs={{0,2},{2,4},{4,6},{6,7},{7,5},{5,3},{3,1},{1,0},{8,10},{10,12},{12... | collective-permute-start | bytes 294920 | tf_op jit(solution)/shard_map/ppermute | solution.py:293
  44.7 13.4 %collective-permute-start.23 = (bf16[256,768]{1,0:T(8,128)(2,1)S(1)}, bf16[256,768]{1,0:T(8,128)(2,1)S(1)}, u32[]{:S(2)}, u32[]{:S(2)}) collective-permute-start(bf16[256,768]{1,0:T(8,128)(2,1)S(1)} %get-tuple-element.100.own), channel_id=1, source_target_pairs={{0,16},{8,24},{16,0},{24,8},{1,17},{9,25},{17,1},{25,9},{2,18},{10... | collective-permute-start | bytes 1179656 | tf_op jit(solution)/shard_map/ppermute | solution.py:19
  51.8 2.3 %collective-permute-start.21 = (bf16[256,384]{1,0:T(8,128)(2,1)S(1)}, bf16[256,384]{1,0:T(8,128)(2,1)S(1)}, u32[]{:S(2)}, u32[]{:S(2)}) collective-permute-start(bf16[256,384]{1,0:T(8,128)(2,1)S(1)} %get-tuple-element.112), channel_id=1, source_target_pairs={{0,8},{8,0},{16,24},{24,16},{1,9},{9,1},{17,25},{25,17},{2,10},{10... | collective-permute-start | bytes 589832 | tf_op jit(solution)/shard_map/ppermute | solution.py:19
  51.9 10.9 %collective-permute-start.29 = (bf16[256,384]{1,0:T(8,128)(2,1)S(1)}, bf16[256,384]{1,0:T(8,128)(2,1)S(1)}, u32[]{:S(2)}, u32[]{:S(2)}) collective-permute-start(bf16[256,384]{1,0:T(8,128)(2,1)S(1)} %get-tuple-element.109), channel_id=1, source_target_pairs={{0,24},{8,16},{16,8},{24,0},{1,25},{9,17},{17,9},{25,1},{2,26},{10... | collective-permute-start | bytes 589832 | tf_op jit(solution)/shard_map/ppermute | solution.py:19
  53.6 10.1 %collective-permute-start.28 = (bf16[256,384]{1,0:T(8,128)(2,1)S(1)}, bf16[256,384]{1,0:T(8,128)(2,1)S(1)}, u32[]{:S(2)}, u32[]{:S(2)}) collective-permute-start(bf16[256,384]{1,0:T(8,128)(2,1)S(1)} %get-tuple-element.110), channel_id=1, source_target_pairs={{0,16},{8,24},{16,0},{24,8},{1,17},{9,25},{17,1},{25,9},{2,18},{10... | collective-permute-start | bytes 589832 | tf_op jit(solution)/shard_map/ppermute | solution.py:19
  54.2 4.7 %collective-permute-start.24 = (bf16[128,384]{1,0:T(8,128)(2,1)S(1)}, bf16[128,384]{1,0:T(8,128)(2,1)S(1)}, u32[]{:S(2)}, u32[]{:S(2)}) collective-permute-start(bf16[128,384]{1,0:T(8,128)(2,1)S(1)} %slice.50), channel_id=1, source_target_pairs={{2,0},{4,2},{6,4},{7,6},{5,7},{3,5},{1,3},{0,1},{10,8},{12,10},{14... | collective-permute-start | bytes 294920 | tf_op jit(solution)/shard_map/ppermute | solution.py:293
  54.6 4.6 %collective-permute-start.22 = (bf16[128,384]{1,0:T(8,128)(2,1)S(1)}, bf16[128,384]{1,0:T(8,128)(2,1)S(1)}, u32[]{:S(2)}, u32[]{:S(2)}) collective-permute-start(bf16[128,384]{1,0:T(8,128)(2,1)S(1)} %slice.49), channel_id=1, source_target_pairs={{0,2},{2,4},{4,6},{6,7},{7,5},{5,3},{3,1},{1,0},{8,10},{10,12},{12... | collective-permute-start | bytes 294920 | tf_op jit(solution)/shard_map/ppermute | solution.py:293
  59.7 7.0 %collective-permute-start.25 = (bf16[256,384]{1,0:T(8,128)(2,1)S(1)}, bf16[256,384]{1,0:T(8,128)(2,1)S(1)}, u32[]{:S(2)}, u32[]{:S(2)}) collective-permute-start(bf16[256,384]{1,0:T(8,128)(2,1)S(1)} %get-tuple-element.115), channel_id=1, source_target_pairs={{0,8},{8,0},{16,24},{24,16},{1,9},{9,1},{17,25},{25,17},{2,10},{10... | collective-permute-start | bytes 589832 | tf_op jit(solution)/shard_map/ppermute | solution.py:19
  60.4 4.3 %collective-permute-start.30 = (bf16[256,1536]{1,0:T(8,128)(2,1)S(1)}, bf16[256,1536]{1,0:T(8,128)(2,1)S(1)}, u32[]{:S(2)}, u32[]{:S(2)}) collective-permute-start(bf16[256,1536]{1,0:T(8,128)(2,1)S(1)} %pad_maximum_fusion), channel_id=1, source_target_pairs={{0,8},{8,0},{16,24},{24,16},{1,9},{9,1},{17,25},{25,17},{2,10},{10... | collective-permute-start | bytes 2359304 | tf_op jit(solution)/shard_map/ppermute | solution.py:19
  61.5 3.2 %copy-start = (f32[256,2048]{1,0:T(8,128)S(1)}, f32[256,2048]{1,0:T(8,128)}, u32[]{:S(2)}) copy-start(f32[256,2048]{1,0:T(8,128)} %outer_q.1) | copy-start | bytes 6291460
  61.5 3.2 %copy-start.1 = (f32[256,512]{1,0:T(8,128)S(1)}, f32[256,512]{1,0:T(8,128)}, u32[]{:S(2)}) copy-start(f32[256,512]{1,0:T(8,128)} %outer_k.1) | copy-start | bytes 1572868
  61.5 3.2 %copy-start.2 = (f32[256,512]{1,0:T(8,128)S(1)}, f32[256,512]{1,0:T(8,128)}, u32[]{:S(2)}) copy-start(f32[256,512]{1,0:T(8,128)} %outer_v.1) | copy-start | bytes 1572868
  61.6 7.1 %collective-permute-start.27 = (bf16[256,384]{1,0:T(8,128)(2,1)S(1)}, bf16[256,384]{1,0:T(8,128)(2,1)S(1)}, u32[]{:S(2)}, u32[]{:S(2)}) collective-permute-start(bf16[256,384]{1,0:T(8,128)(2,1)S(1)} %get-tuple-element.113), channel_id=1, source_target_pairs={{0,24},{8,16},{16,8},{24,0},{1,25},{9,17},{17,9},{25,1},{2,26},{10... | collective-permute-start | bytes 589832 | tf_op jit(solution)/shard_map/ppermute | solution.py:19
  62.9 10.2 %collective-permute-start.26 = (bf16[256,384]{1,0:T(8,128)(2,1)S(1)}, bf16[256,384]{1,0:T(8,128)(2,1)S(1)}, u32[]{:S(2)}, u32[]{:S(2)}) collective-permute-start(bf16[256,384]{1,0:T(8,128)(2,1)S(1)} %get-tuple-element.114), channel_id=1, source_target_pairs={{0,16},{8,24},{16,0},{24,8},{1,17},{9,25},{17,1},{25,9},{2,18},{10... | collective-permute-start | bytes 589832 | tf_op jit(solution)/shard_map/ppermute | solution.py:19
